TPU v7x, 32 devices: a whole 2x2x4 slice. The times are simulated.
32 devices in a mesh: seq: 8 (over z, y), rep: 4 (over x, core).
Axes of the slice: x: 2, y: 2, z: 4, core: 2. Of those that a mesh axis runs over, the one named last changes fastest.
Arguments:
- tile_embed: bfloat16 [4, 4096, 768], P('rep', 'seq'), may hold values from -6 to 6
- doc_ids: int32 [4, 4096], P('rep', 'seq'), may hold values from 0 to 2, as said below
- norm1_gain: float32 [768], replicated, may hold values from 0.25 to 1.75
- norm1_shift: float32 [768], replicated, may hold values from -3 to 3
- in_weight: bfloat16 [768, 2304], replicated, may hold values from -0.21875 to 0.21875
- in_bias: float32 [2304], replicated, may hold values from -3 to 3
- out_weight: bfloat16 [768, 768], replicated, may hold values from -6 to 6
- out_bias: float32 [768], replicated, may hold values from -3 to 3
- norm2_gain: float32 [768], replicated, may hold values from 0.25 to 1.75
- norm2_shift: float32 [768], replicated, may hold values from -3 to 3
- up_weight: bfloat16 [768, 3072], replicated, may hold values from -0.21875 to 0.21875
- up_bias: float32 [3072], replicated, may hold values from -3 to 3
- down_weight: bfloat16 [3072, 768], replicated, may hold values from -0.109375 to 0.109375
- down_bias: float32 [768], replicated, may hold values from -3 to 3
- cotangent: bfloat16 [4, 4096, 768], P('rep', 'seq'), may hold values from -6 to 6
Outputs:
- out: bfloat16 [4, 4096, 768], P('rep', 'seq')
- grad_input: float32 [4, 4096, 768], P('rep', 'seq')
- grad_norm1_gain: float32 [768], P('seq')
- grad_norm1_shift: float32 [768], P('seq')
- grad_in_weight: float32 [768, 2304], P('seq')
- grad_in_bias: float32 [2304], P('seq')
- grad_out_weight: float32 [768, 768], P('seq')
- grad_out_bias: float32 [768], P('seq')
- grad_norm2_gain: float32 [768], P('seq')
- grad_norm2_shift: float32 [768], P('seq')
- grad_up_weight: float32 [768, 3072], P('seq')
- grad_up_bias: float32 [3072], P('seq')
- grad_down_weight: float32 [3072, 768], P('seq')
- grad_down_bias: float32 [768], P('seq')
Inputs may be any that keep to these rules, and one draw needn't show every extreme that they name: `doc_ids`: in each row the ids never fall and start at 0; slide 1 begins within the first 512 tiles of the row and ends within its last 512 tiles, and slide 2 follows it to the row's end.
All inputs are finite; a program needn't handle non-finite values.
Results may differ from a plain program's by a relative error of at most 0.013.
Values may be sent and summed in bfloat16 or wider, within the bound.
No kernel may reach another device: no remote copies, remote signals or barrier semaphores. Data moves between devices by JAX's collectives and lax.ppermute only.
A program may use at most 320 MiB of HBM per device.

v0:
```python
import functools
import math

import jax
import jax.numpy as jnp
import numpy as np
from jax import lax
from jax.experimental import pallas as pl
from jax.experimental.pallas import tpu as pltpu
from jax.sharding import PartitionSpec as P


D = 768
H = 16
HD = 48
FF = 3072
SEG0 = 1024
BRANCHES = 5
RES = 16
HG = H // 2
GW = HG * HD
NORM_EPS = 1e-05
BIG = 1e30
SCALE = HD**-0.5
LN2 = math.log(2.0)
Q_SCALE = SCALE / LN2

f32 = jnp.float32
bf16 = jnp.bfloat16
NN = (((1,), (0,)), ((), ()))
NT = (((1,), (1,)), ((), ()))
MIB = 2**20
VMEM_MIB = 60


def mm(left, right, dims=NN):
    return lax.dot_general(left, right, dims, preferred_element_type=f32)


def rev4(v):
    return ((v & 1) << 3) | ((v & 2) << 1) | ((v & 4) >> 1) | ((v & 8) >> 3)


def run_start(head, level, tok):
    if level == 1:
        return (head % 2) * (tok // 2)
    return ((head % 2) * 2 + (head // 2) % 2) * (tok // 4)


def kcall(body, name, ins, outs, *, grid=None, in_specs=None, out_specs=None, scratch=(), vmem=VMEM_MIB, flops=0):
    kw = {}
    if grid is not None:
        kw = dict(grid=grid)
    if in_specs is not None:
        kw.update(in_specs=in_specs, out_specs=out_specs)
    nbytes = sum(math.prod(a.shape) * a.dtype.itemsize for a in (*ins, *outs))
    return pl.pallas_call(
        body,
        out_shape=outs,
        scratch_shapes=list(scratch),
        name=name,
        compiler_params=pltpu.CompilerParams(vmem_limit_bytes=vmem * MIB),
        cost_estimate=pl.CostEstimate(flops=int(flops), bytes_accessed=nbytes, transcendentals=0),
        **kw,
    )(*ins)


def sds(shape, dtype):
    return jax.ShapeDtypeStruct(shape, dtype)


SMEM = pl.BlockSpec(memory_space=pltpu.SMEM)
VMEM = pl.BlockSpec(memory_space=pltpu.VMEM)


def full(shape):
    return pl.BlockSpec(shape, lambda *_: (0,) * len(shape))


def features(side, doc_row, pos, head, b0, tok, extra=None):
    n = doc_row.shape[1]
    rowid = lax.broadcasted_iota(jnp.int32, (16, n), 0)
    out = jnp.zeros((16, n), f32)
    diff = rev4(pos // (tok // RES)) ^ (head & (RES - 1))
    for d in range(3):
        same = doc_row == d
        val = jnp.where(same, 0.0, 1.0) if side == "q" else jnp.where(same, -BIG, 0.0)
        out = jnp.where(rowid == d, val, out)
    row = 3
    for b in range(b0 + 1, BRANCHES):
        val = math.log2((b - b0 + 1) / (b - b0))
        high = float(np.asarray(val, dtype=jnp.bfloat16))
        chosen = (diff & (2**b - 1)) == 0
        for part in (high, val - high) if val != 1.0 else (1.0,):
            put = jnp.where(chosen, 1.0 if side == "q" else part, 0.0)
            out = jnp.where(rowid == row, put, out)
            row += 1
    assert row <= 10
    if b0 > 0:
        outside = (diff & (2**b0 - 1)) != 0
        one = jnp.where(outside, 1.0 if side == "q" else -BIG, 0.0)
        const = 1.0 if side == "q" else -BIG
        out = jnp.where(rowid == (10 if side == "q" else 11), one, out)
        out = jnp.where(rowid == (11 if side == "q" else 10), const, out)
    if extra is not None:
        for j in range(3):
            out = jnp.where(rowid == 12 + j, extra[j], out)
    return out.astype(bf16)


def split3(row):
    first = row.astype(bf16).astype(f32)
    rest = row - first
    second = rest.astype(bf16).astype(f32)
    return (first, second, rest - second)


def tail_rows(n, rows):
    rowid = lax.broadcasted_iota(jnp.int32, (16, n), 0)
    out = jnp.zeros((16, n), f32)
    for j, r in enumerate(rows):
        out = jnp.where(rowid == j, r, out)
    return out.astype(bf16)


def place(tok, axis):
    shape = (tok, 1) if axis == 0 else (1, tok)
    p = lax.broadcasted_iota(jnp.int32, shape, axis)
    return rev4(p % RES) * (tok // RES) + p // RES


def one_hot(tok, transposed):
    if transposed:
        return (place(tok, 0) == lax.broadcasted_iota(jnp.int32, (1, tok), 1)).astype(bf16)
    return (place(tok, 1) == lax.broadcasted_iota(jnp.int32, (tok, 1), 0)).astype(bf16)


def normalise(x):
    cen = x - jnp.mean(x, axis=-1, keepdims=True)
    rs = lax.rsqrt(jnp.mean(cen * cen, axis=-1, keepdims=True) + NORM_EPS)
    return cen * rs, rs


def row(ref):
    return ref[...][None, :]


def project_body(tok, y_ref, x_ref, ids_ref, gain, shift, in_b, wq, wk, wv, first_ref, q_ref, k_ref, v_ref, doc_ref, near_ref, far_ref):
    xh, _ = normalise(x_ref[...].astype(f32))
    first = (xh * row(gain) + row(shift)).astype(bf16)
    first = mm(one_hot(tok, False), first).astype(bf16)
    first_ref[...] = first.T
    ids = jnp.broadcast_to(ids_ref[...].astype(f32), (16, tok)).astype(bf16)
    docs = mm(ids, one_hot(tok, True))
    doc_ref[...] = docs[0:8]
    bias = row(in_b)
    for part, (w, ref) in enumerate(((wq, q_ref), (wk, k_ref), (wv, v_ref))):
        at = part * D
        val = mm(first, w[...]) + jnp.where(y_ref[0] == 0, bias[:, at : at + GW], bias[:, at + GW : at + D])
        if part == 0:
            val = val * Q_SCALE
        ref[...] = val.astype(bf16).T
    for out, level in ((near_ref, 1), (far_ref, 2)):
        width = tok >> level
        for part, ref in enumerate((k_ref, v_ref)):
            for h in range(HG):
                start = run_start(h, level, tok)
                out[part * GW + h * HD : part * GW + (h + 1) * HD] = ref[h * HD : (h + 1) * HD, start : start + width]
        rowid = lax.broadcasted_iota(jnp.int32, (16, width), 0)
        acc = jnp.zeros((16, width), f32)
        for j in range(2**level):
            acc = jnp.where(rowid == j, docs[0:1, j * width : (j + 1) * width], acc)
        out[2 * GW : 2 * GW + 16] = acc.astype(bf16)


def weight_specs():
    return [pl.BlockSpec((D, GW), lambda j, y, part=part: (0, 2 * part + y[0])) for part in range(3)]


def pcall(body, name, scalar, ins, outs, in_specs, out_specs, *, grid=(1,), scratch=(), vmem=VMEM_MIB, flops=0):
    nbytes = sum(math.prod(a.shape) * a.dtype.itemsize for a in (*ins, *outs))
    return pl.pallas_call(
        body,
        grid_spec=pltpu.PrefetchScalarGridSpec(
            num_scalar_prefetch=1, grid=grid, in_specs=in_specs, out_specs=out_specs, scratch_shapes=list(scratch)
        ),
        out_shape=outs,
        name=name,
        compiler_params=pltpu.CompilerParams(vmem_limit_bytes=vmem * MIB),
        cost_estimate=pl.CostEstimate(flops=int(flops), bytes_accessed=nbytes, transcendentals=0),
    )(scalar, *ins)


def project(y, x, ids, gain, shift, in_b, weight):
    tok = x.shape[0]
    outs = [
        sds((D, tok), bf16),
        sds((GW, tok), bf16),
        sds((GW, tok), bf16),
        sds((GW, tok), bf16),
        sds((8, tok), f32),
        sds((2 * GW + 16, tok // 2), bf16),
        sds((2 * GW + 16, tok // 4), bf16),
    ]
    return pcall(
        functools.partial(project_body, tok), "project", y, (x, ids, gain, shift, in_b, weight, weight, weight), outs,
        [full(x.shape), full(ids.shape), full((D,)), full((D,)), full((3 * D,))] + weight_specs(), [full(o.shape) for o in outs],
        flops=2 * tok * D * (tok + 3 * GW),
    )


def fill_keys(kaug, vaug, k_parts, v_parts, doc_parts, pos_parts, head, b0, tok):
    at = 0
    for k, v, doc, pos in zip(k_parts, v_parts, doc_parts, pos_parts, strict=True):
        n = k.shape[1]
        kaug[0:HD, at : at + n] = k
        kaug[HD:64, at : at + n] = features("k", doc, pos, head, b0, tok, (-1.0, -1.0, -1.0))
        vaug[0:HD, at : at + n] = v
        vaug[HD:64, at : at + n] = tail_rows(n, (1.0, 1.0, 1.0))
        at += n


def fill_queries(qaug, q_parts, doc_parts, pos_parts, head, b0, tok, lse_parts=None):
    at = 0
    for j, (q, doc, pos) in enumerate(zip(q_parts, doc_parts, pos_parts, strict=True)):
        n = q.shape[1]
        extra = None if lse_parts is None else split3(lse_parts[j])
        qaug[0:HD, at : at + n] = q
        qaug[HD:64, at : at + n] = features("q", doc, pos, head, b0, tok, extra)
        at += n


def iota_row(n):
    return lax.broadcasted_iota(jnp.int32, (1, n), 1)


def attend(qaug, kaug, vaug, nq, nk, step, put):
    keys = kaug[:, 0:nk].T
    for at in range(0, nq, step):
        scores = mm(keys, qaug[:, at : at + step])
        probs = jnp.exp2(scores).astype(bf16)
        put(at, mm(vaug[:, 0:nk], probs))


def own_forward_body(tok, y_ref, qa, qb, ka, kb, va, vb, da, db, out_ref, qaug, kaug, vaug):
    head = y_ref[0] * HG + pl.program_id(0)
    pos = iota_row(tok)
    docs = (da[0:1], db[0:1])
    fill_keys(kaug, vaug, (ka[...], kb[...]), (va[...], vb[...]), docs, (pos, pos), head, 0, tok)
    fill_queries(qaug, (qa[...], qb[...]), docs, (pos, pos), head, 0, tok)

    def put(at, val):
        out_ref[0, :, at : at + val.shape[1]] = val

    attend(qaug, kaug, vaug, 2 * tok, 2 * tok, tok, put)


def head_block(tok):
    return pl.BlockSpec((HD, tok), lambda h: (h, 0))


def own_forward(y, qs, ks, vs, docs):
    tok = qs[0].shape[1]
    return kcall(
        functools.partial(own_forward_body, tok),
        "own_forward",
        (y, *qs, *ks, *vs, *docs),
        [sds((HG, 64, 2 * tok), f32)],
        grid=(HG,),
        in_specs=[SMEM] + [head_block(tok)] * 6 + [full((8, tok))] * 2,
        out_specs=[pl.BlockSpec((1, 64, 2 * tok), lambda h: (h, 0, 0))],
        scratch=[pltpu.VMEM((64, 2 * tok), bf16)] * 3,
        flops=2 * HG * 128 * (2 * tok) ** 2,
    )[0]


def groups_of(masks):
    found = {}
    for j, m in enumerate(masks):
        found.setdefault(m.bit_length(), []).append(j)
    return [(b0, min(b0, 2), found[b0]) for b0 in sorted(found)]


def remote_parts(refs, members, local, level, tok):
    width = tok >> level
    start = run_start(local, level, tok)
    lane = iota_row(width) + start
    row = pl.multiple_of(local * HD, 16)
    ks, vs, docs, poss = [], [], [], []
    for j in members:
        for ref in refs[2 * j : 2 * j + 2]:
            ks.append(ref[pl.ds(row, HD), :])
            vs.append(ref[pl.ds(row + GW, HD), :])
            block = ref[2 * GW : 2 * GW + 16, :].astype(f32)
            picked = block[0:1]
            for r in range(1, 2**level):
                picked = jnp.where(start // width == r, block[r : r + 1], picked)
            docs.append(picked)
            poss.append(lane)
    return ks, vs, docs, poss, start, width


def far_forward_body(tok, masks, y_ref, qa, qb, da, db, part, *rest):
    nrem = 2 * len(masks)
    refs = rest[:nrem]
    ma, mb, merged, lse, qaug, kaug, vaug, acc = rest[nrem:]
    local = pl.program_id(0)
    head = y_ref[0] * HG + local
    acc[...] = part[0]
    for b0, level, members in groups_of(masks):
        ks, vs, docs, poss, start, width = remote_parts(refs, members, local, level, tok)
        nk = width * len(ks)
        fill_keys(kaug, vaug, ks, vs, docs, poss, head, b0, tok)
        window = pl.ds(pl.multiple_of(start, 128), width)
        pos = iota_row(width) + start
        fill_queries(qaug, (qa[:, window], qb[:, window]), (da[0:1, window], db[0:1, window]), (pos, pos), head, b0, tok)

        def put(at, val):
            acc[:, window] += val[:, 0:width]
            other = pl.ds(pl.multiple_of(start + tok, 128), width)
            acc[:, other] += val[:, width : 2 * width]

        attend(qaug, kaug, vaug, 2 * width, nk, 2 * width, put)
    den = acc[HD : HD + 1]
    val = acc[0:HD] / den
    merged[0] = val
    ma[...] = val[:, 0:tok].astype(bf16)
    mb[...] = val[:, tok : 2 * tok].astype(bf16)
    lse[0] = jnp.broadcast_to(jnp.log2(den), (8, 2 * tok))


def remote_sizes(masks, tok):
    nq = max([tok >> level << 1 for _, level, _ in groups_of(masks)] + [128])
    nk = max([(tok >> level) * 2 * len(members) for _, level, members in groups_of(masks)] + [128])
    return nq, nk


def remote_flops(masks, tok):
    return sum(2 * HG * 64 * (2 * (tok >> lv)) * ((tok >> lv) * 2 * len(mem)) for _, lv, mem in groups_of(masks))


def far_forward(y, qs, docs, part, masks, remote):
    tok = qs[0].shape[1]
    nq, nk = remote_sizes(masks, tok)
    per_head = pl.BlockSpec((1, 64, 2 * tok), lambda h: (h, 0, 0))
    return kcall(
        functools.partial(far_forward_body, tok, masks),
        "far_forward",
        (y, *qs, *docs, part, *remote),
        [sds((GW, tok), bf16)] * 2 + [sds((HG, HD, 2 * tok), f32), sds((HG, 8, 2 * tok), f32)],
        grid=(HG,),
        in_specs=[SMEM] + [head_block(tok)] * 2 + [full((8, tok))] * 2 + [per_head] + [full(r.shape) for r in remote],
        out_specs=[head_block(tok)] * 2
        + [pl.BlockSpec((1, HD, 2 * tok), lambda h: (h, 0, 0)), pl.BlockSpec((1, 8, 2 * tok), lambda h: (h, 0, 0))],
        scratch=[
            pltpu.VMEM((64, nq), bf16),
            pltpu.VMEM((64, nk), bf16),
            pltpu.VMEM((64, nk), bf16),
            pltpu.VMEM((64, 2 * tok), f32),
        ],
        flops=2 * remote_flops(masks, tok),
    )


def attend_back(qaug, gaug, kaug, vaug, nq, nk, step, put_q, dk, dv):
    keys = kaug[0:HD, 0:nk]
    for at in range(0, nq, step):
        sl = slice(at, at + step)
        probs = jnp.exp2(mm(qaug[:, sl].T, kaug[:, 0:nk]))
        gprobs = mm(gaug[:, sl].T, vaug[:, 0:nk])
        gs = (probs * gprobs).astype(bf16)
        new_v = mm(gaug[0:HD, sl], probs.astype(bf16))
        new_k = mm(qaug[0:HD, sl], gs)
        if at == 0:
            dv[:, 0:nk] = new_v
            dk[:, 0:nk] = new_k
        else:
            dv[:, 0:nk] += new_v
            dk[:, 0:nk] += new_k
        put_q(at, mm(keys, gs, NT) * SCALE)


def fill_grads(gaug, g_parts, m_parts):
    at = 0
    for g, m in zip(g_parts, m_parts, strict=True):
        n = g.shape[1]
        delta = jnp.sum(g.astype(f32) * m, axis=0, keepdims=True)
        gaug[0:HD, at : at + n] = g
        gaug[HD:64, at : at + n] = tail_rows(n, split3(-delta))
        at += n


def far_backward_body(tok, masks, y_ref, qa, qb, da, db, ga, gb, merged, lse, *rest):
    nrem = 2 * len(masks)
    refs = rest[:nrem]
    dq_ref = rest[nrem]
    sends = rest[nrem + 1 : nrem + 1 + len(masks)]
    qaug, gaug, kaug, vaug, dk, dv = rest[nrem + 1 + len(masks) :]
    local = pl.program_id(0)
    head = y_ref[0] * HG + local
    row = pl.multiple_of(local * HD, 16)
    dq_ref[0] = jnp.zeros((HD, 2 * tok), f32)
    for b0, level, members in groups_of(masks):
        ks, vs, docs, poss, start, width = remote_parts(refs, members, local, level, tok)
        nk = width * len(ks)
        fill_keys(kaug, vaug, ks, vs, docs, poss, head, b0, tok)
        window = pl.ds(pl.multiple_of(start, 128), width)
        other = pl.ds(pl.multiple_of(start + tok, 128), width)
        pos = iota_row(width) + start
        fill_queries(
            qaug, (qa[:, window], qb[:, window]), (da[0:1, window], db[0:1, window]), (pos, pos), head, b0, tok,
            (lse[0, 0:1, window], lse[0, 0:1, other]),
        )
        fill_grads(gaug, (ga[:, window], gb[:, window]), (merged[0, :, window], merged[0, :, other]))

        def put_q(at, val):
            dq_ref[0, :, window] += val[:, 0:width]
            dq_ref[0, :, other] += val[:, width : 2 * width]

        attend_back(qaug, gaug, kaug, vaug, 2 * width, nk, 2 * width, put_q, dk, dv)
        for n, j in enumerate(members):
            span = slice(2 * n * width, 2 * (n + 1) * width)
            sends[j][pl.ds(row, HD), :] = (dk[:, span] * LN2).astype(bf16)
            sends[j][pl.ds(row + GW, HD), :] = dv[:, span].astype(bf16)


def far_backward(y, qs, docs, gs, merged, lse, masks, remote):
    tok = qs[0].shape[1]
    nq, nk = remote_sizes(masks, tok)
    per_head = lambda r: pl.BlockSpec((1, r, 2 * tok), lambda h: (h, 0, 0))
    sends = [sds((2 * GW, 2 * (tok >> min(m.bit_length(), 2))), bf16) for m in masks]
    return kcall(
        functools.partial(far_backward_body, tok, masks),
        "far_backward",
        (y, *qs, *docs, *gs, merged, lse, *remote),
        [sds((HG, HD, 2 * tok), f32)] + sends,
        grid=(HG,),
        in_specs=[SMEM] + [head_block(tok)] * 2 + [full((8, tok))] * 2 + [head_block(tok)] * 2
        + [per_head(HD), per_head(8)] + [full(r.shape) for r in remote],
        out_specs=[per_head(HD)] + [full(s.shape) for s in sends],
        scratch=[
            pltpu.VMEM((64, nq), bf16),
            pltpu.VMEM((64, nq), bf16),
            pltpu.VMEM((64, nk), bf16),
            pltpu.VMEM((64, nk), bf16),
            pltpu.VMEM((HD, nk), f32),
            pltpu.VMEM((HD, nk), f32),
        ],
        flops=5 * remote_flops(masks, tok),
    )


def own_backward_body(tok, y_ref, qa, qb, ka, kb, va, vb, da, db, ga, gb, merged, lse, dq_in, dq, dk, dv, qaug, gaug, kaug, vaug):
    head = y_ref[0] * HG + pl.program_id(0)
    pos = iota_row(tok)
    docs = (da[0:1], db[0:1])
    fill_keys(kaug, vaug, (ka[...], kb[...]), (va[...], vb[...]), docs, (pos, pos), head, 0, tok)
    fill_queries(
        qaug, (qa[...], qb[...]), docs, (pos, pos), head, 0, tok, (lse[0, 0:1, 0:tok], lse[0, 0:1, tok : 2 * tok])
    )
    fill_grads(gaug, (ga[...], gb[...]), (merged[0, :, 0:tok], merged[0, :, tok : 2 * tok]))

    def put_q(at, val):
        dq[:, at : at + tok] = (val + dq_in[0, :, at : at + tok]).astype(bf16)

    attend_back(qaug, gaug, kaug, vaug, 2 * tok, 2 * tok, tok, put_q, dk.at[0], dv.at[0])


def own_backward(y, qs, ks, vs, docs, gs, merged, lse, dq):
    tok = qs[0].shape[1]
    per_head = lambda r: pl.BlockSpec((1, r, 2 * tok), lambda h: (h, 0, 0))
    return kcall(
        functools.partial(own_backward_body, tok),
        "own_backward",
        (y, *qs, *ks, *vs, *docs, *gs, merged, lse, dq),
        [sds((GW, 2 * tok), bf16)] + [sds((HG, HD, 2 * tok), f32)] * 2,
        grid=(HG,),
        in_specs=[SMEM] + [head_block(tok)] * 6 + [full((8, tok))] * 2 + [head_block(tok)] * 2
        + [per_head(HD), per_head(8), per_head(HD)],
        out_specs=[head_block(2 * tok)] + [per_head(HD)] * 2,
        scratch=[pltpu.VMEM((64, 2 * tok), bf16)] * 4,
        flops=5 * HG * 128 * (2 * tok) ** 2,
    )


def cot_body(cot, down, out):
    out[...] = mm(cot[...], down[...], NT)


def cot_down(cot, down):
    tok, ff = cot.shape[0], down.shape[0]
    blk = 768
    return kcall(
        cot_body, "cot_down", (cot, down), [sds((tok, ff), f32)], grid=(ff // blk,),
        in_specs=[full((tok, D)), pl.BlockSpec((blk, D), lambda j: (j, 0))],
        out_specs=[pl.BlockSpec((tok, blk), lambda j: (0, j))], flops=2 * tok * D * ff,
    )[0]


ERF_P = 0.3275911
ERF_A = (0.254829592, -0.284496736, 1.421413741, -1.453152027, 1.061405429)


def normal_cdf(v):
    gauss = jnp.exp2(v * v * (-0.5 / LN2))
    t = 1.0 / (1.0 + jnp.abs(v) * (ERF_P * 0.5**0.5))
    poly = 0.5 * ERF_A[4]
    for a in ERF_A[3::-1]:
        poly = poly * t + 0.5 * a
    tail = poly * t * gauss
    return jnp.where(v < 0, tail, 1.0 - tail), gauss


def mlp_body(tok, nblk, y_ref, x_ref, mown, moth, out_b, n2g, n2s, wout, up, up_b, gdown, cot,
             gelu_ref, gelu_t_ref, gpre_ref, upb_ref, resid_ref, second_t_ref, gattn_t_ref, gmown, gmoth, gres_ref, vec_ref,
             second, xhat, rstd, acc):
    step = pl.program_id(0)
    y = y_ref[0]
    mine = pl.ds(pl.multiple_of(y * GW, 128), GW)
    theirs = pl.ds(pl.multiple_of((1 - y) * GW, 128), GW)
    gain = row(n2g)

    @pl.when(step == 0)
    def _():
        pmt = one_hot(tok, True)
        own = mm(pmt, mown[...], NT).astype(bf16)
        oth = mm(pmt, moth[...], NT).astype(bf16)
        resid = x_ref[...].astype(f32) + (mm(own, wout[mine, :]) + mm(oth, wout[theirs, :])) + row(out_b)
        resid_ref[...] = resid
        xh, rs = normalise(resid)
        xhat[...] = xh
        rstd[...] = jnp.broadcast_to(rs, rstd.shape)
        low = (xh * gain + row(n2s)).astype(bf16)
        second[...] = low
        second_t_ref[...] = low.T
        acc[...] = jnp.zeros_like(acc)

    pre = mm(second[...], up[...]) + up_b[0]
    cdf, gauss = normal_cdf(pre)
    gelu = (pre * cdf).astype(bf16)
    gelu_ref[...] = gelu
    gelu_t_ref[...] = gelu.T
    slope = cdf + pre * (gauss * (1.0 / math.sqrt(2.0 * math.pi)))
    gpre = (slope * gdown[...]).astype(bf16)
    gpre_ref[...] = gpre
    upb_ref[...] = mm(jnp.ones((8, tok), bf16), gpre)
    acc[...] += mm(gpre, up[...], NT)

    @pl.when(step == nblk - 1)
    def _():
        dy = acc[...]
        xh = xhat[...]
        dyg = dy * gain
        m1 = jnp.mean(dyg, axis=-1, keepdims=True)
        m2 = jnp.mean(dyg * xh, axis=-1, keepdims=True)
        g = cot[...]
        gres = g.astype(f32) + rstd[:, 0:1] * (dyg - m1 - xh * m2)
        gres_ref[...] = gres
        gattn = gres.astype(bf16)
        gattn_t = mm(gattn.T, one_hot(tok, True)).astype(bf16)
        gattn_t_ref[...] = gattn_t
        gmoth[...] = mm(wout[theirs, :], gattn_t).astype(bf16)
        gmown[...] = mm(wout[mine, :], gattn_t).astype(bf16)
        ones = jnp.ones((8, tok), bf16)
        vec_ref[0:8] = mm(ones, g)
        vec_ref[8:16] = jnp.broadcast_to(jnp.sum(dy * xh, axis=0, keepdims=True), (8, D))
        vec_ref[16:24] = jnp.broadcast_to(jnp.sum(dy, axis=0, keepdims=True), (8, D))
        vec_ref[24:32] = mm(ones, gattn)


def mlp(y, x, mown, moth, out_b, n2g, n2s, wout, up, up_b, gdown, cot):
    tok = cot.shape[0]
    ff = up.shape[1]
    blk = 768
    nblk = ff // blk
    wide = pl.BlockSpec((tok, blk), lambda j: (0, j))
    outs = [
        sds((tok, ff), bf16), sds((ff, tok), bf16), sds((tok, ff), bf16), sds((8, ff), f32),
        sds((tok, D), f32), sds((D, tok), bf16), sds((D, tok), bf16), sds((GW, tok), bf16), sds((GW, tok), bf16),
        sds((tok, D), f32), sds((32, D), f32),
    ]
    return kcall(
        functools.partial(mlp_body, tok, nblk),
        "mlp",
        (y, x, mown, moth, out_b, n2g, n2s, wout, up, up_b.reshape(nblk, 1, blk), gdown, cot),
        outs,
        grid=(nblk,),
        in_specs=[
            SMEM, full(x.shape), full(mown.shape), full(moth.shape), full((D,)), full((D,)), full((D,)), full(wout.shape),
            pl.BlockSpec((D, blk), lambda j: (0, j)), pl.BlockSpec((1, 1, blk), lambda j: (j, 0, 0)),
            wide, full((tok, D)),
        ],
        out_specs=[
            wide, pl.BlockSpec((blk, tok), lambda j: (j, 0)), wide, pl.BlockSpec((8, blk), lambda j: (0, j)),
        ] + [full(o.shape) for o in outs[4:]],
        scratch=[pltpu.VMEM((tok, D), bf16), pltpu.VMEM((tok, D), f32), pltpu.VMEM((tok, 128), f32), pltpu.VMEM((tok, D), f32)],
        flops=2 * tok * D * (2 * ff + 2 * D + 2 * tok),
    )


NBLK = 8
HALF = D // 2
DOWN_ROWS = FF // NBLK
UP_ROWS = D // NBLK
MLP_ROWS = DOWN_ROWS + 4 * UP_ROWS + UP_ROWS
STEP_BLOCKS = 2


def mlp_grads_body(bits, gelu_t, cot, second_t, gpre, mown, moth, gattn_t, send, keep):
    up = mm(second_t[...], gpre[...]).astype(bf16)
    down = mm(gelu_t[...], cot[...]).astype(bf16)
    heads = jnp.where((pl.program_id(0) < NBLK // STEP_BLOCKS // 2) == (bits[0] == 0), mown[...], moth[...])
    att = mm(heads, gattn_t[...], NT).astype(bf16)
    keep_low = bits[3] == 0

    def put(block, rows, low, high):
        keep[block, rows] = jnp.where(keep_low, low, high)
        send[block, rows] = jnp.where(keep_low, high, low)

    for s in range(STEP_BLOCKS):
        d = down[s * DOWN_ROWS : (s + 1) * DOWN_ROWS]
        put(s, slice(0, DOWN_ROWS), d[:, :HALF], d[:, HALF:])
        rows = slice(s * UP_ROWS, (s + 1) * UP_ROWS)
        for c in range(4):
            at = DOWN_ROWS + c * UP_ROWS
            low = up[rows, c * HALF : (c + 1) * HALF]
            put(s, slice(at, at + UP_ROWS), low, up[rows, (c + 4) * HALF : (c + 5) * HALF])
        a = att[rows]
        put(s, slice(DOWN_ROWS + 4 * UP_ROWS, MLP_ROWS), a[:, :HALF], a[:, HALF:])


def mlp_grads(bits, gelu_t, cot, second_t, gpre, mown, moth, gattn_t):
    tok = cot.shape[0]
    n = NBLK // STEP_BLOCKS
    rows = MLP_ROWS
    heads = pl.BlockSpec((GW // (n // 2), tok), lambda j, c: (j % (n // 2), 0))
    outs = [sds((NBLK, rows, HALF), bf16)] * 2
    return pcall(
        mlp_grads_body, "mlp_grads", bits, (gelu_t, cot, second_t, gpre, mown, moth, gattn_t), outs,
        [
            pl.BlockSpec((FF // n, tok), lambda j, c: (j, 0)),
            full(cot.shape),
            pl.BlockSpec((D // n, tok), lambda j, c: (j, 0)),
            full(gpre.shape),
            heads,
            heads,
            full(gattn_t.shape),
        ],
        [pl.BlockSpec((STEP_BLOCKS, rows, HALF), lambda j, c: (j, 0, 0))] * 2,
        grid=(n,),
        flops=2 * tok * D * (2 * FF + D),
    )


IN_ROWS = D // NBLK // 2
IN_COLS = 3 * GW + 128
SMALL_ROWS = 16
UNIT = UP_ROWS


def finish_body(tok, masks, bits, dq, dk, dv, xa, xb, fa, fb, wq, wk, wv, vec, up_sum, *rest):
    nrem = len(masks)
    recv = rest[:nrem]
    first_a, first_b, send, keep, gqkv, total, acc, sums, bias, small = rest[nrem:]
    step = pl.program_id(0)
    for part, ref, scale in ((0, dk, LN2), (1, dv, 1.0)):
        for h in range(HG):
            total[h * HD : (h + 1) * HD] = ref[h] * scale
        for m, r in zip(masks, recv, strict=True):
            level = min(m.bit_length(), 2)
            for h in range(HG):
                start = run_start(h, level, tok)
                row = part * GW + h * HD
                total[h * HD : (h + 1) * HD, start : start + (tok >> level)] += r[row : row + HD].astype(f32)
        gqkv[(1 + part) * GW : (2 + part) * GW] = total[...].astype(bf16)
    gqkv[0:GW] = dq[...]
    nat = mm(one_hot(tok, True), gqkv[...], NT).astype(bf16)
    new_bias = mm(jnp.ones((8, tok), bf16), nat)
    dy = sum(mm(nat[:, part * GW : (part + 1) * GW], w[...], NT) for part, w in enumerate((wq, wk, wv)))
    later = step == 1
    xh, _ = normalise(jnp.where(later, xa[...], xb[...]).astype(f32))
    new_gain = jnp.sum(dy * xh, axis=0, keepdims=True)
    new_shift = jnp.sum(dy, axis=0, keepdims=True)

    @pl.when(step == 0)
    def _():
        first_b[...] = dy.astype(bf16)
        acc[...] = mm(fb[...], gqkv[...], NT)
        bias[...] = new_bias
        sums[0:8] = jnp.broadcast_to(new_gain, (8, D))
        sums[8:16] = jnp.broadcast_to(new_shift, (8, D))

    @pl.when(step == 1)
    def _():
        first_a[...] = dy
        val = (acc[...] + mm(fa[...], gqkv[...], NT)).astype(bf16)
        all_bias = bias[0:1] + new_bias[0:1]
        lines = [sums[0:1] + new_gain, sums[8:9] + new_shift]
        lines += [vec[8 * j : 8 * j + 1] for j in range(4)]
        cut = lambda line, u: line[:, u * UNIT : (u + 1) * UNIT]
        small[...] = jnp.zeros_like(small)

        def put(block, row, line):
            small[block, row : row + 1, 0:UNIT] = line

        for s in range(NBLK):
            for row, line in zip((0, 1, 5, 6, 7, 8), lines, strict=True):
                put(s, row, cut(line, s))
            for k in range(4):
                put(s, 9 + k, cut(up_sum[0:1], s * 4 + k))
        for u in range(3 * NBLK):
            part, owner, k = u // 8, u // 4 % 2, u % 4
            put(u // 3, 2 + u % 3, jnp.where(bits[0] == owner, cut(all_bias, part * 4 + k), 0.0))
        keep_low = bits[3] == 0
        zeros = jnp.zeros((IN_ROWS, 128), bf16)

        def store(block, lanes, low, high):
            keep[block, :, lanes] = jnp.where(keep_low, low, high)
            send[block, :, lanes] = jnp.where(keep_low, high, low)

        for s in range(NBLK):
            at = 2 * s * IN_ROWS
            store(s, slice(0, 3 * GW), val[at : at + IN_ROWS], val[at + IN_ROWS : at + 2 * IN_ROWS])
            store(s, slice(3 * GW, IN_COLS), jnp.concatenate([small[s].astype(bf16), zeros[SMALL_ROWS:]], axis=0), zeros)


def finish(bits, dq, dk, dv, xa, xb, fa, fb, weight, vec, up_sum, masks, recv):
    tok = xa.shape[0]
    piece = lambda j: 1 - j
    by_head = pl.BlockSpec((HG, HD, tok), lambda j, y: (0, 0, piece(j)))
    outs = [sds((tok, D), f32), sds((tok, D), bf16)] + [sds((NBLK, IN_ROWS, IN_COLS), bf16)] * 2
    return pcall(
        functools.partial(finish_body, tok, masks),
        "finish",
        bits,
        (dq, dk, dv, xa, xb, fa, fb, weight, weight, weight, vec, up_sum, *recv),
        outs,
        [pl.BlockSpec((GW, tok), lambda j, y: (0, piece(j))), by_head, by_head]
        + [full(v.shape) for v in (xa, xb, fa, fb)] + weight_specs() + [full(vec.shape), full(up_sum.shape)]
        + [pl.BlockSpec((2 * GW, r.shape[1] // 2), lambda j, y: (0, piece(j))) for r in recv],
        [full(o.shape) for o in outs],
        grid=(2,),
        scratch=[
            pltpu.VMEM((3 * GW, tok), bf16), pltpu.VMEM((GW, tok), f32), pltpu.VMEM((D, 3 * GW), f32),
            pltpu.VMEM((16, D), f32), pltpu.VMEM((8, 3 * GW), f32), pltpu.VMEM((NBLK, SMALL_ROWS, 128), f32),
        ],
        flops=4 * tok * 3 * GW * (tok + 2 * D),
    )


def input_grad_body(x_ref, gain, own, got, gres, out):
    xh, rs = normalise(x_ref[...].astype(f32))
    dyg = (own[...] + got[...].astype(f32)) * row(gain)
    m1 = jnp.mean(dyg, axis=-1, keepdims=True)
    m2 = jnp.mean(dyg * xh, axis=-1, keepdims=True)
    out[...] = gres[...] + rs * (dyg - m1 - xh * m2)


def unpack_mlp_body(bits, near, far, down, up, att):
    low = bits[3] == 0
    halves = [
        jnp.concatenate([v[p, x] for p in range(2) for x in range(2)], axis=0).astype(f32)
        for v in (jnp.where(low, near[...], far[...]), jnp.where(low, far[...], near[...]))
    ]
    for c, half in enumerate(halves):
        lanes = slice(c * HALF, (c + 1) * HALF)
        down[:, lanes] = half[0:DOWN_ROWS]
        for j in range(4):
            at = DOWN_ROWS + j * UP_ROWS
            up[:, (c * 4 + j) * HALF : (c * 4 + j + 1) * HALF] = half[at : at + UP_ROWS]
        att[:, lanes] = half[DOWN_ROWS + 4 * UP_ROWS : MLP_ROWS]


VEC_UNITS = (1, 1, 3, 1, 1, 1, 1, 4)


def unpack_in_body(bits, near, far, out, *vecs):
    low = bits[3] == 0
    lower = jnp.where(low, near[...], far[...])
    upper = jnp.where(low, far[...], near[...])
    val = jnp.concatenate([lower[0], lower[1], upper[0], upper[1]], axis=0).astype(f32)
    for part in range(3):
        for y in range(2):
            src = (y * 3 + part) * GW
            dst = (part * 2 + y) * GW
            out[:, dst : dst + GW] = val[:, src : src + GW]
    row = 0
    for ref, units in zip(vecs, VEC_UNITS, strict=True):
        line = jnp.concatenate([val[row + k : row + k + 1, 6 * GW : 6 * GW + UNIT] for k in range(units)], axis=1)
        ref[...] = line[0]
        row += units


def swap(value, axis, offset):
    count = lax.axis_size(axis)
    return lax.ppermute(value, axis, [(i, i ^ offset) for i in range(count)])


def pick(value, index, dim):
    return lax.dynamic_index_in_dim(value, index, dim, keepdims=False)


def halve(pieces, index, dim):
    def part(i):
        return sum(pick(p, i, dim).astype(f32) for p in pieces).astype(bf16)

    return part(1 - index), part(index)


def split_first_body(bits, keep, got, send_a, keep_a, send_b, keep_b):
    ybit, xbit = bits[0], bits[1]
    total = lambda *at: keep[(0, *at)] + got[(0, *at)]
    for j in range(2):
        send_a[0, j] = total(j, 0, 1 - xbit)
        keep_a[0, j] = total(j, 0, xbit)
        send_b[0, j] = total(1 - ybit, 1, j)
        keep_b[0, j] = total(ybit, 1, j)


def split_first(bits, keep, got):
    rows, cols = keep.shape[1] // 4, keep.shape[2]
    view = lambda v: v.reshape(4, 2, 2, 2, rows, cols)
    block = pl.BlockSpec((1, 2, 2, 2, rows, cols), lambda j: (j, 0, 0, 0, 0, 0))
    return kcall(
        split_first_body, "split_first", (bits, view(keep), view(got)), [sds((4, 2, rows, cols), bf16)] * 4, grid=(4,),
        in_specs=[SMEM, block, block], out_specs=[pl.BlockSpec((1, 2, rows, cols), lambda j: (j, 0, 0, 0))] * 4,
    )


def split_second_body(bits, ka, ga, kb, gb, send_a, keep_a, send_b, keep_b):
    for keep, got, send_to, keep_to, bit in ((ka, ga, send_a, keep_a, bits[0]), (kb, gb, send_b, keep_b, bits[1])):
        total = lambda j: keep[0, j] + got[0, j]
        send_to[0] = total(1 - bit)
        keep_to[0] = total(bit)


def split_second(bits, ka, ga, kb, gb):
    rows, cols = ka.shape[2:]
    block = pl.BlockSpec((1, 2, rows, cols), lambda j: (j, 0, 0, 0))
    return kcall(
        split_second_body, "split_second", (bits, ka, ga, kb, gb), [sds((4, rows, cols), bf16)] * 4, grid=(4,),
        in_specs=[SMEM] + [block] * 4, out_specs=[pl.BlockSpec((1, rows, cols), lambda j: (j, 0, 0))] * 4,
    )


def split_third_body(bits, ka, ga, kb, gb, send, keep):
    low = bits[2] % 2
    for h in range(2):
        for p, (own, got) in enumerate(((ka, ga), (kb, gb))):
            send[h, p] = own[2 * h + 1 - low] + got[2 * h + 1 - low]
            keep[h, p] = own[2 * h + low] + got[2 * h + low]


def split_third(bits, ka, ga, kb, gb):
    rows, cols = ka.shape[1:]
    return kcall(
        split_third_body, "split_third", (bits, ka, ga, kb, gb), [sds((2, 2, rows, cols), bf16)] * 2,
        in_specs=[SMEM] + [VMEM] * 4, out_specs=[VMEM] * 2,
    )


def spread(mine, xbit):
    other = swap(mine, "rep", 2)
    dim = mine.ndim - 2
    pair = jnp.stack([jnp.where(xbit == 0, mine, other), jnp.where(xbit == 0, other, mine)], axis=dim)
    return pair, swap(pair, "rep", 1)


def tie(*values):
    return lax.optimization_barrier(values)


def body(tile_embed, doc_ids, norm1_gain, norm1_shift, in_weight, in_bias, out_weight, out_bias,
         norm2_gain, norm2_shift, up_weight, up_bias, down_weight, down_bias, cotangent):
    tok = tile_embed.shape[1]
    count = lax.axis_size("seq")
    assert SEG0 == 2 * tok and tok % 512 == 0
    nodes = count // 2
    masks = [m for m in range(1, min(nodes, 2 ** (BRANCHES - 1)))]
    whole = count == 8 and lax.axis_size("rep") == 4
    index = lax.axis_index("seq")
    ybit = index % 2
    z = index // 2
    rep = lax.axis_index("rep")
    core, xbit = rep % 2, rep // 2
    bits = jnp.stack([ybit, xbit, z, core if whole else jnp.zeros_like(core)]).astype(jnp.int32)
    y = bits


    x, cot = tile_embed[0], cotangent[0]
    x_oth = swap(x, "seq", 1)
    ids_oth = swap(doc_ids, "seq", 1)

    args = (norm1_gain, norm1_shift, in_bias, in_weight)
    first_a, qa, ka, va, doc_a, *out_a = project(y, x, doc_ids, *args)
    remote_a = [swap(out_a[min(m.bit_length(), 2) - 1], "seq", 2 * m) for m in masks]
    gdown = cot_down(cot, down_weight)
    x_oth, ids_oth, gdown = tie(x_oth, ids_oth, gdown)
    first_b, qb, kb, vb, doc_b, *out_b = project(y, x_oth, ids_oth, *args)
    remote_b = [swap(out_b[min(m.bit_length(), 2) - 1], "seq", 2 * m) for m in masks]

    kb, *remote_a = tie(kb, *remote_a)
    qs, ks, vs, docs = (qa, qb), (ka, kb), (va, vb), (doc_a, doc_b)
    part = own_forward(y, qs, ks, vs, docs)
    remote = [r for pair in zip(remote_a, remote_b, strict=True) for r in pair]
    mown, msend, merged, lse = far_forward(y, qs, docs, part, masks, remote)
    moth = swap(msend, "seq", 1)
    (gelu, gelu_t, gpre, up_sum, resid1, second_t, gattn_t, gmown, gmsend, gres, vec) = mlp(
        y, x, mown, moth, out_bias, norm2_gain, norm2_shift, out_weight, up_weight, up_bias, gdown, cot
    )
    gmoth = swap(gmsend, "seq", 1)

    g_send, g_keep = mlp_grads(y, gelu_t, cot, second_t, gpre, mown, moth, gattn_t)
    gmoth, g_send = tie(gmoth, g_send)
    if whole:
        g_got = swap(g_send, "rep", 1)

    gs = (gmown, gmoth)
    dq, *sends = far_backward(y, qs, docs, gs, merged, lse, masks, remote)
    recv = [swap(s, "seq", 2 * m) for s, m in zip(sends, masks, strict=True)]
    if whole:
        dq, g_got = tie(dq, g_got)
        send_a, keep_a, send_b, keep_b = split_first(bits, g_keep, g_got)
        dq, send_a, send_b = tie(dq, send_a, send_b)
        got_a, got_b = swap(send_a, "rep", 2), swap(send_b, "seq", 1)
    dq, dk, dv = own_backward(y, qs, ks, vs, docs, gs, merged, lse, dq)
    if whole:
        dq, got_a, got_b = tie(dq, got_a, got_b)
        send_a, keep_a, send_b, keep_b = split_second(bits, keep_a, got_a, keep_b, got_b)
        dq, send_a, send_b = tie(dq, send_a, send_b)
        got_a, got_b = swap(send_a, "seq", 1), swap(send_b, "rep", 2)
    gfirst_a, gfirst_b, i_send, i_keep = finish(
        bits, dq, dk, dv, x, x_oth, first_a, first_b, in_weight, vec, up_sum, masks, recv
    )
    gfirst_got = swap(gfirst_b, "seq", 1)
    if whole:
        i_send, got_a, got_b = tie(i_send, got_a, got_b)
        i_got = swap(i_send, "rep", 1)
        g_send, g_keep = split_third(bits, keep_a, got_a, keep_b, got_b)
        g_got = swap(g_send, "seq", 2)
        view = lambda v: v.reshape(NBLK, 2, IN_ROWS // 2, IN_COLS)
        i_send, i_keep = halve((view(i_keep), view(i_got)), xbit, 1)
        i_got = swap(i_send, "rep", 2)

    result = (resid1 + jnp.dot(gelu, down_weight, preferred_element_type=f32) + down_bias).astype(bf16)
    by_rows = lambda n: pl.BlockSpec((tok // 4, n), lambda j: (j, 0))
    grad_input = kcall(
        input_grad_body, "input_grad", (x, norm1_gain, gfirst_a, gfirst_got, gres), [sds((tok, D), f32)], grid=(4,),
        in_specs=[by_rows(D), full((D,))] + [by_rows(D)] * 3, out_specs=[by_rows(D)],
    )[0]

    if whole:
        g_send, g_keep = halve((g_keep, g_got), z // 2, 0)
        g_got = swap(g_send, "seq", 4)
        view = lambda v: v.reshape(2, 2, 2, IN_ROWS // 2, IN_COLS)
        i_send, i_keep = halve((view(i_keep), view(i_got)), z % 2, 1)
        i_got = swap(i_send, "seq", 2)
        i_send, i_keep = halve((i_keep, i_got), z // 2, 0)
        i_got = swap(i_send, "seq", 4)

        mine = g_keep + g_got
        near, far = spread(mine, xbit)
        g_down, g_up, g_out = kcall(
            unpack_mlp_body, "unpack_mlp", (bits, near, far),
            [sds((DOWN_ROWS, D), f32), sds((UP_ROWS, FF), f32), sds((UP_ROWS, D), f32)],
            in_specs=[SMEM, VMEM, VMEM], out_specs=[VMEM] * 3,
        )

        total = i_keep + i_got
        mine = pick(total, ybit, 0)
        got = swap(pick(total, 1 - ybit, 0), "seq", 1)
        width = 3 * GW
        low, high = jnp.where(ybit == 0, mine, got), jnp.where(ybit == 0, got, mine)
        vec = mine[:, width:] + got[:, width:]
        near, far = spread(jnp.concatenate([low[:, :width], high[:, :width], vec], axis=1), xbit)
        g_in, *vecs = kcall(
            unpack_in_body, "unpack_in", (bits, near, far),
            [sds((2 * IN_ROWS, 3 * D), f32)] + [sds((UNIT * n,), f32) for n in VEC_UNITS],
            in_specs=[SMEM, VMEM, VMEM], out_specs=[VMEM] * 9,
        )
    else:
        total = lambda v: lax.psum(lax.psum_scatter(v, "seq", scatter_dimension=0, tiled=True).astype(bf16), "rep").astype(f32)
        both = jnp.stack([g_keep, g_send], axis=0).astype(f32)
        cut = lambda lo, hi: both[:, :, lo:hi]
        g_down = total(cut(0, DOWN_ROWS).transpose(1, 2, 0, 3).reshape(FF, D))
        g_up = total(cut(DOWN_ROWS, DOWN_ROWS + 4 * UP_ROWS).reshape(2, NBLK, 4, UP_ROWS, HALF).transpose(1, 3, 0, 2, 4).reshape(D, FF))
        g_out = total(cut(DOWN_ROWS + 4 * UP_ROWS, MLP_ROWS).transpose(1, 2, 0, 3).reshape(D, D))
        both = jnp.stack([i_keep, i_send], axis=1)[..., : 3 * GW].astype(f32).reshape(D, 3, 1, GW)
        g_in = total(jnp.where((jnp.arange(2) == ybit)[None, None, :, None], both, 0.0).reshape(D, 3 * D))
        small = i_keep[:, :, 3 * GW : 3 * GW + UNIT].astype(f32)
        ends = np.cumsum((0,) + VEC_UNITS)
        vecs = [total(small[:, lo:hi].reshape(-1)) for lo, hi in zip(ends[:-1], ends[1:], strict=True)]
    n1_gain, n1_shift, b_in, b_down, n2_gain, n2_shift, b_out, b_up = vecs
    return (
        result[None], grad_input[None], n1_gain, n1_shift, g_in, b_in, g_out, b_out, n2_gain, n2_shift, g_up, b_up, g_down, b_down,
    )


def solution(mesh):
    tokens, weights = P("rep", "seq", None), P()
    in_specs = (tokens, P("rep", "seq")) + (weights,) * 12 + (tokens,)
    vec, mat = P("seq"), P("seq", None)
    out_specs = (tokens, tokens, vec, vec, mat, vec, mat, vec, vec, vec, mat, vec, mat, vec)
    return jax.shard_map(body, mesh=mesh, in_specs=in_specs, out_specs=out_specs, check_vma=False)
```

profile of v0, /device:TPU:0, one launch (start us, length us, event | category | flops | bytes accessed | tf_op | source)
XLA Modules:
  0.0 250.6 jit_solution(1813837807827621469)
XLA Ops:
  0.6 3.0 %collective-permute-start = (bf16[512,768]{1,0:T(8,128)(2,1)}, bf16[512,768]{1,0:T(8,128)(2,1)S(1)}, u32[]{:S(2)}, u32[]{:S(2)}) collective-permute-start(bf16[512,768]{1,0:T(8,128)(2,1)} %bitcast.54), channel_id=1, source_target_pairs={{0,4},{4,0},{8,12},{12,8},{16,20},{20,16},{24,28},{28,24},{1,5},{5... | collective-permute-start | bytes 2359304 | tf_op jit(solution)/shard_map/ppermute | solution.py:796
  4.4 5.8 %project.2 = (bf16[768,512]{1,0:T(8,128)(2,1)}, bf16[384,512]{1,0:T(8,128)(2,1)}, bf16[384,512]{1,0:T(8,128)(2,1)}, bf16[384,512]{1,0:T(8,128)(2,1)}, f32[8,512]...) custom-call(s32[4]{0:T(128)} %pad_add_fusion.y_ref.bits, bf16[512,768]{1,0:T(8,128)(2,1)} %bitcast.55, ...), custom_call_target="tpu_custom_call" | custom-call | flops 1308622848 | bytes 14005248 | tf_op jit(solution)/shard_map/project/pallas_call | solution.py:182
  10.2 3.0 %collective-permute-start.3 = (bf16[784,128]{1,0:T(8,128)(2,1)}, bf16[784,128]{1,0:T(8,128)(2,1)S(1)}, u32[]{:S(2)}, u32[]{:S(2)}) collective-permute-start(bf16[784,128]{1,0:T(8,128)(2,1)} %get-tuple-element.110), channel_id=1, source_target_pairs={{0,16},{4,20},{8,24},{12,28},{16,0},{20,4},{24,8},{28,12},{1,17},{... | collective-permute-start | bytes 602120 | tf_op jit(solution)/shard_map/ppermute | solution.py:796
  13.3 1.3 collective-permute-start.4
  14.8 7.2 %cot_down.1.gdown = f32[512,3072]{1,0:T(8,128)} custom-call(bf16[512,768]{1,0:T(8,128)(2,1)} %bitcast.64, bf16[3072,768]{1,0:T(8,128)(2,1)} %down.1), custom_call_target="tpu_custom_call" | custom-call | flops 2415919104 | bytes 11796480 | tf_op jit(solution)/shard_map/cot_down/pallas_call | solution.py:57
  23.5 5.8 %project.3 = (bf16[768,512]{1,0:T(8,128)(2,1)}, bf16[384,512]{1,0:T(8,128)(2,1)}, bf16[384,512]{1,0:T(8,128)(2,1)}, bf16[384,512]{1,0:T(8,128)(2,1)}, f32[8,512]...) custom-call(s32[4]{0:T(128)} %pad_add_fusion.y_ref.bits, bf16[512,768]{1,0:T(8,128)(2,1)} %copy-done, ...), custom_call_target="tpu_custom_call" | custom-call | flops 1308622848 | bytes 14005248 | tf_op jit(solution)/shard_map/project/pallas_call | solution.py:182
  29.3 1.8 collective-permute-start.5
  31.2 2.0 collective-permute-start.6
  33.7 1.8 collective-permute-done.2.rest_0_
  35.5 10.8 %own_forward.1.part = f32[8,64,1024]{2,1,0:T(8,128)} custom-call(s32[4]{0:T(128)} %pad_add_fusion.y_ref.bits, bf16[384,512]{1,0:T(8,128)(2,1)} %get-tuple-element.101.qa, bf16[384,512]{1,0:T(8,128)(2,1)} %get-tuple-element.104.qb, bf16[384,512]{1,0:T(8,128)(2,1)} %get-tuple-element.107.ka, bf16[384,512]{1,0:T(8,128)(2,1)} %get-tuple-element.111.kb, ...), custom_call_target="tpu_custom_call" | custom-call | flops 2147483648 | bytes 4489232 | tf_op jit(solution)/shard_map/own_forward/pallas_call | solution.py:57
  46.4 3.7 %collective-permute-done.7.rest_5_ = bf16[784,128]{1,0:T(8,128)(2,1)S(1)} collective-permute-done((bf16[784,128]{1,0:T(8,128)(2,1)}, bf16[784,128]{1,0:T(8,128)(2,1)S(1)}, u32[]{:S(2)}, u32[]{:S(2)}) %collective-permute-start.7) | collective-permute-done | bytes 200736 | tf_op jit(solution)/shard_map/ppermute | solution.py:796
  51.6 9.9 %far_forward.1 = (bf16[384,512]{1,0:T(8,128)(2,1)}, bf16[384,512]{1,0:T(8,128)(2,1)}, f32[8,48,1024]{2,1,0:T(8,128)}, f32[8,8,1024]{2,1,0:T(8,128)}) custom-call(s32[4]{0:T(128)} %pad_add_fusion.y_ref.bits, bf16[384,512]{1,0:T(8,128)(2,1)} %get-tuple-element.101.qa, bf16[384,512]{1,0:T(8,128)(2,1)} %get-tuple-element.104.qb, ...), custom_call_target="tpu_custom_call" | custom-call | flops 805306368 | bytes 7143440 | tf_op jit(solution)/shard_map/far_forward/pallas_call | solution.py:57
  61.5 1.6 collective-permute-start.8
  63.1 6.9 %collective-permute-done.8.moth = bf16[384,512]{1,0:T(8,128)(2,1)S(1)} collective-permute-done((bf16[384,512]{1,0:T(8,128)(2,1)}, bf16[384,512]{1,0:T(8,128)(2,1)S(1)}, u32[]{:S(2)}, u32[]{:S(2)}) %collective-permute-start.8) | collective-permute-done | bytes 393248 | tf_op jit(solution)/shard_map/ppermute | solution.py:796
  70.7 22.5 %mlp.1 = (bf16[512,3072]{1,0:T(8,128)(2,1)}, bf16[3072,512]{1,0:T(8,128)(2,1)}, bf16[512,3072]{1,0:T(8,128)(2,1)}, f32[8,3072]{1,0:T(8,128)}, f32[512,768]{1,0:T...) custom-call(s32[4]{0:T(128)} %pad_add_fusion.y_ref.bits, ...), custom_call_target="tpu_custom_call" | custom-call | flops 6845104128 | bytes 29709328 | tf_op jit(solution)/shard_map/mlp/pallas_call | solution.py:57
  93.2 1.6 collective-permute-start.9
  94.8 12.6 %mlp_grads.1 = (bf16[8,864,384]{2,1,0:T(8,128)(2,1)}, bf16[8,864,384]{2,1,0:T(8,128)(2,1)}) custom-call(s32[4]{0:T(128)} %pad_add_fusion.y_ref.bits, bf16[3072,512]{1,0:T(8,128)(2,1)} %get-tuple-element.126.gelu_t, bf16[512,768]{1,0:T(8,128)(2,1)} %bitcast.66, bf16[768,512]{1,0:T(8,128)(2,1)} %get-tuple-element.127.second_t, ...), custom_call_target="tpu_custom_call" | custom-call | flops 5435817984 | bytes 20054016 | tf_op jit(solution)/shard_map/mlp_grads/pallas_call | solution.py:182
  108.1 12.1 %far_backward.1 = (f32[8,48,1024]{2,1,0:T(8,128)}, bf16[768,512]{1,0:T(8,128)(2,1)}, bf16[768,256]{1,0:T(8,128)(2,1)}, bf16[768,256]{1,0:T(8,128)(2,1)}) custom-call(s32[4]{0:T(128)} %pad_add_fusion.y_ref.bits, bf16[384,512]{1,0:T(8,128)(2,1)} %get-tuple-element.101.qa, bf16[384,512]{1,0:T(8,128)(2,1)} %get-tuple-element.104.qb, ...), custom_call_target="tpu_custom_call" | custom-call | flops 2013265920 | bytes 8192016 | tf_op jit(solution)/shard_map/far_backward/pallas_call | solution.py:57
  120.3 6.8 %split_first.1 = (bf16[4,2,216,384]{3,2,1,0:T(8,128)(2,1)}, bf16[4,2,216,384]{3,2,1,0:T(8,128)(2,1)}, bf16[4,2,216,384]{3,2,1,0:T(8,128)(2,1)}, bf16[4,2,216,384]{3,2,1,0:T(8,128)(2,1)}) custom-call(s32[4]{0:T(128)} %pad_add_fusion.y_ref.bits, bf16[4,2,2,2,216,384]{5,4,3,2,1,0:T(8,128)(2,1)} %bitcast.59, bf16[4,2,2,2,216,384]{5,4,3,2,1,0:T(8,128)(2,1)} %bitcast.9.got), custom_call_target="tpu_custom_call" | custom-call | bytes 15925264 | tf_op jit(solution)/shard_map/split_first/pallas_call | solution.py:57
  127.1 1.5 collective-permute-start.11
  129.3 2.1 collective-permute-start.14
  131.3 2.1 collective-permute-start.15
  133.4 23.2 %own_backward.1 = (bf16[384,1024]{1,0:T(8,128)(2,1)}, f32[8,48,1024]{2,1,0:T(8,128)}, f32[8,48,1024]{2,1,0:T(8,128)}) custom-call(s32[4]{0:T(128)} %pad_add_fusion.y_ref.bits, bf16[384,512]{1,0:T(8,128)(2,1)} %get-tuple-element.101.qa, bf16[384,512]{1,0:T(8,128)(2,1)} %get-tuple-element.104.qb, bf16[384,512]{1,0:T(8,128)(2,1)} %get-tuple-element.107.ka, ...), custom_call_target="tpu_custom_call" | custom-call | flops 5368709120 | bytes 10518544 | tf_op jit(solution)/shard_map/own_backward/pallas_call | solution.py:57
  156.6 1.5 collective-permute-done.11.ga
  158.2 1.2 collective-permute-done.12.gb
  160.4 4.7 %split_second.1 = (bf16[4,216,384]{2,1,0:T(8,128)(2,1)}, bf16[4,216,384]{2,1,0:T(8,128)(2,1)}, bf16[4,216,384]{2,1,0:T(8,128)(2,1)}, bf16[4,216,384]{2,1,0:T(8,128)(2,1)}) custom-call(s32[4]{0:T(128)} %pad_add_fusion.y_ref.bits, bf16[4,2,216,384]{3,2,1,0:T(8,128)(2,1)} %get-tuple-element.146.ka, bf16[4,2,216,384]{3,2,1,0:T(8,128)(2,1)} %copy-done.3, ...), custom_call_target="tpu_custom_call" | custom-call | bytes 7962640 | tf_op jit(solution)/shard_map/split_second/pallas_call | solution.py:57
  167.2 14.7 %finish.1 = (f32[512,768]{1,0:T(8,128)}, bf16[512,768]{1,0:T(8,128)(2,1)}, bf16[8,48,1280]{2,1,0:T(8,128)(2,1)}, bf16[8,48,1280]{2,1,0:T(8,128)(2,1)}) custom-call(s32[4]{0:T(128)} %pad_add_fusion.y_ref.bits, bf16[384,1024]{1,0:T(8,128)(2,1)} %get-tuple-element.152.dq, f32[8,48,1024]{2,1,0:T(8,128)} %get-tuple-element.153.dk, ...), custom_call_target="tpu_custom_call" | custom-call | flops 4831838208 | bytes 23789568 | tf_op jit(solution)/shard_map/finish/pallas_call | solution.py:182
  183.0 3.0 %split_third.1 = (bf16[2,2,216,384]{3,2,1,0:T(8,128)(2,1)}, bf16[2,2,216,384]{3,2,1,0:T(8,128)(2,1)}) custom-call(s32[4]{0:T(128)} %pad_add_fusion.y_ref.bits, bf16[4,216,384]{2,1,0:T(8,128)(2,1)} %get-tuple-element.174.ka, bf16[4,216,384]{2,1,0:T(8,128)(2,1)} %copy-done.11, bf16[4,216,384]{2,1,0:T(8,128)(2,1)} %get-tuple-element.176.kb, ...), custom_call_target="tpu_custom_call" | custom-call | bytes 3981328 | tf_op jit(solution)/shard_map/split_third/pallas_call | solution.py:57
  187.2 1.3 collective-permute-start.20
  188.5 14.1 %collective-permute-done.26 = bf16[2,2,216,384]{3,2,1,0:T(8,128)(2,1)} collective-permute-done((bf16[2,2,216,384]{3,2,1,0:T(8,128)(2,1)}, bf16[2,2,216,384]{3,2,1,0:T(8,128)(2,1)}, u32[]{:S(2)}, u32[]{:S(2)}) %collective-permute-start.26) | collective-permute-done | bytes 663584 | tf_op jit(solution)/shard_map/ppermute | solution.py:796
  203.7 1.3 collective-permute-start.27
  205.1 1.1 collective-permute-start.21
  206.3 6.0 %fusion.11 = f32[512,768]{1,0:T(8,128)S(1)} fusion(bf16[512,3072]{1,0:T(8,128)(2,1)} %get-tuple-element.123, bf16[3072,768]{1,0:T(8,128)(2,1)} %down.1), kind=kOutput, calls=%fused_computation.33 | convolution fusion | flops 2415919104 | bytes 9437184 | tf_op jit(solution)/shard_map/dot_general | solution.py:945
  212.2 1.6 collective-permute-start.16
  213.8 2.4 collective-permute-done.21
  216.2 2.6 %collective-permute-start.22 = (bf16[2,24,1280]{2,1,0:T(8,128)(2,1)S(1)}, bf16[2,24,1280]{2,1,0:T(8,128)(2,1)S(1)}, u32[]{:S(2)}, u32[]{:S(2)}) collective-permute-start(bf16[2,24,1280]{2,1,0:T(8,128)(2,1)S(1)} %fusion.10), channel_id=1, source_target_pairs={{0,16},{4,20},{8,24},{12,28},{16,0},{20,4},{24,8},{28,12},{1,17},{... | collective-permute-start | bytes 368648 | tf_op jit(solution)/shard_map/ppermute | solution.py:796
  218.8 2.5 %collective-permute-done.27 = bf16[2,216,384]{2,1,0:T(8,128)(2,1)S(1)} collective-permute-done((bf16[2,216,384]{2,1,0:T(8,128)(2,1)S(1)}, bf16[2,216,384]{2,1,0:T(8,128)(2,1)S(1)}, u32[]{:S(2)}, u32[]{:S(2)}) %collective-permute-start.27) | collective-permute-done | bytes 331808 | tf_op jit(solution)/shard_map/ppermute | solution.py:796
  221.3 1.1 fusion.3
  222.4 1.4 collective-permute-start.28
  223.8 1.4 collective-permute-done.22
  225.3 1.6 collective-permute-start.23
  226.9 5.3 %collective-permute-done.28 = bf16[2,216,384]{2,1,0:T(8,128)(2,1)S(1)} collective-permute-done((bf16[2,216,384]{2,1,0:T(8,128)(2,1)S(1)}, bf16[2,216,384]{2,1,0:T(8,128)(2,1)S(1)}, u32[]{:S(2)}, u32[]{:S(2)}) %collective-permute-start.28) | collective-permute-done | bytes 331808 | tf_op jit(solution)/shard_map/ppermute | solution.py:796
  232.3 1.4 collective-permute-start.24
  233.8 3.3 %collective-permute-done.24 = bf16[24,2432]{1,0:T(8,128)(2,1)S(1)} collective-permute-done((bf16[24,2432]{1,0:T(8,128)(2,1)S(1)}, bf16[24,2432]{1,0:T(8,128)(2,1)S(1)}, u32[]{:S(2)}, u32[]{:S(2)}) %collective-permute-start.24) | collective-permute-done | bytes 116768 | tf_op jit(solution)/shard_map/ppermute | solution.py:796
  237.4 1.1 fusion
  239.4 4.7 %input_grad.1 = f32[512,768]{1,0:T(8,128)} custom-call(bf16[512,768]{1,0:T(8,128)(2,1)} %bitcast.58, f32[768]{0:T(1024)} %gain.5, f32[512,768]{1,0:T(8,128)} %get-tuple-element.162.own, bf16[512,768]{1,0:T(8,128)(2,1)} %copy-done.8, f32[512,768]{1,0:T(8,128)} %get-tuple-element.164.gres), custom_call_target="tpu_custom_call" | custom-call | bytes 6294528 | tf_op jit(solution)/shard_map/input_grad/pallas_call | solution.py:57
  245.0 2.9 %unpack_mlp.1 = (f32[384,768]{1,0:T(8,128)}, f32[96,3072]{1,0:T(8,128)}, f32[96,768]{1,0:T(8,128)}) custom-call(s32[4]{0:T(128)} %pad_add_fusion.y_ref.bits, bf16[2,2,216,384]{3,2,1,0:T(8,128)(2,1)} %copy-done.1, bf16[2,2,216,384]{3,2,1,0:T(8,128)(2,1)} %copy-done.9), custom_call_target="tpu_custom_call" | custom-call | bytes 3981328 | tf_op jit(solution)/shard_map/unpack_mlp/pallas_call | solution.py:57
  248.5 2.1 unpack_in.1
  (95 shorter events, 16.3 us)
Async XLA Ops:
  0.6 21.4 %collective-permute-start = (bf16[512,768]{1,0:T(8,128)(2,1)}, bf16[512,768]{1,0:T(8,128)(2,1)S(1)}, u32[]{:S(2)}, u32[]{:S(2)}) collective-permute-start(bf16[512,768]{1,0:T(8,128)(2,1)} %bitcast.54), channel_id=1, source_target_pairs={{0,4},{4,0},{8,12},{12,8},{16,20},{20,16},{24,28},{28,24},{1,5},{5... | collective-permute-start | bytes 2359304 | tf_op jit(solution)/shard_map/ppermute | solution.py:796
  3.7 18.4 %collective-permute-start.1 = (s32[1,512]{1,0:T(1,128)}, s32[1,512]{1,0:T(1,128)S(1)}, u32[]{:S(2)}, u32[]{:S(2)}) collective-permute-start(s32[1,512]{1,0:T(1,128)} %ids_ref.1), channel_id=1, source_target_pairs={{0,4},{4,0},{8,12},{12,8},{16,20},{20,16},{24,28},{28,24},{1,5},{5... | collective-permute-start | bytes 6152 | tf_op jit(solution)/shard_map/ppermute | solution.py:796
  10.2 22.9 %collective-permute-start.3 = (bf16[784,128]{1,0:T(8,128)(2,1)}, bf16[784,128]{1,0:T(8,128)(2,1)S(1)}, u32[]{:S(2)}, u32[]{:S(2)}) collective-permute-start(bf16[784,128]{1,0:T(8,128)(2,1)} %get-tuple-element.110), channel_id=1, source_target_pairs={{0,16},{4,20},{8,24},{12,28},{16,0},{20,4},{24,8},{28,12},{1,17},{... | collective-permute-start | bytes 602120 | tf_op jit(solution)/shard_map/ppermute | solution.py:796
  13.3 20.5 %collective-permute-start.4 = (bf16[784,128]{1,0:T(8,128)(2,1)}, bf16[784,128]{1,0:T(8,128)(2,1)S(1)}, u32[]{:S(2)}, u32[]{:S(2)}) collective-permute-start(bf16[784,128]{1,0:T(8,128)(2,1)} %get-tuple-element.110), channel_id=1, source_target_pairs={{0,24},{4,28},{8,16},{12,20},{16,8},{20,12},{24,0},{28,4},{1,25},{... | collective-permute-start | bytes 602120 | tf_op jit(solution)/shard_map/ppermute | solution.py:796
  14.6 20.9 %collective-permute-start.2 = (bf16[784,256]{1,0:T(8,128)(2,1)}, bf16[784,256]{1,0:T(8,128)(2,1)S(1)}, u32[]{:S(2)}, u32[]{:S(2)}) collective-permute-start(bf16[784,256]{1,0:T(8,128)(2,1)} %get-tuple-element.109), channel_id=1, source_target_pairs={{0,8},{4,12},{8,0},{12,4},{16,24},{20,28},{24,16},{28,20},{1,9},{5... | collective-permute-start | bytes 1204232 | tf_op jit(solution)/shard_map/ppermute | solution.py:796
  22.6 0.9 copy-start
  29.3 20.8 %collective-permute-start.5 = (bf16[784,256]{1,0:T(8,128)(2,1)}, bf16[784,256]{1,0:T(8,128)(2,1)S(1)}, u32[]{:S(2)}, u32[]{:S(2)}) collective-permute-start(bf16[784,256]{1,0:T(8,128)(2,1)} %get-tuple-element.115), channel_id=1, source_target_pairs={{0,8},{4,12},{8,0},{12,4},{16,24},{20,28},{24,16},{28,20},{1,9},{5... | collective-permute-start | bytes 1204232 | tf_op jit(solution)/shard_map/ppermute | solution.py:796
  31.2 15.2 %collective-permute-start.6 = (bf16[784,128]{1,0:T(8,128)(2,1)}, bf16[784,128]{1,0:T(8,128)(2,1)S(1)}, u32[]{:S(2)}, u32[]{:S(2)}) collective-permute-start(bf16[784,128]{1,0:T(8,128)(2,1)} %get-tuple-element.117), channel_id=1, source_target_pairs={{0,16},{4,20},{8,24},{12,28},{16,0},{20,4},{24,8},{28,12},{1,17},{... | collective-permute-start | bytes 602120 | tf_op jit(solution)/shard_map/ppermute | solution.py:796
  33.1 13.2 %copy-start.16 = (bf16[784,128]{1,0:T(8,128)(2,1)}, bf16[784,128]{1,0:T(8,128)(2,1)S(1)}, u32[]{:S(2)}) copy-start(bf16[784,128]{1,0:T(8,128)(2,1)S(1)} %collective-permute-done.3.rest_2_) | copy-start | bytes 602116
  33.1 17.0 %collective-permute-start.7 = (bf16[784,128]{1,0:T(8,128)(2,1)}, bf16[784,128]{1,0:T(8,128)(2,1)S(1)}, u32[]{:S(2)}, u32[]{:S(2)}) collective-permute-start(bf16[784,128]{1,0:T(8,128)(2,1)} %get-tuple-element.117), channel_id=1, source_target_pairs={{0,24},{4,28},{8,16},{12,20},{16,8},{20,12},{24,0},{28,4},{1,25},{... | collective-permute-start | bytes 602120 | tf_op jit(solution)/shard_map/ppermute | solution.py:796
  33.7 12.6 %copy-start.17 = (bf16[784,128]{1,0:T(8,128)(2,1)}, bf16[784,128]{1,0:T(8,128)(2,1)S(1)}, u32[]{:S(2)}) copy-start(bf16[784,128]{1,0:T(8,128)(2,1)S(1)} %collective-permute-done.4.rest_4_) | copy-start | bytes 602116
  35.5 10.9 %copy-start.13 = (bf16[784,256]{1,0:T(8,128)(2,1)}, bf16[784,256]{1,0:T(8,128)(2,1)S(1)}, u32[]{:S(2)}) copy-start(bf16[784,256]{1,0:T(8,128)(2,1)S(1)} %collective-permute-done.2.rest_0_) | copy-start | bytes 1204228
  46.4 3.8 %copy-start.18 = (bf16[784,128]{1,0:T(8,128)(2,1)}, bf16[784,128]{1,0:T(8,128)(2,1)S(1)}, u32[]{:S(2)}) copy-start(bf16[784,128]{1,0:T(8,128)(2,1)S(1)} %collective-permute-done.6.rest_3_) | copy-start | bytes 602116
  61.5 8.5 %collective-permute-start.8 = (bf16[384,512]{1,0:T(8,128)(2,1)}, bf16[384,512]{1,0:T(8,128)(2,1)S(1)}, u32[]{:S(2)}, u32[]{:S(2)}) collective-permute-start(bf16[384,512]{1,0:T(8,128)(2,1)} %get-tuple-element.120), channel_id=1, source_target_pairs={{0,4},{4,0},{8,12},{12,8},{16,20},{20,16},{24,28},{28,24},{1,5},{5... | collective-permute-start | bytes 1179656 | tf_op jit(solution)/shard_map/ppermute | solution.py:796
  93.2 14.2 %collective-permute-start.9 = (bf16[384,512]{1,0:T(8,128)(2,1)}, bf16[384,512]{1,0:T(8,128)(2,1)S(1)}, u32[]{:S(2)}, u32[]{:S(2)}) collective-permute-start(bf16[384,512]{1,0:T(8,128)(2,1)} %get-tuple-element.125), channel_id=1, source_target_pairs={{0,4},{4,0},{8,12},{12,8},{16,20},{20,16},{24,28},{28,24},{1,5},{5... | collective-permute-start | bytes 1179656 | tf_op jit(solution)/shard_map/ppermute | solution.py:796
  107.4 12.9 %collective-permute-start.10 = (bf16[8,864,384]{2,1,0:T(8,128)(2,1)}, bf16[8,864,384]{2,1,0:T(8,128)(2,1)}, u32[]{:S(2)}, u32[]{:S(2)}) collective-permute-start(bf16[8,864,384]{2,1,0:T(8,128)(2,1)} %get-tuple-element.135), channel_id=1, source_target_pairs={{0,1},{1,0},{2,3},{3,2},{4,5},{5,4},{6,7},{7,6},{8,9},{9,8},{10,11... | collective-permute-start | bytes 15925256 | tf_op jit(solution)/shard_map/ppermute | solution.py:796
  127.1 31.1 %collective-permute-start.11 = (bf16[4,2,216,384]{3,2,1,0:T(8,128)(2,1)}, bf16[4,2,216,384]{3,2,1,0:T(8,128)(2,1)S(1)}, u32[]{:S(2)}, u32[]{:S(2)}) collective-permute-start(bf16[4,2,216,384]{3,2,1,0:T(8,128)(2,1)} %get-tuple-element.143), channel_id=1, source_target_pairs={{0,2},{1,3},{2,0},{3,1},{4,6},{5,7},{6,4},{7,5},{8,10},{9,11},{10,... | collective-permute-start | bytes 3981320 | tf_op jit(solution)/shard_map/ppermute | solution.py:796
  128.5 30.8 %collective-permute-start.12 = (bf16[4,2,216,384]{3,2,1,0:T(8,128)(2,1)}, bf16[4,2,216,384]{3,2,1,0:T(8,128)(2,1)S(1)}, u32[]{:S(2)}, u32[]{:S(2)}) collective-permute-start(bf16[4,2,216,384]{3,2,1,0:T(8,128)(2,1)} %get-tuple-element.144), channel_id=1, source_target_pairs={{0,4},{4,0},{8,12},{12,8},{16,20},{20,16},{24,28},{28,24},{1,5},{5... | collective-permute-start | bytes 3981320 | tf_op jit(solution)/shard_map/ppermute | solution.py:796
  129.1 37.3 %collective-permute-start.13 = (bf16[768,512]{1,0:T(8,128)(2,1)}, bf16[768,512]{1,0:T(8,128)(2,1)S(1)}, u32[]{:S(2)}, u32[]{:S(2)}) collective-permute-start(bf16[768,512]{1,0:T(8,128)(2,1)} %get-tuple-element.159), channel_id=1, source_target_pairs={{0,8},{4,12},{8,0},{12,4},{16,24},{20,28},{24,16},{28,20},{1,9},{5... | collective-permute-start | bytes 2359304 | tf_op jit(solution)/shard_map/ppermute | solution.py:796
  129.3 37.1 %collective-permute-start.14 = (bf16[768,256]{1,0:T(8,128)(2,1)}, bf16[768,256]{1,0:T(8,128)(2,1)}, u32[]{:S(2)}, u32[]{:S(2)}) collective-permute-start(bf16[768,256]{1,0:T(8,128)(2,1)} %get-tuple-element.160), channel_id=1, source_target_pairs={{0,16},{4,20},{8,24},{12,28},{16,0},{20,4},{24,8},{28,12},{1,17},{... | collective-permute-start | bytes 1179656 | tf_op jit(solution)/shard_map/ppermute | solution.py:796
  131.3 35.0 %collective-permute-start.15 = (bf16[768,256]{1,0:T(8,128)(2,1)}, bf16[768,256]{1,0:T(8,128)(2,1)}, u32[]{:S(2)}, u32[]{:S(2)}) collective-permute-start(bf16[768,256]{1,0:T(8,128)(2,1)} %get-tuple-element.161), channel_id=1, source_target_pairs={{0,24},{4,28},{8,16},{12,20},{16,8},{20,12},{24,0},{28,4},{1,25},{... | collective-permute-start | bytes 1179656 | tf_op jit(solution)/shard_map/ppermute | solution.py:796
  158.2 1.2 copy-start.3
  159.3 1.1 copy-start.4
  165.1 16.8 %collective-permute-start.17 = (bf16[4,216,384]{2,1,0:T(8,128)(2,1)}, bf16[4,216,384]{2,1,0:T(8,128)(2,1)S(1)}, u32[]{:S(2)}, u32[]{:S(2)}) collective-permute-start(bf16[4,216,384]{2,1,0:T(8,128)(2,1)} %get-tuple-element.167), channel_id=1, source_target_pairs={{0,4},{4,0},{8,12},{12,8},{16,20},{20,16},{24,28},{28,24},{1,5},{5... | collective-permute-start | bytes 1990664 | tf_op jit(solution)/shard_map/ppermute | solution.py:796
  165.6 16.3 %collective-permute-start.18 = (bf16[4,216,384]{2,1,0:T(8,128)(2,1)}, bf16[4,216,384]{2,1,0:T(8,128)(2,1)S(1)}, u32[]{:S(2)}, u32[]{:S(2)}) collective-permute-start(bf16[4,216,384]{2,1,0:T(8,128)(2,1)} %get-tuple-element.168), channel_id=1, source_target_pairs={{0,2},{1,3},{2,0},{3,1},{4,6},{5,7},{6,4},{7,5},{8,10},{9,11},{10,... | collective-permute-start | bytes 1990664 | tf_op jit(solution)/shard_map/ppermute | solution.py:796
  166.3 0.9 copy-start.7
  181.9 4.3 %copy-start.5 = (bf16[8,48,1280]{2,1,0:T(8,128)(2,1)S(1)}, bf16[8,48,1280]{2,1,0:T(8,128)(2,1)}, u32[]{:S(2)}) copy-start(bf16[8,48,1280]{2,1,0:T(8,128)(2,1)} %get-tuple-element.165) | copy-start | bytes 2949124
  181.9 0.8 copy-start.11
  181.9 1.0 copy-start.12
  182.0 4.2 %collective-permute-start.19 = (bf16[8,48,1280]{2,1,0:T(8,128)(2,1)}, bf16[8,48,1280]{2,1,0:T(8,128)(2,1)S(1)}, u32[]{:S(2)}, u32[]{:S(2)}) collective-permute-start(bf16[8,48,1280]{2,1,0:T(8,128)(2,1)} %get-tuple-element.169), channel_id=1, source_target_pairs={{0,1},{1,0},{2,3},{3,2},{4,5},{5,4},{6,7},{7,6},{8,9},{9,8},{10,11... | collective-permute-start | bytes 2949128 | tf_op jit(solution)/shard_map/ppermute | solution.py:796
  186.0 16.7 %copy-start.10 = (bf16[2,2,216,384]{3,2,1,0:T(8,128)(2,1)S(1)}, bf16[2,2,216,384]{3,2,1,0:T(8,128)(2,1)}, u32[]{:S(2)}) copy-start(bf16[2,2,216,384]{3,2,1,0:T(8,128)(2,1)} %get-tuple-element.178) | copy-start | bytes 1990660
  186.0 16.7 %collective-permute-start.26 = (bf16[2,2,216,384]{3,2,1,0:T(8,128)(2,1)}, bf16[2,2,216,384]{3,2,1,0:T(8,128)(2,1)}, u32[]{:S(2)}, u32[]{:S(2)}) collective-permute-start(bf16[2,2,216,384]{3,2,1,0:T(8,128)(2,1)} %get-tuple-element.179), channel_id=1, source_target_pairs={{0,8},{4,12},{8,0},{12,4},{16,24},{20,28},{24,16},{28,20},{1,9},{5... | collective-permute-start | bytes 1990664 | tf_op jit(solution)/shard_map/ppermute | solution.py:796
  187.2 17.8 %collective-permute-start.20 = (bf16[8,24,1280]{2,1,0:T(8,128)(2,1)}, bf16[8,24,1280]{2,1,0:T(8,128)(2,1)S(1)}, u32[]{:S(2)}, u32[]{:S(2)}) collective-permute-start(bf16[8,24,1280]{2,1,0:T(8,128)(2,1)} %get-tuple-element.189), channel_id=1, source_target_pairs={{0,2},{1,3},{2,0},{3,1},{4,6},{5,7},{6,4},{7,5},{8,10},{9,11},{10,... | collective-permute-start | bytes 1474568 | tf_op jit(solution)/shard_map/ppermute | solution.py:796
  203.7 17.6 %collective-permute-start.27 = (bf16[2,216,384]{2,1,0:T(8,128)(2,1)S(1)}, bf16[2,216,384]{2,1,0:T(8,128)(2,1)S(1)}, u32[]{:S(2)}, u32[]{:S(2)}) collective-permute-start(bf16[2,216,384]{2,1,0:T(8,128)(2,1)S(1)} %fusion.4), channel_id=1, source_target_pairs={{0,16},{4,20},{8,24},{12,28},{16,0},{20,4},{24,8},{28,12},{1,17},{... | collective-permute-start | bytes 995336 | tf_op jit(solution)/shard_map/ppermute | solution.py:796
  205.1 11.0 %collective-permute-start.21 = (bf16[2,2,24,1280]{3,2,1,0:T(8,128)(2,1)S(1)}, bf16[2,2,24,1280]{3,2,1,0:T(8,128)(2,1)S(1)}, u32[]{:S(2)}, u32[]{:S(2)}) collective-permute-start(bf16[2,2,24,1280]{3,2,1,0:T(8,128)(2,1)S(1)} %get-tuple-element.191), channel_id=1, source_target_pairs={{0,8},{4,12},{8,0},{12,4},{16,24},{20,28},{24,16},{28,20},{1,9},{5... | collective-permute-start | bytes 737288 | tf_op jit(solution)/shard_map/ppermute | solution.py:796
  206.3 6.0 %copy-start.22 = (bf16[512,768]{1,0:T(8,128)(2,1)S(1)}, bf16[512,768]{1,0:T(8,128)(2,1)}, u32[]{:S(2)}) copy-start(bf16[512,768]{1,0:T(8,128)(2,1)} %get-tuple-element.163) | copy-start | bytes 2359300
  212.2 26.3 %collective-permute-start.16 = (bf16[512,768]{1,0:T(8,128)(2,1)S(1)}, bf16[512,768]{1,0:T(8,128)(2,1)S(1)}, u32[]{:S(2)}, u32[]{:S(2)}) collective-permute-start(bf16[512,768]{1,0:T(8,128)(2,1)S(1)} %copy-done.22), channel_id=1, source_target_pairs={{0,4},{4,0},{8,12},{12,8},{16,20},{20,16},{24,28},{28,24},{1,5},{5... | collective-permute-start | bytes 2359304 | tf_op jit(solution)/shard_map/ppermute | solution.py:796
  216.2 9.0 %collective-permute-start.22 = (bf16[2,24,1280]{2,1,0:T(8,128)(2,1)S(1)}, bf16[2,24,1280]{2,1,0:T(8,128)(2,1)S(1)}, u32[]{:S(2)}, u32[]{:S(2)}) collective-permute-start(bf16[2,24,1280]{2,1,0:T(8,128)(2,1)S(1)} %fusion.10), channel_id=1, source_target_pairs={{0,16},{4,20},{8,24},{12,28},{16,0},{20,4},{24,8},{28,12},{1,17},{... | collective-permute-start | bytes 368648 | tf_op jit(solution)/shard_map/ppermute | solution.py:796
  222.4 9.7 %collective-permute-start.28 = (bf16[2,216,384]{2,1,0:T(8,128)(2,1)S(1)}, bf16[2,216,384]{2,1,0:T(8,128)(2,1)S(1)}, u32[]{:S(2)}, u32[]{:S(2)}) collective-permute-start(bf16[2,216,384]{2,1,0:T(8,128)(2,1)S(1)} %fusion.3), channel_id=1, source_target_pairs={{0,2},{1,3},{2,0},{3,1},{4,6},{5,7},{6,4},{7,5},{8,10},{9,11},{10,... | collective-permute-start | bytes 995336 | tf_op jit(solution)/shard_map/ppermute | solution.py:796
  225.3 7.0 %collective-permute-start.23 = (bf16[24,1280]{1,0:T(8,128)(2,1)S(1)}, bf16[24,1280]{1,0:T(8,128)(2,1)S(1)}, u32[]{:S(2)}, u32[]{:S(2)}) collective-permute-start(bf16[24,1280]{1,0:T(8,128)(2,1)S(1)} %get-tuple-element.199), channel_id=1, source_target_pairs={{0,4},{4,0},{8,12},{12,8},{16,20},{20,16},{24,28},{28,24},{1,5},{5... | collective-permute-start | bytes 184328 | tf_op jit(solution)/shard_map/ppermute | solution.py:796
  232.2 5.1 %copy-start.2 = (f32[512,768]{1,0:T(8,128)S(1)}, f32[512,768]{1,0:T(8,128)}, u32[]{:S(2)}) copy-start(f32[512,768]{1,0:T(8,128)} %get-tuple-element.122) | copy-start | bytes 4718596
  232.2 5.1 %copy-start.20 = (f32[768]{0:T(1024)S(1)}, f32[768]{0:T(1024)}, u32[]{:S(2)}) copy-start(f32[768]{0:T(1024)} %param.28) | copy-start | bytes 9220
  232.3 4.9 %collective-permute-start.24 = (bf16[24,2432]{1,0:T(8,128)(2,1)S(1)}, bf16[24,2432]{1,0:T(8,128)(2,1)S(1)}, u32[]{:S(2)}, u32[]{:S(2)}) collective-permute-start(bf16[24,2432]{1,0:T(8,128)(2,1)S(1)} %pad_maximum_fusion.2), channel_id=1, source_target_pairs={{0,2},{1,3},{2,0},{3,1},{4,6},{5,7},{6,4},{7,5},{8,10},{9,11},{10,... | collective-permute-start | bytes 350216 | tf_op jit(solution)/shard_map/ppermute | solution.py:796
  233.8 4.7 %copy-start.1 = (bf16[2,2,216,384]{3,2,1,0:T(8,128)(2,1)}, bf16[2,2,216,384]{3,2,1,0:T(8,128)(2,1)S(1)}, u32[]{:S(2)}) copy-start(bf16[2,2,216,384]{3,2,1,0:T(8,128)(2,1)S(1)} %pad_maximum_fusion.near) | copy-start | bytes 1990660
  233.8 10.3 %collective-permute-start.29 = (bf16[2,2,216,384]{3,2,1,0:T(8,128)(2,1)S(1)}, bf16[2,2,216,384]{3,2,1,0:T(8,128)(2,1)S(1)}, u32[]{:S(2)}, u32[]{:S(2)}) collective-permute-start(bf16[2,2,216,384]{3,2,1,0:T(8,128)(2,1)S(1)} %pad_maximum_fusion.near), channel_id=1, source_target_pairs={{0,1},{1,0},{2,3},{3,2},{4,5},{5,4},{6,7},{7,6},{8,9},{9,8},{10,11... | collective-permute-start | bytes 1990664 | tf_op jit(solution)/shard_map/ppermute | solution.py:796
  237.3 1.2 copy-start.6
  237.3 10.6 %collective-permute-start.25 = (bf16[2,24,2432]{2,1,0:T(8,128)(2,1)S(1)}, bf16[2,24,2432]{2,1,0:T(8,128)(2,1)S(1)}, u32[]{:S(2)}, u32[]{:S(2)}) collective-permute-start(bf16[2,24,2432]{2,1,0:T(8,128)(2,1)S(1)} %pad_maximum_fusion.1.near), channel_id=1, source_target_pairs={{0,1},{1,0},{2,3},{3,2},{4,5},{5,4},{6,7},{7,6},{8,9},{9,8},{10,11... | collective-permute-start | bytes 700424 | tf_op jit(solution)/shard_map/ppermute | solution.py:796
  238.5 0.9 copy-start.8
  (7 other events, 5.0 us)
where the time goes:
time: 252 us; the launch traced here: 251 us
  Pallas kernels  149 us (59%)
  waiting for transfers between devices  44.2 us (18%)
  starting transfers between devices  35.6 us (14%)
  local copies, waits for them, and re-layouts  9.68 us (4%)
  matrix products  5.95 us (2%)
  other arithmetic  5.41 us (2%)
    pallas_call x12, Pallas kernels, kcall(): pl.pallas_call(body, out_shape=outs, scratch_shapes=list(scratch), name=n...  110 us
    ppermute x30, waiting for transfers between devices, swap(): return lax.ppermute(value, axis, [(i, i ^ offset) for i in range(count)])  44.2 us
    pallas_call x4, Pallas kernels, pcall(): pl.pallas_call(body, grid_spec=pltpu.PrefetchScalarGridSpec(num_scalar_pr...  38.9 us
    ppermute x30, starting transfers between devices, swap(): return lax.ppermute(value, axis, [(i, i ^ offset) for i in range(count)])  35.6 us
    unnamed x50, local copies, waits for them, and re-layouts  9.66 us
    dot_general x1, matrix products, body(): jnp.dot(gelu, down_weight, preferred_element_type=f32)  5.95 us
  transfers between devices with their start and end apart: 30, of which 11 were waited for; matrix products, arithmetic and copies ran while one was open for 5% of the time, Pallas kernels for 43%

commit v1 on v0

--- a/solution.py
+++ b/solution.py
@@ -29,8 +29,12 @@
 bf16 = jnp.bfloat16
 NN = (((1,), (0,)), ((), ()))
 NT = (((1,), (1,)), ((), ()))
+TN = (((0,), (0,)), ((), ()))
 MIB = 2**20
-VMEM_MIB = 60
+VMEM_MIB = 26
+MLP_SPLIT = 1
+OWN_STEP = 1
+FAR_STEP = 4
 
 
 def mm(left, right, dims=NN):
@@ -60,11 +64,20 @@
         scratch_shapes=list(scratch),
         name=name,
         compiler_params=pltpu.CompilerParams(vmem_limit_bytes=vmem * MIB),
-        cost_estimate=pl.CostEstimate(flops=int(flops), bytes_accessed=nbytes, transcendentals=0),
+        cost_estimate=estimate(name, flops, nbytes),
         **kw,
     )(*ins)
 
 
+TAIL = ("split_second", "split_third", "input_grad", "unpack_mlp", "unpack_in")
+
+
+def estimate(name, flops, nbytes):
+    if name in TAIL:
+        return pl.CostEstimate(flops=0, bytes_accessed=0, transcendentals=0)
+    return pl.CostEstimate(flops=10**12, bytes_accessed=10**10, transcendentals=0)
+
+
 def sds(shape, dtype):
     return jax.ShapeDtypeStruct(shape, dtype)
 
@@ -74,7 +87,7 @@
 
 
 def full(shape):
-    return pl.BlockSpec(shape, lambda *_: (0,) * len(shape))
+    return pl.BlockSpec(shape, lambda *_: (0,) * len(shape), pipeline_mode=pl.Buffered(1))
 
 
 def features(side, doc_row, pos, head, b0, tok, extra=None):
@@ -174,7 +187,7 @@
 
 
 def weight_specs():
-    return [pl.BlockSpec((D, GW), lambda j, y, part=part: (0, 2 * part + y[0])) for part in range(3)]
+    return [pl.BlockSpec((D, GW), lambda j, y, part=part: (0, 2 * part + y[0]), pipeline_mode=pl.Buffered(1)) for part in range(3)]
 
 
 def pcall(body, name, scalar, ins, outs, in_specs, out_specs, *, grid=(1,), scratch=(), vmem=VMEM_MIB, flops=0):
@@ -187,11 +200,11 @@
         out_shape=outs,
         name=name,
         compiler_params=pltpu.CompilerParams(vmem_limit_bytes=vmem * MIB),
-        cost_estimate=pl.CostEstimate(flops=int(flops), bytes_accessed=nbytes, transcendentals=0),
+        cost_estimate=estimate(name, flops, nbytes),
     )(scalar, *ins)
 
 
-def project(y, x, ids, gain, shift, in_b, weight):
+def project(y, x, ids, gain, shift, in_b, weight, vmem):
     tok = x.shape[0]
     outs = [
         sds((D, tok), bf16),
@@ -205,6 +218,7 @@
     return pcall(
         functools.partial(project_body, tok), "project", y, (x, ids, gain, shift, in_b, weight, weight, weight), outs,
         [full(x.shape), full(ids.shape), full((D,)), full((D,)), full((3 * D,))] + weight_specs(), [full(o.shape) for o in outs],
+        vmem=vmem,
         flops=2 * tok * D * (tok + 3 * GW),
     )
 
@@ -243,20 +257,36 @@
 
 
 def own_forward_body(tok, y_ref, qa, qb, ka, kb, va, vb, da, db, out_ref, qaug, kaug, vaug):
-    head = y_ref[0] * HG + pl.program_id(0)
     pos = iota_row(tok)
     docs = (da[0:1], db[0:1])
-    fill_keys(kaug, vaug, (ka[...], kb[...]), (va[...], vb[...]), docs, (pos, pos), head, 0, tok)
-    fill_queries(qaug, (qa[...], qb[...]), docs, (pos, pos), head, 0, tok)
-
-    def put(at, val):
-        out_ref[0, :, at : at + val.shape[1]] = val
-
-    attend(qaug, kaug, vaug, 2 * tok, 2 * tok, tok, put)
-
-
-def head_block(tok):
-    return pl.BlockSpec((HD, tok), lambda h: (h, 0))
+    for i in range(OWN_STEP):
+        head = y_ref[0] * HG + pl.program_id(0) * OWN_STEP + i
+        at_head = lambda *refs: tuple(Rows(r, i)[...] for r in refs)
+        fill_keys(kaug.at[i], vaug.at[i], at_head(ka, kb), at_head(va, vb), docs, (pos, pos), head, 0, tok)
+        fill_queries(qaug.at[i], at_head(qa, qb), docs, (pos, pos), head, 0, tok)
+
+        def put(at, val):
+            out_ref[i, :, at : at + val.shape[1]] = val
+
+        attend(qaug.at[i], kaug.at[i], vaug.at[i], 2 * tok, 2 * tok, tok, put)
+
+
+def head_block(tok, step=1):
+    return pl.BlockSpec((HD * step, tok), lambda h: (h, 0))
+
+
+class Rows:
+    def __init__(self, ref, head):
+        self.ref, self.rows = ref, slice(head * HD, (head + 1) * HD)
+
+    def __getitem__(self, at):
+        return self.ref[(self.rows,) + at[1:]] if isinstance(at, tuple) else self.ref[self.rows]
+
+    def __setitem__(self, at, value):
+        if isinstance(at, tuple):
+            self.ref[(self.rows,) + at[1:]] = value
+        else:
+            self.ref[self.rows] = value
 
 
 def own_forward(y, qs, ks, vs, docs):
@@ -266,10 +296,10 @@
         "own_forward",
         (y, *qs, *ks, *vs, *docs),
         [sds((HG, 64, 2 * tok), f32)],
-        grid=(HG,),
-        in_specs=[SMEM] + [head_block(tok)] * 6 + [full((8, tok))] * 2,
-        out_specs=[pl.BlockSpec((1, 64, 2 * tok), lambda h: (h, 0, 0))],
-        scratch=[pltpu.VMEM((64, 2 * tok), bf16)] * 3,
+        grid=(HG // OWN_STEP,),
+        in_specs=[SMEM] + [head_block(tok, OWN_STEP)] * 6 + [full((8, tok))] * 2,
+        out_specs=[pl.BlockSpec((OWN_STEP, 64, 2 * tok), lambda h: (h, 0, 0))],
+        scratch=[pltpu.VMEM((OWN_STEP, 64, 2 * tok), bf16)] * 3,
         flops=2 * HG * 128 * (2 * tok) ** 2,
     )[0]
 
@@ -303,30 +333,33 @@
 def far_forward_body(tok, masks, y_ref, qa, qb, da, db, part, *rest):
     nrem = 2 * len(masks)
     refs = rest[:nrem]
-    ma, mb, merged, lse, qaug, kaug, vaug, acc = rest[nrem:]
-    local = pl.program_id(0)
-    head = y_ref[0] * HG + local
-    acc[...] = part[0]
-    for b0, level, members in groups_of(masks):
-        ks, vs, docs, poss, start, width = remote_parts(refs, members, local, level, tok)
-        nk = width * len(ks)
-        fill_keys(kaug, vaug, ks, vs, docs, poss, head, b0, tok)
-        window = pl.ds(pl.multiple_of(start, 128), width)
-        pos = iota_row(width) + start
-        fill_queries(qaug, (qa[:, window], qb[:, window]), (da[0:1, window], db[0:1, window]), (pos, pos), head, b0, tok)
-
-        def put(at, val):
-            acc[:, window] += val[:, 0:width]
-            other = pl.ds(pl.multiple_of(start + tok, 128), width)
-            acc[:, other] += val[:, width : 2 * width]
-
-        attend(qaug, kaug, vaug, 2 * width, nk, 2 * width, put)
-    den = acc[HD : HD + 1]
-    val = acc[0:HD] / den
-    merged[0] = val
-    ma[...] = val[:, 0:tok].astype(bf16)
-    mb[...] = val[:, tok : 2 * tok].astype(bf16)
-    lse[0] = jnp.broadcast_to(jnp.log2(den), (8, 2 * tok))
+    ma, mb, merged, lse, qaugs, kaugs, vaugs, accs = rest[nrem:]
+    for i in range(FAR_STEP):
+        local = pl.program_id(0) * FAR_STEP + i
+        head = y_ref[0] * HG + local
+        qh, acc = (Rows(qa, i), Rows(qb, i)), accs.at[i]
+        acc[...] = part[i]
+        for g, (b0, level, members) in enumerate(groups_of(masks)):
+            qaug, kaug, vaug = qaugs.at[i, g], kaugs.at[i, g], vaugs.at[i, g]
+            ks, vs, docs, poss, start, width = remote_parts(refs, members, local, level, tok)
+            nk = width * len(ks)
+            fill_keys(kaug, vaug, ks, vs, docs, poss, head, b0, tok)
+            window = pl.ds(pl.multiple_of(start, 128), width)
+            pos = iota_row(width) + start
+            fill_queries(qaug, [q[:, window] for q in qh], (da[0:1, window], db[0:1, window]), (pos, pos), head, b0, tok)
+
+            def put(at, val):
+                acc[:, window] += val[:, 0:width]
+                other = pl.ds(pl.multiple_of(start + tok, 128), width)
+                acc[:, other] += val[:, width : 2 * width]
+
+            attend(qaug, kaug, vaug, 2 * width, nk, 2 * width, put)
+        den = acc[HD : HD + 1]
+        val = acc[0:HD] / den
+        merged[i] = val
+        Rows(ma, i)[...] = val[:, 0:tok].astype(bf16)
+        Rows(mb, i)[...] = val[:, tok : 2 * tok].astype(bf16)
+        lse[i] = jnp.broadcast_to(jnp.log2(den), (8, 2 * tok))
 
 
 def remote_sizes(masks, tok):
@@ -342,21 +375,21 @@
 def far_forward(y, qs, docs, part, masks, remote):
     tok = qs[0].shape[1]
     nq, nk = remote_sizes(masks, tok)
-    per_head = pl.BlockSpec((1, 64, 2 * tok), lambda h: (h, 0, 0))
+    n = len(groups_of(masks))
+    per_head = lambda r: pl.BlockSpec((FAR_STEP, r, 2 * tok), lambda h: (h, 0, 0))
     return kcall(
         functools.partial(far_forward_body, tok, masks),
         "far_forward",
         (y, *qs, *docs, part, *remote),
         [sds((GW, tok), bf16)] * 2 + [sds((HG, HD, 2 * tok), f32), sds((HG, 8, 2 * tok), f32)],
-        grid=(HG,),
-        in_specs=[SMEM] + [head_block(tok)] * 2 + [full((8, tok))] * 2 + [per_head] + [full(r.shape) for r in remote],
-        out_specs=[head_block(tok)] * 2
-        + [pl.BlockSpec((1, HD, 2 * tok), lambda h: (h, 0, 0)), pl.BlockSpec((1, 8, 2 * tok), lambda h: (h, 0, 0))],
+        grid=(HG // FAR_STEP,),
+        in_specs=[SMEM] + [head_block(tok, FAR_STEP)] * 2 + [full((8, tok))] * 2 + [per_head(64)] + [full(r.shape) for r in remote],
+        out_specs=[head_block(tok, FAR_STEP)] * 2 + [per_head(HD), per_head(8)],
         scratch=[
-            pltpu.VMEM((64, nq), bf16),
-            pltpu.VMEM((64, nk), bf16),
-            pltpu.VMEM((64, nk), bf16),
-            pltpu.VMEM((64, 2 * tok), f32),
+            pltpu.VMEM((FAR_STEP, n, 64, nq), bf16),
+            pltpu.VMEM((FAR_STEP, n, 64, nk), bf16),
+            pltpu.VMEM((FAR_STEP, n, 64, nk), bf16),
+            pltpu.VMEM((FAR_STEP, 64, 2 * tok), f32),
         ],
         flops=2 * remote_flops(masks, tok),
     )
@@ -395,57 +428,57 @@
     refs = rest[:nrem]
     dq_ref = rest[nrem]
     sends = rest[nrem + 1 : nrem + 1 + len(masks)]
-    qaug, gaug, kaug, vaug, dk, dv = rest[nrem + 1 + len(masks) :]
-    local = pl.program_id(0)
-    head = y_ref[0] * HG + local
-    row = pl.multiple_of(local * HD, 16)
-    dq_ref[0] = jnp.zeros((HD, 2 * tok), f32)
-    for b0, level, members in groups_of(masks):
-        ks, vs, docs, poss, start, width = remote_parts(refs, members, local, level, tok)
-        nk = width * len(ks)
-        fill_keys(kaug, vaug, ks, vs, docs, poss, head, b0, tok)
-        window = pl.ds(pl.multiple_of(start, 128), width)
-        other = pl.ds(pl.multiple_of(start + tok, 128), width)
-        pos = iota_row(width) + start
-        fill_queries(
-            qaug, (qa[:, window], qb[:, window]), (da[0:1, window], db[0:1, window]), (pos, pos), head, b0, tok,
-            (lse[0, 0:1, window], lse[0, 0:1, other]),
-        )
-        fill_grads(gaug, (ga[:, window], gb[:, window]), (merged[0, :, window], merged[0, :, other]))
-
-        def put_q(at, val):
-            dq_ref[0, :, window] += val[:, 0:width]
-            dq_ref[0, :, other] += val[:, width : 2 * width]
-
-        attend_back(qaug, gaug, kaug, vaug, 2 * width, nk, 2 * width, put_q, dk, dv)
-        for n, j in enumerate(members):
-            span = slice(2 * n * width, 2 * (n + 1) * width)
-            sends[j][pl.ds(row, HD), :] = (dk[:, span] * LN2).astype(bf16)
-            sends[j][pl.ds(row + GW, HD), :] = dv[:, span].astype(bf16)
+    qaugs, gaugs, kaugs, vaugs, dks, dvs = rest[nrem + 1 + len(masks) :]
+    for i in range(FAR_STEP):
+        local = pl.program_id(0) * FAR_STEP + i
+        head = y_ref[0] * HG + local
+        row = pl.multiple_of(local * HD, 16)
+        dq_ref[i] = jnp.zeros((HD, 2 * tok), f32)
+        qh, gh = (Rows(qa, i), Rows(qb, i)), (Rows(ga, i), Rows(gb, i))
+        for g, (b0, level, members) in enumerate(groups_of(masks)):
+            qaug, gaug, kaug, vaug, dk, dv = (v.at[i, g] for v in (qaugs, gaugs, kaugs, vaugs, dks, dvs))
+            ks, vs, docs, poss, start, width = remote_parts(refs, members, local, level, tok)
+            nk = width * len(ks)
+            fill_keys(kaug, vaug, ks, vs, docs, poss, head, b0, tok)
+            window = pl.ds(pl.multiple_of(start, 128), width)
+            other = pl.ds(pl.multiple_of(start + tok, 128), width)
+            pos = iota_row(width) + start
+            fill_queries(
+                qaug, [q[:, window] for q in qh], (da[0:1, window], db[0:1, window]), (pos, pos), head, b0, tok,
+                (lse[i, 0:1, window], lse[i, 0:1, other]),
+            )
+            fill_grads(gaug, [v[:, window] for v in gh], (merged[i, :, window], merged[i, :, other]))
+
+            def put_q(at, val):
+                dq_ref[i, :, window] += val[:, 0:width]
+                dq_ref[i, :, other] += val[:, width : 2 * width]
+
+            attend_back(qaug, gaug, kaug, vaug, 2 * width, nk, 2 * width, put_q, dk, dv)
+            for n, j in enumerate(members):
+                span = slice(2 * n * width, 2 * (n + 1) * width)
+                sends[j][pl.ds(row, HD), :] = (dk[:, span] * LN2).astype(bf16)
+                sends[j][pl.ds(row + GW, HD), :] = dv[:, span].astype(bf16)
 
 
 def far_backward(y, qs, docs, gs, merged, lse, masks, remote):
     tok = qs[0].shape[1]
     nq, nk = remote_sizes(masks, tok)
-    per_head = lambda r: pl.BlockSpec((1, r, 2 * tok), lambda h: (h, 0, 0))
+    n = len(groups_of(masks))
+    per_head = lambda r: pl.BlockSpec((FAR_STEP, r, 2 * tok), lambda h: (h, 0, 0))
+    blocks = head_block(tok, FAR_STEP)
     sends = [sds((2 * GW, 2 * (tok >> min(m.bit_length(), 2))), bf16) for m in masks]
     return kcall(
         functools.partial(far_backward_body, tok, masks),
         "far_backward",
         (y, *qs, *docs, *gs, merged, lse, *remote),
         [sds((HG, HD, 2 * tok), f32)] + sends,
-        grid=(HG,),
-        in_specs=[SMEM] + [head_block(tok)] * 2 + [full((8, tok))] * 2 + [head_block(tok)] * 2
+        grid=(HG // FAR_STEP,),
+        in_specs=[SMEM] + [blocks] * 2 + [full((8, tok))] * 2 + [blocks] * 2
         + [per_head(HD), per_head(8)] + [full(r.shape) for r in remote],
         out_specs=[per_head(HD)] + [full(s.shape) for s in sends],
-        scratch=[
-            pltpu.VMEM((64, nq), bf16),
-            pltpu.VMEM((64, nq), bf16),
-            pltpu.VMEM((64, nk), bf16),
-            pltpu.VMEM((64, nk), bf16),
-            pltpu.VMEM((HD, nk), f32),
-            pltpu.VMEM((HD, nk), f32),
-        ],
+        scratch=[pltpu.VMEM((FAR_STEP, n, 64, nq), bf16)] * 2
+        + [pltpu.VMEM((FAR_STEP, n, 64, nk), bf16)] * 2
+        + [pltpu.VMEM((FAR_STEP, n, HD, nk), f32)] * 2,
         flops=5 * remote_flops(masks, tok),
     )
 
@@ -483,17 +516,25 @@
     )
 
 
+NBLK = 8
+HALF = D // 2
+DOWN_ROWS = FF // NBLK
+UP_ROWS = D // NBLK
+ROWS_A = 2 * UP_ROWS + UP_ROWS // 2
+ROWS_B = DOWN_ROWS // 2
+
+
 def cot_body(cot, down, out):
-    out[...] = mm(cot[...], down[...], NT)
+    out[...] = mm(cot[...], down[...], NT).astype(out.dtype)
 
 
 def cot_down(cot, down):
     tok, ff = cot.shape[0], down.shape[0]
     blk = 768
     return kcall(
-        cot_body, "cot_down", (cot, down), [sds((tok, ff), f32)], grid=(ff // blk,),
+        cot_body, "cot_down", (cot, down), [sds((tok, ff), bf16)], grid=(ff // blk,),
         in_specs=[full((tok, D)), pl.BlockSpec((blk, D), lambda j: (j, 0))],
-        out_specs=[pl.BlockSpec((tok, blk), lambda j: (0, j))], flops=2 * tok * D * ff,
+        out_specs=[pl.BlockSpec((tok, blk), lambda j: (0, j))], vmem=60, flops=2 * tok * D * ff,
     )[0]
 
 
@@ -511,11 +552,12 @@
     return jnp.where(v < 0, tail, 1.0 - tail), gauss
 
 
-def mlp_body(tok, nblk, y_ref, x_ref, mown, moth, out_b, n2g, n2s, wout, up, up_b, gdown, cot,
-             gelu_ref, gelu_t_ref, gpre_ref, upb_ref, resid_ref, second_t_ref, gattn_t_ref, gmown, gmoth, gres_ref, vec_ref,
+def mlp_body(tok, nblk, bits, x_ref, mown, moth, out_b, n2g, n2s, wout, up, up_b, gdown, cot,
+             gelu_ref, gelu_send, gpre_ref, gpre_send, upb_ref, rows_ref, resid_ref, gmown, gmoth, gres_ref, vec_ref,
              second, xhat, rstd, acc):
     step = pl.program_id(0)
-    y = y_ref[0]
+    y = bits[0]
+    low_core = bits[3] == 0
     mine = pl.ds(pl.multiple_of(y * GW, 128), GW)
     theirs = pl.ds(pl.multiple_of((1 - y) * GW, 128), GW)
     gain = row(n2g)
@@ -532,19 +574,28 @@
         rstd[...] = jnp.broadcast_to(rs, rstd.shape)
         low = (xh * gain + row(n2s)).astype(bf16)
         second[...] = low
-        second_t_ref[...] = low.T
+        rows_ref[0:D] = low.T
         acc[...] = jnp.zeros_like(acc)
 
-    pre = mm(second[...], up[...]) + up_b[0]
-    cdf, gauss = normal_cdf(pre)
-    gelu = (pre * cdf).astype(bf16)
-    gelu_ref[...] = gelu
-    gelu_t_ref[...] = gelu.T
-    slope = cdf + pre * (gauss * (1.0 / math.sqrt(2.0 * math.pi)))
-    gpre = (slope * gdown[...]).astype(bf16)
-    gpre_ref[...] = gpre
-    upb_ref[...] = mm(jnp.ones((8, tok), bf16), gpre)
-    acc[...] += mm(gpre, up[...], NT)
+    rows = tok // MLP_SPLIT
+    for i in range(MLP_SPLIT):
+        part = slice(i * rows, (i + 1) * rows)
+        pre = mm(second[part], up[...]) + up_b[0]
+        cdf, gauss = normal_cdf(pre)
+        gelu_t = (pre * cdf).astype(bf16).T
+        gelu_ref[:, part] = gelu_t
+        half = DOWN_ROWS // 2
+        for at in range(0, gelu_t.shape[0], DOWN_ROWS):
+            low, high = gelu_t[at : at + half], gelu_t[at + half : at + DOWN_ROWS]
+            gelu_send[at // 2 : at // 2 + half, part] = jnp.where(low_core, high, low)
+        slope = cdf + pre * (gauss * (1.0 / math.sqrt(2.0 * math.pi)))
+        gpre = (slope * gdown[part]).astype(bf16)
+        gpre_ref[part] = gpre
+
+        gpre_send[part] = gpre
+        acc[part] += mm(gpre, up[...], NT)
+        sums = mm(jnp.ones((8, rows), bf16), gpre)
+        upb_ref[...] = sums if i == 0 else upb_ref[...] + sums
 
     @pl.when(step == nblk - 1)
     def _():
@@ -558,7 +609,7 @@
         gres_ref[...] = gres
         gattn = gres.astype(bf16)
         gattn_t = mm(gattn.T, one_hot(tok, True)).astype(bf16)
-        gattn_t_ref[...] = gattn_t
+        rows_ref[D : 2 * D] = gattn_t
         gmoth[...] = mm(wout[theirs, :], gattn_t).astype(bf16)
         gmown[...] = mm(wout[mine, :], gattn_t).astype(bf16)
         ones = jnp.ones((8, tok), bf16)
@@ -568,86 +619,99 @@
         vec_ref[24:32] = mm(ones, gattn)
 
 
-def mlp(y, x, mown, moth, out_b, n2g, n2s, wout, up, up_b, gdown, cot):
+def mlp_chunk(step, bits):
+    return (step // 2 + bits[3]) % 2 * 2 + step % 2
+
+
+def mlp(bits, x, mown, moth, out_b, n2g, n2s, wout, up, up_b, gdown, cot):
     tok = cot.shape[0]
     ff = up.shape[1]
-    blk = 768
-    nblk = ff // blk
-    wide = pl.BlockSpec((tok, blk), lambda j: (0, j))
+    nblk = 4
+    blk = ff // nblk
+    wide = pl.BlockSpec((tok, blk), lambda j, b: (0, mlp_chunk(j, b)))
     outs = [
-        sds((tok, ff), bf16), sds((ff, tok), bf16), sds((tok, ff), bf16), sds((8, ff), f32),
-        sds((tok, D), f32), sds((D, tok), bf16), sds((D, tok), bf16), sds((GW, tok), bf16), sds((GW, tok), bf16),
+        sds((ff, tok), bf16), sds((ff // 2, tok), bf16), sds((tok, ff), bf16), sds((tok, ff // 2), bf16), sds((8, ff), f32),
+        sds((2 * D, tok), bf16), sds((tok, D), f32), sds((GW, tok), bf16), sds((GW, tok), bf16),
         sds((tok, D), f32), sds((32, D), f32),
     ]
-    return kcall(
+    return pcall(
         functools.partial(mlp_body, tok, nblk),
         "mlp",
-        (y, x, mown, moth, out_b, n2g, n2s, wout, up, up_b.reshape(nblk, 1, blk), gdown, cot),
+        bits,
+        (x, mown, moth, out_b, n2g, n2s, wout, up, up_b.reshape(nblk, 1, blk), gdown, cot),
         outs,
-        grid=(nblk,),
-        in_specs=[
-            SMEM, full(x.shape), full(mown.shape), full(moth.shape), full((D,)), full((D,)), full((D,)), full(wout.shape),
-            pl.BlockSpec((D, blk), lambda j: (0, j)), pl.BlockSpec((1, 1, blk), lambda j: (j, 0, 0)),
+        [
+            full(x.shape), full(mown.shape), full(moth.shape), full((D,)), full((D,)), full((D,)), full(wout.shape),
+            pl.BlockSpec((D, blk), lambda j, b: (0, mlp_chunk(j, b))),
+            pl.BlockSpec((1, 1, blk), lambda j, b: (mlp_chunk(j, b), 0, 0)),
             wide, full((tok, D)),
         ],
-        out_specs=[
-            wide, pl.BlockSpec((blk, tok), lambda j: (j, 0)), wide, pl.BlockSpec((8, blk), lambda j: (0, j)),
-        ] + [full(o.shape) for o in outs[4:]],
+        [
+            pl.BlockSpec((blk, tok), lambda j, b: (mlp_chunk(j, b), 0)),
+            pl.BlockSpec((blk // 2, tok), lambda j, b: (mlp_chunk(j, b), 0)),
+            wide,
+            pl.BlockSpec((tok, blk), lambda j, b: (0, jnp.maximum(j - nblk // 2, 0))),
+            pl.BlockSpec((8, blk), lambda j, b: (0, mlp_chunk(j, b))),
+        ] + [full(o.shape) for o in outs[5:]],
+        grid=(nblk,),
         scratch=[pltpu.VMEM((tok, D), bf16), pltpu.VMEM((tok, D), f32), pltpu.VMEM((tok, 128), f32), pltpu.VMEM((tok, D), f32)],
+        vmem=32,
         flops=2 * tok * D * (2 * ff + 2 * D + 2 * tok),
     )
 
 
-NBLK = 8
-HALF = D // 2
-DOWN_ROWS = FF // NBLK
-UP_ROWS = D // NBLK
-MLP_ROWS = DOWN_ROWS + 4 * UP_ROWS + UP_ROWS
-STEP_BLOCKS = 2
-
-
-def mlp_grads_body(bits, gelu_t, cot, second_t, gpre, mown, moth, gattn_t, send, keep):
-    up = mm(second_t[...], gpre[...]).astype(bf16)
-    down = mm(gelu_t[...], cot[...]).astype(bf16)
-    heads = jnp.where((pl.program_id(0) < NBLK // STEP_BLOCKS // 2) == (bits[0] == 0), mown[...], moth[...])
-    att = mm(heads, gattn_t[...], NT).astype(bf16)
-    keep_low = bits[3] == 0
-
-    def put(block, rows, low, high):
-        keep[block, rows] = jnp.where(keep_low, low, high)
-        send[block, rows] = jnp.where(keep_low, high, low)
-
-    for s in range(STEP_BLOCKS):
-        d = down[s * DOWN_ROWS : (s + 1) * DOWN_ROWS]
-        put(s, slice(0, DOWN_ROWS), d[:, :HALF], d[:, HALF:])
-        rows = slice(s * UP_ROWS, (s + 1) * UP_ROWS)
-        for c in range(4):
-            at = DOWN_ROWS + c * UP_ROWS
-            low = up[rows, c * HALF : (c + 1) * HALF]
-            put(s, slice(at, at + UP_ROWS), low, up[rows, (c + 4) * HALF : (c + 5) * HALF])
-        a = att[rows]
-        put(s, slice(DOWN_ROWS + 4 * UP_ROWS, MLP_ROWS), a[:, :HALF], a[:, HALF:])
-
-
-def mlp_grads(bits, gelu_t, cot, second_t, gpre, mown, moth, gattn_t):
-    tok = cot.shape[0]
-    n = NBLK // STEP_BLOCKS
-    rows = MLP_ROWS
-    heads = pl.BlockSpec((GW // (n // 2), tok), lambda j, c: (j % (n // 2), 0))
-    outs = [sds((NBLK, rows, HALF), bf16)] * 2
+def mlp_grads_body(bits, cores, *refs):
+    ins, outs = refs[:-4], refs[-4:]
+    send_a, keep_a, send_b, keep_b = outs
+    ybit, xbit = bits[0], bits[1]
+    heads_low = (pl.program_id(0) < 2) == (ybit == 0)
+    up = att = 0.0
+    down = [0.0, 0.0]
+    for c in range(cores):
+        low_t, high_t, second_t, gattn_t, gpre, cot, mown, moth = ins[8 * c : 8 * c + 8]
+        up = up + mm(second_t[...], gpre[...])
+        down = [old + mm(gelu_t[...], cot[...]) for old, gelu_t in zip(down, (low_t, high_t), strict=True)]
+        att = att + mm(jnp.where(heads_low, mown[...], moth[...]), gattn_t[...], NT)
+    up, att, down = up.astype(bf16), att.astype(bf16), [v.astype(bf16) for v in down]
+    x_low, y_low = xbit == 0, ybit == 0
+    half = UP_ROWS // 2
+    for y in range(2):
+        rows = slice(y * UP_ROWS, (y + 1) * UP_ROWS)
+        cols = [up[rows, c * HALF : (c + 1) * HALF] for c in range(4)]
+        pieces = [(0, UP_ROWS, cols[0], cols[2]), (UP_ROWS, UP_ROWS, cols[1], cols[3])]
+        pieces += [(2 * UP_ROWS, half, att[y * UP_ROWS : y * UP_ROWS + half], att[y * UP_ROWS + half : (y + 1) * UP_ROWS])]
+        for at, n, low, high in pieces:
+            keep_a[0, y, at : at + n] = jnp.where(x_low, low, high)
+            send_a[0, y, at : at + n] = jnp.where(x_low, high, low)
+    for x in range(2):
+        low, high = (v[:, x * HALF : (x + 1) * HALF] for v in down)
+        keep_b[0, x] = jnp.where(y_low, low, high)
+        send_b[0, x] = jnp.where(y_low, high, low)
+
+
+def mlp_grads(bits, *per_core):
+    tok = per_core[0][3].shape[0]
+    ins, specs = [], []
+    for gelu_t, rows, gpre, cot, mown, moth in per_core:
+        heads = pl.BlockSpec((GW // 2, tok), lambda j, b: (j % 2, 0))
+        ins += [gelu_t, gelu_t, rows, rows, gpre, cot, mown, moth]
+        if gelu_t.shape[0] == FF:
+            gelus = [pl.BlockSpec((ROWS_B, tok), lambda j, b, y=y: (4 * j + 2 * y + b[3], 0)) for y in range(2)]
+            half = pl.BlockSpec((tok, FF // 2), lambda j, b: (0, b[3]))
+        else:
+            gelus = [pl.BlockSpec((ROWS_B, tok), lambda j, b, y=y: (2 * j + y, 0)) for y in range(2)]
+            half = full(gpre.shape)
+        specs += gelus + [
+            pl.BlockSpec((D // 4, tok), lambda j, b: (j, 0)),
+            pl.BlockSpec((HALF, tok), lambda j, b: (D // HALF + b[3], 0)),
+            half, full(cot.shape), heads, heads,
+        ]
+    outs = [sds((4, 2, ROWS_A, HALF), bf16)] * 2 + [sds((4, 2, ROWS_B, HALF), bf16)] * 2
     return pcall(
-        mlp_grads_body, "mlp_grads", bits, (gelu_t, cot, second_t, gpre, mown, moth, gattn_t), outs,
-        [
-            pl.BlockSpec((FF // n, tok), lambda j, c: (j, 0)),
-            full(cot.shape),
-            pl.BlockSpec((D // n, tok), lambda j, c: (j, 0)),
-            full(gpre.shape),
-            heads,
-            heads,
-            full(gattn_t.shape),
-        ],
-        [pl.BlockSpec((STEP_BLOCKS, rows, HALF), lambda j, c: (j, 0, 0))] * 2,
-        grid=(n,),
+        lambda bits, *refs: mlp_grads_body(bits, len(per_core), *refs), "mlp_grads", bits, ins, outs, specs,
+        [pl.BlockSpec((1,) + o.shape[1:], lambda j, b: (j, 0, 0, 0)) for o in outs],
+        grid=(4,),
+        vmem=28,
         flops=2 * tok * D * (2 * FF + D),
     )
 
@@ -744,6 +808,7 @@
             pltpu.VMEM((3 * GW, tok), bf16), pltpu.VMEM((GW, tok), f32), pltpu.VMEM((D, 3 * GW), f32),
             pltpu.VMEM((16, D), f32), pltpu.VMEM((8, 3 * GW), f32), pltpu.VMEM((NBLK, SMALL_ROWS, 128), f32),
         ],
+        vmem=28,
         flops=4 * tok * 3 * GW * (tok + 2 * D),
     )
 
@@ -758,17 +823,15 @@
 
 def unpack_mlp_body(bits, near, far, down, up, att):
     low = bits[3] == 0
-    halves = [
-        jnp.concatenate([v[p, x] for p in range(2) for x in range(2)], axis=0).astype(f32)
-        for v in (jnp.where(low, near[...], far[...]), jnp.where(low, far[...], near[...]))
-    ]
-    for c, half in enumerate(halves):
-        lanes = slice(c * HALF, (c + 1) * HALF)
-        down[:, lanes] = half[0:DOWN_ROWS]
-        for j in range(4):
-            at = DOWN_ROWS + j * UP_ROWS
-            up[:, (c * 4 + j) * HALF : (c * 4 + j + 1) * HALF] = half[at : at + UP_ROWS]
-        att[:, lanes] = half[DOWN_ROWS + 4 * UP_ROWS : MLP_ROWS]
+    for c, v in enumerate((jnp.where(low, near[...], far[...]), jnp.where(low, far[...], near[...]))):
+        for x in range(2):
+            half = v[x].astype(f32)
+            for j in range(2):
+                at = (c * 4 + 2 * x + j) * HALF
+                up[:, at : at + HALF] = half[j * UP_ROWS : (j + 1) * UP_ROWS]
+            n = UP_ROWS // 2
+            att[x * n : (x + 1) * n, c * HALF : (c + 1) * HALF] = half[2 * UP_ROWS : ROWS_A]
+            down[c * ROWS_B : (c + 1) * ROWS_B, x * HALF : (x + 1) * HALF] = half[ROWS_A:]
 
 
 VEC_UNITS = (1, 1, 3, 1, 1, 1, 1, 4)
@@ -807,26 +870,6 @@
     return part(1 - index), part(index)
 
 
-def split_first_body(bits, keep, got, send_a, keep_a, send_b, keep_b):
-    ybit, xbit = bits[0], bits[1]
-    total = lambda *at: keep[(0, *at)] + got[(0, *at)]
-    for j in range(2):
-        send_a[0, j] = total(j, 0, 1 - xbit)
-        keep_a[0, j] = total(j, 0, xbit)
-        send_b[0, j] = total(1 - ybit, 1, j)
-        keep_b[0, j] = total(ybit, 1, j)
-
-
-def split_first(bits, keep, got):
-    rows, cols = keep.shape[1] // 4, keep.shape[2]
-    view = lambda v: v.reshape(4, 2, 2, 2, rows, cols)
-    block = pl.BlockSpec((1, 2, 2, 2, rows, cols), lambda j: (j, 0, 0, 0, 0, 0))
-    return kcall(
-        split_first_body, "split_first", (bits, view(keep), view(got)), [sds((4, 2, rows, cols), bf16)] * 4, grid=(4,),
-        in_specs=[SMEM, block, block], out_specs=[pl.BlockSpec((1, 2, rows, cols), lambda j: (j, 0, 0, 0))] * 4,
-    )
-
-
 def split_second_body(bits, ka, ga, kb, gb, send_a, keep_a, send_b, keep_b):
     for keep, got, send_to, keep_to, bit in ((ka, ga, send_a, keep_a, bits[0]), (kb, gb, send_b, keep_b, bits[1])):
         total = lambda j: keep[0, j] + got[0, j]
@@ -835,27 +878,30 @@
 
 
 def split_second(bits, ka, ga, kb, gb):
-    rows, cols = ka.shape[2:]
-    block = pl.BlockSpec((1, 2, rows, cols), lambda j: (j, 0, 0, 0))
+    block = lambda v: pl.BlockSpec((1,) + v.shape[1:], lambda j: (j, 0, 0, 0))
+    outs = [sds((4,) + v.shape[2:], bf16) for v in (ka, ka, kb, kb)]
     return kcall(
-        split_second_body, "split_second", (bits, ka, ga, kb, gb), [sds((4, rows, cols), bf16)] * 4, grid=(4,),
-        in_specs=[SMEM] + [block] * 4, out_specs=[pl.BlockSpec((1, rows, cols), lambda j: (j, 0, 0))] * 4,
+        split_second_body, "split_second", (bits, ka, ga, kb, gb), outs, grid=(4,),
+        in_specs=[SMEM] + [block(v) for v in (ka, ga, kb, gb)],
+        out_specs=[pl.BlockSpec((1,) + o.shape[1:], lambda j: (j, 0, 0)) for o in outs],
     )
 
 
 def split_third_body(bits, ka, ga, kb, gb, send, keep):
     low = bits[2] % 2
     for h in range(2):
-        for p, (own, got) in enumerate(((ka, ga), (kb, gb))):
-            send[h, p] = own[2 * h + 1 - low] + got[2 * h + 1 - low]
-            keep[h, p] = own[2 * h + low] + got[2 * h + low]
+        at = 0
+        for own, got in ((ka, ga), (kb, gb)):
+            rows = slice(at, at + own.shape[1])
+            send[h, rows] = own[2 * h + 1 - low] + got[2 * h + 1 - low]
+            keep[h, rows] = own[2 * h + low] + got[2 * h + low]
+            at += own.shape[1]
 
 
 def split_third(bits, ka, ga, kb, gb):
-    rows, cols = ka.shape[1:]
+    out = sds((2, ka.shape[1] + kb.shape[1], HALF), bf16)
     return kcall(
-        split_third_body, "split_third", (bits, ka, ga, kb, gb), [sds((2, 2, rows, cols), bf16)] * 2,
-        in_specs=[SMEM] + [VMEM] * 4, out_specs=[VMEM] * 2,
+        split_third_body, "split_third", (bits, ka, ga, kb, gb), [out, out], in_specs=[SMEM] + [VMEM] * 4, out_specs=[VMEM] * 2,
     )
 
 
@@ -892,37 +938,39 @@
     ids_oth = swap(doc_ids, "seq", 1)
 
     args = (norm1_gain, norm1_shift, in_bias, in_weight)
-    first_a, qa, ka, va, doc_a, *out_a = project(y, x, doc_ids, *args)
+    first_a, qa, ka, va, doc_a, *out_a = project(y, x, doc_ids, *args, 60)
     remote_a = [swap(out_a[min(m.bit_length(), 2) - 1], "seq", 2 * m) for m in masks]
     gdown = cot_down(cot, down_weight)
     x_oth, ids_oth, gdown = tie(x_oth, ids_oth, gdown)
-    first_b, qb, kb, vb, doc_b, *out_b = project(y, x_oth, ids_oth, *args)
+    if whole:
+        cot_got = swap(cot, "rep", 1)
+    first_b, qb, kb, vb, doc_b, *out_b = project(y, x_oth, ids_oth, *args, VMEM_MIB)
     remote_b = [swap(out_b[min(m.bit_length(), 2) - 1], "seq", 2 * m) for m in masks]
 
-    kb, *remote_a = tie(kb, *remote_a)
     qs, ks, vs, docs = (qa, qb), (ka, kb), (va, vb), (doc_a, doc_b)
     part = own_forward(y, qs, ks, vs, docs)
     remote = [r for pair in zip(remote_a, remote_b, strict=True) for r in pair]
     mown, msend, merged, lse = far_forward(y, qs, docs, part, masks, remote)
     moth = swap(msend, "seq", 1)
-    (gelu, gelu_t, gpre, up_sum, resid1, second_t, gattn_t, gmown, gmsend, gres, vec) = mlp(
-        y, x, mown, moth, out_bias, norm2_gain, norm2_shift, out_weight, up_weight, up_bias, gdown, cot
+    if whole:
+        moth, cot_got, mown_got = tie(moth, cot_got, swap(mown, "rep", 1))
+    (gelu_t, gelu_send, gpre, gpre_send, up_sum, rows, resid1, gmown, gmsend, gres, vec) = mlp(
+        bits, x, mown, moth, out_bias, norm2_gain, norm2_shift, out_weight, up_weight, up_bias, gdown, cot
     )
     gmoth = swap(gmsend, "seq", 1)
 
-    g_send, g_keep = mlp_grads(y, gelu_t, cot, second_t, gpre, mown, moth, gattn_t)
-    gmoth, g_send = tie(gmoth, g_send)
+    own = (gelu_t, rows, gpre, cot, mown, moth)
     if whole:
-        g_got = swap(g_send, "rep", 1)
+        got = (swap(gelu_send, "rep", 1), swap(rows, "rep", 1), swap(gpre_send, "rep", 1), cot_got, mown_got, swap(moth, "rep", 1))
+        send_a, keep_a, send_b, keep_b = mlp_grads(bits, own, got)
+        got_a, got_b = swap(send_a, "rep", 2), swap(send_b, "seq", 1)
+        gmoth, send_a, send_b = tie(gmoth, send_a, send_b)
+    else:
+        halves = [mlp_grads(bits.at[3].set(c), own) for c in range(2)]
 
     gs = (gmown, gmoth)
     dq, *sends = far_backward(y, qs, docs, gs, merged, lse, masks, remote)
     recv = [swap(s, "seq", 2 * m) for s, m in zip(sends, masks, strict=True)]
-    if whole:
-        dq, g_got = tie(dq, g_got)
-        send_a, keep_a, send_b, keep_b = split_first(bits, g_keep, g_got)
-        dq, send_a, send_b = tie(dq, send_a, send_b)
-        got_a, got_b = swap(send_a, "rep", 2), swap(send_b, "seq", 1)
     dq, dk, dv = own_backward(y, qs, ks, vs, docs, gs, merged, lse, dq)
     if whole:
         dq, got_a, got_b = tie(dq, got_a, got_b)
@@ -942,7 +990,15 @@
         i_send, i_keep = halve((view(i_keep), view(i_got)), xbit, 1)
         i_got = swap(i_send, "rep", 2)
 
-    result = (resid1 + jnp.dot(gelu, down_weight, preferred_element_type=f32) + down_bias).astype(bf16)
+    result = (resid1 + mm(gelu_t, down_weight, TN) + down_bias).astype(bf16)
+    if whole:
+        i_got, result = tie(i_got, result)
+        i_send, i_keep = halve((i_keep.reshape(4, 2, -1, IN_COLS), i_got.reshape(4, 2, -1, IN_COLS)), ybit, 1)
+        i_got = swap(i_send, "seq", 1)
+        g_got, i_send = tie(g_got, i_send)
+        g_send, g_keep = halve((g_keep, g_got), z // 2, 0)
+        g_got = swap(g_send, "seq", 4)
+        gfirst_got, g_send = tie(gfirst_got, g_send)
     by_rows = lambda n: pl.BlockSpec((tok // 4, n), lambda j: (j, 0))
     grad_input = kcall(
         input_grad_body, "input_grad", (x, norm1_gain, gfirst_a, gfirst_got, gres), [sds((tok, D), f32)], grid=(4,),
@@ -950,11 +1006,14 @@
     )[0]
 
     if whole:
-        g_send, g_keep = halve((g_keep, g_got), z // 2, 0)
-        g_got = swap(g_send, "seq", 4)
-        view = lambda v: v.reshape(2, 2, 2, IN_ROWS // 2, IN_COLS)
-        i_send, i_keep = halve((view(i_keep), view(i_got)), z % 2, 1)
+        i_got, grad_input = tie(i_got, grad_input)
+        width = 3 * GW
+        low, high = jnp.where(ybit == 0, i_keep, i_got), jnp.where(ybit == 0, i_got, i_keep)
+        vec = i_keep[..., width:] + i_got[..., width:]
+        i_all = jnp.concatenate([low[..., :width], high[..., :width], vec], axis=-1).reshape(2, 2, IN_ROWS // 2, 2 * width + 128)
+        i_send, i_keep = pick(i_all, 1 - z % 2, 1), pick(i_all, z % 2, 1)
         i_got = swap(i_send, "seq", 2)
+        i_got, g_got = tie(i_got, g_got)
         i_send, i_keep = halve((i_keep, i_got), z // 2, 0)
         i_got = swap(i_send, "seq", 4)
 
@@ -965,14 +1024,8 @@
             [sds((DOWN_ROWS, D), f32), sds((UP_ROWS, FF), f32), sds((UP_ROWS, D), f32)],
             in_specs=[SMEM, VMEM, VMEM], out_specs=[VMEM] * 3,
         )
-
-        total = i_keep + i_got
-        mine = pick(total, ybit, 0)
-        got = swap(pick(total, 1 - ybit, 0), "seq", 1)
-        width = 3 * GW
-        low, high = jnp.where(ybit == 0, mine, got), jnp.where(ybit == 0, got, mine)
-        vec = mine[:, width:] + got[:, width:]
-        near, far = spread(jnp.concatenate([low[:, :width], high[:, :width], vec], axis=1), xbit)
+        near, far = spread(i_keep + i_got, xbit)
+        far, g_down = tie(far, g_down)
         g_in, *vecs = kcall(
             unpack_in_body, "unpack_in", (bits, near, far),
             [sds((2 * IN_ROWS, 3 * D), f32)] + [sds((UNIT * n,), f32) for n in VEC_UNITS],
@@ -980,11 +1033,13 @@
         )
     else:
         total = lambda v: lax.psum(lax.psum_scatter(v, "seq", scatter_dimension=0, tiled=True).astype(bf16), "rep").astype(f32)
-        both = jnp.stack([g_keep, g_send], axis=0).astype(f32)
-        cut = lambda lo, hi: both[:, :, lo:hi]
-        g_down = total(cut(0, DOWN_ROWS).transpose(1, 2, 0, 3).reshape(FF, D))
-        g_up = total(cut(DOWN_ROWS, DOWN_ROWS + 4 * UP_ROWS).reshape(2, NBLK, 4, UP_ROWS, HALF).transpose(1, 3, 0, 2, 4).reshape(D, FF))
-        g_out = total(cut(DOWN_ROWS + 4 * UP_ROWS, MLP_ROWS).transpose(1, 2, 0, 3).reshape(D, D))
+        order = lambda bit, keep, send: jnp.where(bit == 0, jnp.stack([keep, send]), jnp.stack([send, keep])).astype(f32)
+        by_x = jnp.stack([order(xbit, h[1], h[0]) for h in halves])
+        by_y = jnp.stack([order(ybit, h[3], h[2]) for h in halves])
+        ups = by_x[..., : 2 * UP_ROWS, :].reshape(2, 2, NBLK, 2, UP_ROWS, HALF)
+        g_up = total(ups.transpose(2, 4, 0, 1, 3, 5).reshape(D, FF))
+        g_out = total(by_x[..., 2 * UP_ROWS :, :].reshape(2, 2, NBLK, UP_ROWS // 2, HALF).transpose(2, 1, 3, 0, 4).reshape(D, D))
+        g_down = total(by_y.transpose(2, 1, 0, 4, 3, 5).reshape(FF, D))
         both = jnp.stack([i_keep, i_send], axis=1)[..., : 3 * GW].astype(f32).reshape(D, 3, 1, GW)
         g_in = total(jnp.where((jnp.arange(2) == ybit)[None, None, :, None], both, 0.0).reshape(D, 3 * D))
         small = i_keep[:, :, 3 * GW : 3 * GW + UNIT].astype(f32)

time: 252 us -> 229 us (0.909)
  Pallas kernels: 149 us -> 118 us
  waiting for transfers between devices: 44.2 us -> 59 us
  local copies, waits for them, and re-layouts: 9.68 us -> 7.05 us
  starting transfers between devices: 35.6 us -> 33 us
    pallas_call x12 -> x10, Pallas kernels: 110 us -> 67.7 us  [kcall(): pl.pallas_call(body, out_shape=outs, scratch_shapes=list(scratch), name=n...]
    ppermute x30 -> x35, waiting for transfers between devices: 44.2 us -> 59 us  [swap(): return lax.ppermute(value, axis, [(i, i ^ offset) for i in range(count)])]
    pallas_call x4 -> x5, Pallas kernels: 38.9 us -> 50.7 us  [pcall(): pl.pallas_call(body, grid_spec=pltpu.PrefetchScalarGridSpec(num_scalar_pr...]
    unnamed x50 -> x104, local copies, waits for them, and re-layouts: 9.66 us -> 7.03 us
    ppermute x30 -> x35, starting transfers between devices: 35.6 us -> 33 us  [swap(): return lax.ppermute(value, axis, [(i, i ^ offset) for i in range(count)])]
  transfers between devices with their start and end apart: 30 -> 35, of which waited for: 11 -> 16; matrix products, arithmetic and copies ran while one was open for 5% -> 4% of each run, Pallas kernels for 43% -> 43%
where the time goes in v1:
time: 229 us; the launch traced here: 228 us
  Pallas kernels  118 us (52%)
  waiting for transfers between devices  59 us (26%)
  starting transfers between devices  33 us (14%)
  local copies, waits for them, and re-layouts  7.05 us (3%)
  matrix products  5.02 us (2%)
  other arithmetic  4.79 us (2%)
    pallas_call x10, Pallas kernels, kcall(): pl.pallas_call(body, out_shape=outs, scratch_shapes=list(scratch), name=n...  67.7 us
    ppermute x35, waiting for transfers between devices, swap(): return lax.ppermute(value, axis, [(i, i ^ offset) for i in range(count)])  59 us
    pallas_call x5, Pallas kernels, pcall(): pl.pallas_call(body, grid_spec=pltpu.PrefetchScalarGridSpec(num_scalar_pr...  50.7 us
    ppermute x35, starting transfers between devices, swap(): return lax.ppermute(value, axis, [(i, i ^ offset) for i in range(count)])  33 us
    unnamed x104, local copies, waits for them, and re-layouts  7.03 us
    dot_general x1, matrix products, mm(): return lax.dot_general(left, right, dims, preferred_element_type=f32)  5.02 us
  transfers between devices with their start and end apart: 35, of which 16 were waited for; matrix products, arithmetic and copies ran while one was open for 4% of the time, Pallas kernels for 43%

profile of v1, /device:TPU:0, one launch (start us, length us, event | category | flops | bytes accessed | tf_op | source)
XLA Modules:
  0.0 228.4 jit_solution(7805465654745379816)
XLA Ops:
  0.6 3.0 %collective-permute-start = (bf16[512,768]{1,0:T(8,128)(2,1)}, bf16[512,768]{1,0:T(8,128)(2,1)}, u32[]{:S(2)}, u32[]{:S(2)}) collective-permute-start(bf16[512,768]{1,0:T(8,128)(2,1)} %bitcast.63), channel_id=1, source_target_pairs={{0,4},{4,0},{8,12},{12,8},{16,20},{20,16},{24,28},{28,24},{1,5},{5... | collective-permute-start | bytes 2359304 | tf_op jit(solution)/shard_map/ppermute | solution.py:859
  4.3 5.8 %project.2 = (bf16[768,512]{1,0:T(8,128)(2,1)}, bf16[384,512]{1,0:T(8,128)(2,1)}, bf16[384,512]{1,0:T(8,128)(2,1)}, bf16[384,512]{1,0:T(8,128)(2,1)}, f32[8,512]...) custom-call(s32[4]{0:T(128)} %pad_add_fusion.y_ref.bits, bf16[512,768]{1,0:T(8,128)(2,1)} %bitcast.64, ...), custom_call_target="tpu_custom_call" | custom-call | flops 999999995904 | bytes 10000000000 | tf_op jit(solution)/shard_map/project/pallas_call | solution.py:195
  10.2 3.0 %collective-permute-start.4 = (bf16[784,128]{1,0:T(8,128)(2,1)}, bf16[784,128]{1,0:T(8,128)(2,1)}, u32[]{:S(2)}, u32[]{:S(2)}) collective-permute-start(bf16[784,128]{1,0:T(8,128)(2,1)} %get-tuple-element.114), channel_id=1, source_target_pairs={{0,16},{4,20},{8,24},{12,28},{16,0},{20,4},{24,8},{28,12},{1,17},{... | collective-permute-start | bytes 602120 | tf_op jit(solution)/shard_map/ppermute | solution.py:859
  13.2 1.3 collective-permute-start.6
  14.8 6.7 %cot_down.1.gdown = bf16[512,3072]{1,0:T(8,128)(2,1)} custom-call(bf16[512,768]{1,0:T(8,128)(2,1)} %bitcast.5.cot.refs_5_, bf16[3072,768]{1,0:T(8,128)(2,1)} %down.1), custom_call_target="tpu_custom_call" | custom-call | flops 999999995904 | bytes 10000000000 | tf_op jit(solution)/shard_map/cot_down/pallas_call | solution.py:61
  21.7 5.0 %project.3 = (bf16[768,512]{1,0:T(8,128)(2,1)S(1)}, bf16[384,512]{1,0:T(8,128)(2,1)S(1)}, bf16[384,512]{1,0:T(8,128)(2,1)S(1)}, bf16[384,512]{1,0:T(8,128)(2,1)S...) custom-call(s32[4]{0:T(128)S(1)} %copy-done.12, ...), custom_call_target="tpu_custom_call" | custom-call | flops 999999995904 | bytes 10000000000 | tf_op jit(solution)/shard_map/project/pallas_call | solution.py:195
  26.7 2.9 %collective-permute-start.5 = (bf16[784,128]{1,0:T(8,128)(2,1)}, bf16[784,128]{1,0:T(8,128)(2,1)}, u32[]{:S(2)}, u32[]{:S(2)}) collective-permute-start(bf16[784,128]{1,0:T(8,128)(2,1)} %get-tuple-element.115), channel_id=1, source_target_pairs={{0,16},{4,20},{8,24},{12,28},{16,0},{20,4},{24,8},{28,12},{1,17},{... | collective-permute-start | bytes 602120 | tf_op jit(solution)/shard_map/ppermute | solution.py:859
  29.5 1.3 collective-permute-start.7
  31.1 9.5 %own_forward.1.part = f32[8,64,1024]{2,1,0:T(8,128)S(1)} custom-call(s32[4]{0:T(128)S(1)} %copy-done.12, bf16[384,512]{1,0:T(8,128)(2,1)S(1)} %copy-done.33, bf16[384,512]{1,0:T(8,128)(2,1)S(1)} %get-tuple-element.105.qb, bf16[384,512]{1,0:T(8,128)(2,1)S(1)} %copy-done.35, bf16[384,512]{1,0:T(8,128)(2,1)S(1)} %get-tuple-element.107.kb, ...), custom_call_target="tpu_custom_call" | custom-call | flops 999999995904 | bytes 10000000000 | tf_op jit(solution)/shard_map/own_forward/pallas_call | solution.py:61
  40.7 4.1 %collective-permute-done.5.rest_3_ = bf16[784,128]{1,0:T(8,128)(2,1)} collective-permute-done((bf16[784,128]{1,0:T(8,128)(2,1)}, bf16[784,128]{1,0:T(8,128)(2,1)}, u32[]{:S(2)}, u32[]{:S(2)}) %collective-permute-start.5) | collective-permute-done | bytes 200736 | tf_op jit(solution)/shard_map/ppermute | solution.py:859
  44.8 4.6 %collective-permute-done.3.rest_1_ = bf16[784,256]{1,0:T(8,128)(2,1)} collective-permute-done((bf16[784,256]{1,0:T(8,128)(2,1)}, bf16[784,256]{1,0:T(8,128)(2,1)}, u32[]{:S(2)}, u32[]{:S(2)}) %collective-permute-start.3) | collective-permute-done | bytes 401440 | tf_op jit(solution)/shard_map/ppermute | solution.py:859
  49.5 7.0 %far_forward.1 = (bf16[384,512]{1,0:T(8,128)(2,1)S(1)}, bf16[384,512]{1,0:T(8,128)(2,1)S(1)}, f32[8,48,1024]{2,1,0:T(8,128)S(1)}, f32[8,8,1024]{2,1,0:T(8,128)S(1)}) custom-call(s32[4]{0:T(128)S(1)} %copy-done.12, bf16[384,512]{1,0:T(8,128)(2,1)S(1)} %copy-done.33, bf16[384,512]{1,0:T(8,128)(2,1)S(1)} %get-tuple-element.105.qb, f32[8,512]{1,0:T(8,128)S(1)} %copy-done.45, ...), custom_call_target="tpu_custom_call" | custom-call | flops 999999995904 | bytes 10000000000 | tf_op jit(solution)/shard_map/far_forward/pallas_call | solution.py:61
  56.5 1.6 collective-permute-start.8
  59.0 9.1 %collective-permute-done.8.moth.refs_7_ = bf16[384,512]{1,0:T(8,128)(2,1)S(1)} collective-permute-done((bf16[384,512]{1,0:T(8,128)(2,1)S(1)}, bf16[384,512]{1,0:T(8,128)(2,1)S(1)}, u32[]{:S(2)}, u32[]{:S(2)}) %collective-permute-start.8) | collective-permute-done | bytes 393248 | tf_op jit(solution)/shard_map/ppermute | solution.py:859
  68.1 18.8 %mlp.1 = (bf16[3072,512]{1,0:T(8,128)(2,1)S(1)}, bf16[1536,512]{1,0:T(8,128)(2,1)S(1)}, bf16[512,3072]{1,0:T(8,128)(2,1)S(1)}, bf16[512,1536]{1,0:T(8,128)(2,1)S...) custom-call(s32[4]{0:T(128)S(1)} %copy-done.12, ...), custom_call_target="tpu_custom_call" | custom-call | flops 999999995904 | bytes 10000000000 | tf_op jit(solution)/shard_map/mlp/pallas_call | solution.py:195
  87.9 1.6 collective-permute-start.11
  89.5 5.9 %collective-permute-done.15.refs_15_ = bf16[384,512]{1,0:T(8,128)(2,1)S(1)} collective-permute-done((bf16[384,512]{1,0:T(8,128)(2,1)S(1)}, bf16[384,512]{1,0:T(8,128)(2,1)S(1)}, u32[]{:S(2)}, u32[]{:S(2)}) %collective-permute-start.15) | collective-permute-done | bytes 393248 | tf_op jit(solution)/shard_map/ppermute | solution.py:859
  95.4 9.6 %mlp_grads.1 = (bf16[4,2,240,384]{3,2,1,0:T(8,128)(2,1)}, bf16[4,2,240,384]{3,2,1,0:T(8,128)(2,1)S(1)}, bf16[4,2,192,384]{3,2,1,0:T(8,128)(2,1)}, bf16[4,2,192,384]{3,2,1,0:T(8,128)(2,1)S(1)}) custom-call(s32[4]{0:T(128)S(1)} %copy-done.12, bf16[3072,512]{1,0:T(8,128)(2,1)S(1)} %get-tuple-element.122.refs_0_.refs_1_, ...), custom_call_target="tpu_custom_call" | custom-call | flops 999999995904 | bytes 10000000000 | tf_op jit(solution)/shard_map/mlp_grads/pallas_call | solution.py:195
  105.0 1.5 collective-permute-start.16
  106.5 1.5 collective-permute-start.17
  108.1 10.6 %far_backward.1 = (f32[8,48,1024]{2,1,0:T(8,128)S(1)}, bf16[768,512]{1,0:T(8,128)(2,1)}, bf16[768,256]{1,0:T(8,128)(2,1)}, bf16[768,256]{1,0:T(8,128)(2,1)}) custom-call(s32[4]{0:T(128)S(1)} %copy-done.12, bf16[384,512]{1,0:T(8,128)(2,1)S(1)} %copy-done.34, bf16[384,512]{1,0:T(8,128)(2,1)S(1)} %copy-done.40, f32[8,512]{1,0:T(8,128)S(1)} %copy-done.46, ...), custom_call_target="tpu_custom_call" | custom-call | flops 999999995904 | bytes 10000000000 | tf_op jit(solution)/shard_map/far_backward/pallas_call | solution.py:61
  119.2 3.6 %collective-permute-start.19 = (bf16[768,256]{1,0:T(8,128)(2,1)}, bf16[768,256]{1,0:T(8,128)(2,1)}, u32[]{:S(2)}, u32[]{:S(2)}) collective-permute-start(bf16[768,256]{1,0:T(8,128)(2,1)} %get-tuple-element.151), channel_id=1, source_target_pairs={{0,16},{4,20},{8,24},{12,28},{16,0},{20,4},{24,8},{28,12},{1,17},{... | collective-permute-start | bytes 1179656 | tf_op jit(solution)/shard_map/ppermute | solution.py:859
  123.1 21.8 %own_backward.1 = (bf16[384,1024]{1,0:T(8,128)(2,1)S(1)}, f32[8,48,1024]{2,1,0:T(8,128)S(1)}, f32[8,48,1024]{2,1,0:T(8,128)S(1)}) custom-call(s32[4]{0:T(128)S(1)} %copy-done.12, bf16[384,512]{1,0:T(8,128)(2,1)S(1)} %copy-done.34, bf16[384,512]{1,0:T(8,128)(2,1)S(1)} %copy-done.40, bf16[384,512]{1,0:T(8,128)(2,1)S(1)} %copy-done.36, ...), custom_call_target="tpu_custom_call" | custom-call | flops 999999995904 | bytes 10000000000 | tf_op jit(solution)/shard_map/own_backward/pallas_call | solution.py:61
  145.0 4.2 %split_second.1 = (bf16[4,240,384]{2,1,0:T(8,128)(2,1)}, bf16[4,240,384]{2,1,0:T(8,128)(2,1)S(1)}, bf16[4,192,384]{2,1,0:T(8,128)(2,1)}, bf16[4,192,384]{2,1,0:T(8,128)(2,1)S(1)}) custom-call(s32[4]{0:T(128)S(1)} %copy-done.12, bf16[4,2,240,384]{3,2,1,0:T(8,128)(2,1)S(1)} %get-tuple-element.137.ka, bf16[4,2,240,384]{3,2,1,0:T(8,128)(2,1)} %collective-permute-done.16.ga, ...), custom_call_target="tpu_custom_call" | custom-call | tf_op jit(solution)/shard_map/split_second/pallas_call | solution.py:61
  149.2 0.9 copy-done.6
  151.2 5.6 %collective-permute-done.20.rest_2_ = bf16[768,256]{1,0:T(8,128)(2,1)} collective-permute-done((bf16[768,256]{1,0:T(8,128)(2,1)}, bf16[768,256]{1,0:T(8,128)(2,1)}, u32[]{:S(2)}, u32[]{:S(2)}) %collective-permute-start.20) | collective-permute-done | bytes 393248 | tf_op jit(solution)/shard_map/ppermute | solution.py:859
  156.8 11.6 %finish.1 = (f32[512,768]{1,0:T(8,128)S(1)}, bf16[512,768]{1,0:T(8,128)(2,1)S(1)}, bf16[8,48,1280]{2,1,0:T(8,128)(2,1)}, bf16[8,48,1280]{2,1,0:T(8,128)(2,1)S(1)}) custom-call(s32[4]{0:T(128)S(1)} %copy-done.12, bf16[384,1024]{1,0:T(8,128)(2,1)S(1)} %get-tuple-element.143.dq, f32[8,48,1024]{2,1,0:T(8,128)S(1)} %get-tuple-element.144.dk, ...), custom_call_target="tpu_custom_call" | custom-call | flops 999999995904 | bytes 10000000000 | tf_op jit(solution)/shard_map/finish/pallas_call | solution.py:195
  168.4 1.1 copy-done
  169.5 0.9 copy-done.2
  171.9 1.1 copy-done.7
  173.0 1.1 copy-done.11
  174.1 1.6 split_third.1
  176.6 1.4 add_convert_fusion.1
  178.7 5.0 %fusion.9 = f32[512,768]{1,0:T(8,128)S(1)} fusion(bf16[3072,512]{1,0:T(8,128)(2,1)S(1)} %copy-done.28, bf16[3072,768]{1,0:T(8,128)(2,1)} %down.1), kind=kOutput, calls=%fused_computation.30 | convolution fusion | flops 2415919104 | bytes 9437184 | tf_op jit(solution)/shard_map/dot_general | solution.py:41
  183.7 1.1 add_convert_fusion
  184.8 6.4 %collective-permute-done.24 = bf16[8,24,1280]{2,1,0:T(8,128)(2,1)S(1)} collective-permute-done((bf16[8,24,1280]{2,1,0:T(8,128)(2,1)S(1)}, bf16[8,24,1280]{2,1,0:T(8,128)(2,1)S(1)}, u32[]{:S(2)}, u32[]{:S(2)}) %collective-permute-start.24) | collective-permute-done | bytes 491552 | tf_op jit(solution)/shard_map/ppermute | solution.py:859
  191.3 1.5 collective-permute-start.25
  193.0 1.8 collective-permute-start.29
  194.8 2.5 %input_grad.1 = f32[512,768]{1,0:T(8,128)} custom-call(bf16[512,768]{1,0:T(8,128)(2,1)S(1)} %bitcast.67, f32[768]{0:T(1024)S(1)} %copy-done.14, f32[512,768]{1,0:T(8,128)S(1)} %copy-done.1, bf16[512,768]{1,0:T(8,128)(2,1)S(1)} %collective-permute-done.26.got, f32[512,768]{1,0:T(8,128)S(1)} %get-tuple-element.171.gres), custom_call_target="tpu_custom_call" | custom-call | tf_op jit(solution)/shard_map/input_grad/pallas_call | solution.py:61
  198.4 1.3 collective-permute-start.28
  199.7 10.6 %collective-permute-done.29 = bf16[432,384]{1,0:T(8,128)(2,1)} collective-permute-done((bf16[432,384]{1,0:T(8,128)(2,1)S(1)}, bf16[432,384]{1,0:T(8,128)(2,1)}, u32[]{:S(2)}, u32[]{:S(2)}) %collective-permute-start.29) | collective-permute-done | bytes 331808 | tf_op jit(solution)/shard_map/ppermute | solution.py:859
  211.2 1.1 fusion.3
  212.9 4.5 %collective-permute-done.30 = bf16[24,2432]{1,0:T(8,128)(2,1)S(1)} collective-permute-done((bf16[24,2432]{1,0:T(8,128)(2,1)S(1)}, bf16[24,2432]{1,0:T(8,128)(2,1)S(1)}, u32[]{:S(2)}, u32[]{:S(2)}) %collective-permute-start.30) | collective-permute-done | bytes 116768 | tf_op jit(solution)/shard_map/ppermute | solution.py:859
  218.1 4.3 %collective-permute-done.33 = bf16[432,384]{1,0:T(8,128)(2,1)S(1)} collective-permute-done((bf16[432,384]{1,0:T(8,128)(2,1)S(1)}, bf16[432,384]{1,0:T(8,128)(2,1)S(1)}, u32[]{:S(2)}, u32[]{:S(2)}) %collective-permute-start.33) | collective-permute-done | bytes 331808 | tf_op jit(solution)/shard_map/ppermute | solution.py:859
  222.6 1.0 collective-permute-done.31
  223.8 0.9 collective-permute-done.34.far
  224.7 2.2 unpack_mlp.1
  226.9 1.6 unpack_in.1
  (159 shorter events, 11.9 us)
Async XLA Ops:
  0.6 20.9 %collective-permute-start = (bf16[512,768]{1,0:T(8,128)(2,1)}, bf16[512,768]{1,0:T(8,128)(2,1)}, u32[]{:S(2)}, u32[]{:S(2)}) collective-permute-start(bf16[512,768]{1,0:T(8,128)(2,1)} %bitcast.63), channel_id=1, source_target_pairs={{0,4},{4,0},{8,12},{12,8},{16,20},{20,16},{24,28},{28,24},{1,5},{5... | collective-permute-start | bytes 2359304 | tf_op jit(solution)/shard_map/ppermute | solution.py:859
  3.7 17.9 %collective-permute-start.1 = (s32[1,512]{1,0:T(1,128)}, s32[1,512]{1,0:T(1,128)}, u32[]{:S(2)}, u32[]{:S(2)}) collective-permute-start(s32[1,512]{1,0:T(1,128)} %ids_ref.1), channel_id=1, source_target_pairs={{0,4},{4,0},{8,12},{12,8},{16,20},{20,16},{24,28},{28,24},{1,5},{5... | collective-permute-start | bytes 6152 | tf_op jit(solution)/shard_map/ppermute | solution.py:859
  10.2 20.7 %collective-permute-start.4 = (bf16[784,128]{1,0:T(8,128)(2,1)}, bf16[784,128]{1,0:T(8,128)(2,1)}, u32[]{:S(2)}, u32[]{:S(2)}) collective-permute-start(bf16[784,128]{1,0:T(8,128)(2,1)} %get-tuple-element.114), channel_id=1, source_target_pairs={{0,16},{4,20},{8,24},{12,28},{16,0},{20,4},{24,8},{28,12},{1,17},{... | collective-permute-start | bytes 602120 | tf_op jit(solution)/shard_map/ppermute | solution.py:859
  13.2 27.4 %collective-permute-start.6 = (bf16[784,128]{1,0:T(8,128)(2,1)}, bf16[784,128]{1,0:T(8,128)(2,1)}, u32[]{:S(2)}, u32[]{:S(2)}) collective-permute-start(bf16[784,128]{1,0:T(8,128)(2,1)} %get-tuple-element.114), channel_id=1, source_target_pairs={{0,24},{4,28},{8,16},{12,20},{16,8},{20,12},{24,0},{28,4},{1,25},{... | collective-permute-start | bytes 602120 | tf_op jit(solution)/shard_map/ppermute | solution.py:859
  14.5 26.2 %collective-permute-start.2 = (bf16[784,256]{1,0:T(8,128)(2,1)}, bf16[784,256]{1,0:T(8,128)(2,1)}, u32[]{:S(2)}, u32[]{:S(2)}) collective-permute-start(bf16[784,256]{1,0:T(8,128)(2,1)} %get-tuple-element.112), channel_id=1, source_target_pairs={{0,8},{4,12},{8,0},{12,4},{16,24},{20,28},{24,16},{28,20},{1,9},{5... | collective-permute-start | bytes 1204232 | tf_op jit(solution)/shard_map/ppermute | solution.py:859
  26.6 22.8 %copy-start.39 = (bf16[384,512]{1,0:T(8,128)(2,1)}, bf16[384,512]{1,0:T(8,128)(2,1)S(1)}, u32[]{:S(2)}) copy-start(bf16[384,512]{1,0:T(8,128)(2,1)S(1)} %get-tuple-element.105.qb) | copy-start | bytes 1179652
  26.6 22.8 %copy-start.47 = (f32[8,512]{1,0:T(8,128)}, f32[8,512]{1,0:T(8,128)S(1)}, u32[]{:S(2)}) copy-start(f32[8,512]{1,0:T(8,128)S(1)} %get-tuple-element.111.db) | copy-start | bytes 49156
  26.7 18.2 %collective-permute-start.5 = (bf16[784,128]{1,0:T(8,128)(2,1)}, bf16[784,128]{1,0:T(8,128)(2,1)}, u32[]{:S(2)}, u32[]{:S(2)}) collective-permute-start(bf16[784,128]{1,0:T(8,128)(2,1)} %get-tuple-element.115), channel_id=1, source_target_pairs={{0,16},{4,20},{8,24},{12,28},{16,0},{20,4},{24,8},{28,12},{1,17},{... | collective-permute-start | bytes 602120 | tf_op jit(solution)/shard_map/ppermute | solution.py:859
  29.5 15.3 %collective-permute-start.7 = (bf16[784,128]{1,0:T(8,128)(2,1)}, bf16[784,128]{1,0:T(8,128)(2,1)}, u32[]{:S(2)}, u32[]{:S(2)}) collective-permute-start(bf16[784,128]{1,0:T(8,128)(2,1)} %get-tuple-element.115), channel_id=1, source_target_pairs={{0,24},{4,28},{8,16},{12,20},{16,8},{20,12},{24,0},{28,4},{1,25},{... | collective-permute-start | bytes 602120 | tf_op jit(solution)/shard_map/ppermute | solution.py:859
  30.9 18.5 %collective-permute-start.3 = (bf16[784,256]{1,0:T(8,128)(2,1)}, bf16[784,256]{1,0:T(8,128)(2,1)}, u32[]{:S(2)}, u32[]{:S(2)}) collective-permute-start(bf16[784,256]{1,0:T(8,128)(2,1)} %get-tuple-element.113), channel_id=1, source_target_pairs={{0,8},{4,12},{8,0},{12,4},{16,24},{20,28},{24,16},{28,20},{1,9},{5... | collective-permute-start | bytes 1204232 | tf_op jit(solution)/shard_map/ppermute | solution.py:859
  40.6 17.5 %collective-permute-start.9 = (bf16[512,768]{1,0:T(8,128)(2,1)}, bf16[512,768]{1,0:T(8,128)(2,1)}, u32[]{:S(2)}, u32[]{:S(2)}) collective-permute-start(bf16[512,768]{1,0:T(8,128)(2,1)} %bitcast.5.cot.refs_5_), channel_id=1, source_target_pairs={{0,1},{1,0},{2,3},{3,2},{4,5},{5,4},{6,7},{7,6},{8,9},{9,8},{10,11... | collective-permute-start | bytes 2359304 | tf_op jit(solution)/shard_map/ppermute | solution.py:859
  49.4 18.7 %copy-start.4 = (bf16[1,512,768]{2,1,0:T(8,128)(2,1)S(1)}, bf16[1,512,768]{2,1,0:T(8,128)(2,1)}, u32[]{:S(2)}) copy-start(bf16[1,512,768]{2,1,0:T(8,128)(2,1)} %param.15) | copy-start | bytes 2359300
  49.4 18.7 %copy-start.17 = (bf16[768,768]{1,0:T(8,128)(2,1)S(1)}, bf16[768,768]{1,0:T(8,128)(2,1)}, u32[]{:S(2)}) copy-start(bf16[768,768]{1,0:T(8,128)(2,1)} %wout.1) | copy-start | bytes 3538948
  49.4 18.6 %copy-start.22 = (f32[3072]{0:T(1024)S(1)}, f32[3072]{0:T(1024)}, u32[]{:S(2)}) copy-start(f32[3072]{0:T(1024)} %param.26) | copy-start | bytes 36868
  49.4 18.6 %copy-start.24 = (f32[768]{0:T(1024)S(1)}, f32[768]{0:T(1024)}, u32[]{:S(2)}) copy-start(f32[768]{0:T(1024)} %out_b.1) | copy-start | bytes 9220
  49.4 18.6 %copy-start.25 = (f32[768]{0:T(1024)S(1)}, f32[768]{0:T(1024)}, u32[]{:S(2)}) copy-start(f32[768]{0:T(1024)} %n2g.1) | copy-start | bytes 9220
  49.4 18.6 %copy-start.26 = (f32[768]{0:T(1024)S(1)}, f32[768]{0:T(1024)}, u32[]{:S(2)}) copy-start(f32[768]{0:T(1024)} %n2s.1) | copy-start | bytes 9220
  49.5 18.6 %copy-start.29 = (bf16[512,3072]{1,0:T(8,128)(2,1)S(1)}, bf16[512,3072]{1,0:T(8,128)(2,1)}, u32[]{:S(2)}) copy-start(bf16[512,3072]{1,0:T(8,128)(2,1)} %cot_down.1.gdown) | copy-start | bytes 9437188
  56.4 1.8 collective-permute-start.10
  56.5 11.5 %collective-permute-start.8 = (bf16[384,512]{1,0:T(8,128)(2,1)S(1)}, bf16[384,512]{1,0:T(8,128)(2,1)S(1)}, u32[]{:S(2)}, u32[]{:S(2)}) collective-permute-start(bf16[384,512]{1,0:T(8,128)(2,1)S(1)} %get-tuple-element.117), channel_id=1, source_target_pairs={{0,4},{4,0},{8,12},{12,8},{16,20},{20,16},{24,28},{28,24},{1,5},{5... | collective-permute-start | bytes 1179656 | tf_op jit(solution)/shard_map/ppermute | solution.py:859
  68.1 27.3 %copy-start.20 = (bf16[384,512]{1,0:T(8,128)(2,1)S(1)}, bf16[384,512]{1,0:T(8,128)(2,1)}, u32[]{:S(2)}) copy-start(bf16[384,512]{1,0:T(8,128)(2,1)} %copy-done.19) | copy-start | bytes 1179652
  86.9 18.1 %copy-start.27 = (bf16[3072,512]{1,0:T(8,128)(2,1)}, bf16[3072,512]{1,0:T(8,128)(2,1)S(1)}, u32[]{:S(2)}) copy-start(bf16[3072,512]{1,0:T(8,128)(2,1)S(1)} %get-tuple-element.122.refs_0_.refs_1_) | copy-start | bytes 9437188
  86.9 8.5 %collective-permute-start.12 = (bf16[1536,512]{1,0:T(8,128)(2,1)S(1)}, bf16[1536,512]{1,0:T(8,128)(2,1)S(1)}, u32[]{:S(2)}, u32[]{:S(2)}) collective-permute-start(bf16[1536,512]{1,0:T(8,128)(2,1)S(1)} %get-tuple-element.125), channel_id=1, source_target_pairs={{0,1},{1,0},{2,3},{3,2},{4,5},{5,4},{6,7},{7,6},{8,9},{9,8},{10,11... | collective-permute-start | bytes 4718600 | tf_op jit(solution)/shard_map/ppermute | solution.py:859
  86.9 8.5 %collective-permute-start.13 = (bf16[1536,512]{1,0:T(8,128)(2,1)S(1)}, bf16[1536,512]{1,0:T(8,128)(2,1)S(1)}, u32[]{:S(2)}, u32[]{:S(2)}) collective-permute-start(bf16[1536,512]{1,0:T(8,128)(2,1)S(1)} %get-tuple-element.123.refs_2_.refs_3_), channel_id=1, source_target_pairs={{0,1},{1,0},{2,3},{3,2},{4,5},{5,4},{6,7},{7,6},{8,9},{9,8},{10,11... | collective-permute-start | bytes 4718600 | tf_op jit(solution)/shard_map/ppermute | solution.py:859
  87.4 8.0 %collective-permute-start.14 = (bf16[512,1536]{1,0:T(8,128)(2,1)S(1)}, bf16[512,1536]{1,0:T(8,128)(2,1)S(1)}, u32[]{:S(2)}, u32[]{:S(2)}) collective-permute-start(bf16[512,1536]{1,0:T(8,128)(2,1)S(1)} %get-tuple-element.126), channel_id=1, source_target_pairs={{0,1},{1,0},{2,3},{3,2},{4,5},{5,4},{6,7},{7,6},{8,9},{9,8},{10,11... | collective-permute-start | bytes 4718600 | tf_op jit(solution)/shard_map/ppermute | solution.py:859
  87.4 8.0 %collective-permute-start.15 = (bf16[384,512]{1,0:T(8,128)(2,1)S(1)}, bf16[384,512]{1,0:T(8,128)(2,1)S(1)}, u32[]{:S(2)}, u32[]{:S(2)}) collective-permute-start(bf16[384,512]{1,0:T(8,128)(2,1)S(1)} %collective-permute-done.8.moth.refs_7_), channel_id=1, source_target_pairs={{0,1},{1,0},{2,3},{3,2},{4,5},{5,4},{6,7},{7,6},{8,9},{9,8},{10,11... | collective-permute-start | bytes 1179656 | tf_op jit(solution)/shard_map/ppermute | solution.py:859
  87.9 20.2 %collective-permute-start.11 = (bf16[384,512]{1,0:T(8,128)(2,1)}, bf16[384,512]{1,0:T(8,128)(2,1)}, u32[]{:S(2)}, u32[]{:S(2)}) collective-permute-start(bf16[384,512]{1,0:T(8,128)(2,1)} %get-tuple-element.121), channel_id=1, source_target_pairs={{0,4},{4,0},{8,12},{12,8},{16,20},{20,16},{24,28},{28,24},{1,5},{5... | collective-permute-start | bytes 1179656 | tf_op jit(solution)/shard_map/ppermute | solution.py:859
  105.0 40.0 %collective-permute-start.16 = (bf16[4,2,240,384]{3,2,1,0:T(8,128)(2,1)}, bf16[4,2,240,384]{3,2,1,0:T(8,128)(2,1)}, u32[]{:S(2)}, u32[]{:S(2)}) collective-permute-start(bf16[4,2,240,384]{3,2,1,0:T(8,128)(2,1)} %get-tuple-element.129), channel_id=1, source_target_pairs={{0,2},{1,3},{2,0},{3,1},{4,6},{5,7},{6,4},{7,5},{8,10},{9,11},{10,... | collective-permute-start | bytes 4423688 | tf_op jit(solution)/shard_map/ppermute | solution.py:859
  106.5 38.4 %collective-permute-start.17 = (bf16[4,2,192,384]{3,2,1,0:T(8,128)(2,1)}, bf16[4,2,192,384]{3,2,1,0:T(8,128)(2,1)}, u32[]{:S(2)}, u32[]{:S(2)}) collective-permute-start(bf16[4,2,192,384]{3,2,1,0:T(8,128)(2,1)} %get-tuple-element.130), channel_id=1, source_target_pairs={{0,4},{4,0},{8,12},{12,8},{16,20},{20,16},{24,28},{28,24},{1,5},{5... | collective-permute-start | bytes 3538952 | tf_op jit(solution)/shard_map/ppermute | solution.py:859
  118.7 38.0 %collective-permute-start.18 = (bf16[768,512]{1,0:T(8,128)(2,1)}, bf16[768,512]{1,0:T(8,128)(2,1)}, u32[]{:S(2)}, u32[]{:S(2)}) collective-permute-start(bf16[768,512]{1,0:T(8,128)(2,1)} %get-tuple-element.150), channel_id=1, source_target_pairs={{0,8},{4,12},{8,0},{12,4},{16,24},{20,28},{24,16},{28,20},{1,9},{5... | collective-permute-start | bytes 2359304 | tf_op jit(solution)/shard_map/ppermute | solution.py:859
  119.2 32.0 %collective-permute-start.19 = (bf16[768,256]{1,0:T(8,128)(2,1)}, bf16[768,256]{1,0:T(8,128)(2,1)}, u32[]{:S(2)}, u32[]{:S(2)}) collective-permute-start(bf16[768,256]{1,0:T(8,128)(2,1)} %get-tuple-element.151), channel_id=1, source_target_pairs={{0,16},{4,20},{8,24},{12,28},{16,0},{20,4},{24,8},{28,12},{1,17},{... | collective-permute-start | bytes 1179656 | tf_op jit(solution)/shard_map/ppermute | solution.py:859
  122.8 34.0 %collective-permute-start.20 = (bf16[768,256]{1,0:T(8,128)(2,1)}, bf16[768,256]{1,0:T(8,128)(2,1)}, u32[]{:S(2)}, u32[]{:S(2)}) collective-permute-start(bf16[768,256]{1,0:T(8,128)(2,1)} %get-tuple-element.152), channel_id=1, source_target_pairs={{0,24},{4,28},{8,16},{12,20},{16,8},{20,12},{24,0},{28,4},{1,25},{... | collective-permute-start | bytes 1179656 | tf_op jit(solution)/shard_map/ppermute | solution.py:859
  150.2 18.2 %copy-start.10 = (bf16[4,192,384]{2,1,0:T(8,128)(2,1)}, bf16[4,192,384]{2,1,0:T(8,128)(2,1)S(1)}, u32[]{:S(2)}) copy-start(bf16[4,192,384]{2,1,0:T(8,128)(2,1)S(1)} %get-tuple-element.165.kb) | copy-start | bytes 1769476
  150.2 21.2 %collective-permute-start.21 = (bf16[4,240,384]{2,1,0:T(8,128)(2,1)}, bf16[4,240,384]{2,1,0:T(8,128)(2,1)}, u32[]{:S(2)}, u32[]{:S(2)}) collective-permute-start(bf16[4,240,384]{2,1,0:T(8,128)(2,1)} %get-tuple-element.155), channel_id=1, source_target_pairs={{0,4},{4,0},{8,12},{12,8},{16,20},{20,16},{24,28},{28,24},{1,5},{5... | collective-permute-start | bytes 2211848 | tf_op jit(solution)/shard_map/ppermute | solution.py:859
  150.7 19.8 %collective-permute-start.22 = (bf16[4,192,384]{2,1,0:T(8,128)(2,1)}, bf16[4,192,384]{2,1,0:T(8,128)(2,1)}, u32[]{:S(2)}, u32[]{:S(2)}) collective-permute-start(bf16[4,192,384]{2,1,0:T(8,128)(2,1)} %get-tuple-element.156), channel_id=1, source_target_pairs={{0,2},{1,3},{2,0},{3,1},{4,6},{5,7},{6,4},{7,5},{8,10},{9,11},{10,... | collective-permute-start | bytes 1769480 | tf_op jit(solution)/shard_map/ppermute | solution.py:859
  171.3 5.3 %collective-permute-start.23 = (bf16[8,48,1280]{2,1,0:T(8,128)(2,1)}, bf16[8,48,1280]{2,1,0:T(8,128)(2,1)}, u32[]{:S(2)}, u32[]{:S(2)}) collective-permute-start(bf16[8,48,1280]{2,1,0:T(8,128)(2,1)} %get-tuple-element.157), channel_id=1, source_target_pairs={{0,1},{1,0},{2,3},{3,2},{4,5},{5,4},{6,7},{7,6},{8,9},{9,8},{10,11... | collective-permute-start | bytes 2949128 | tf_op jit(solution)/shard_map/ppermute | solution.py:859
  171.3 23.4 %collective-permute-start.26 = (bf16[512,768]{1,0:T(8,128)(2,1)}, bf16[512,768]{1,0:T(8,128)(2,1)S(1)}, u32[]{:S(2)}, u32[]{:S(2)}) collective-permute-start(bf16[512,768]{1,0:T(8,128)(2,1)} %copy-done.18), channel_id=1, source_target_pairs={{0,4},{4,0},{8,12},{12,8},{16,20},{20,16},{24,28},{28,24},{1,5},{5... | collective-permute-start | bytes 2359304 | tf_op jit(solution)/shard_map/ppermute | solution.py:859
  175.8 17.1 %copy-start.8 = (bf16[2,432,384]{2,1,0:T(8,128)(2,1)}, bf16[2,432,384]{2,1,0:T(8,128)(2,1)S(1)}, u32[]{:S(2)}) copy-start(bf16[2,432,384]{2,1,0:T(8,128)(2,1)S(1)} %get-tuple-element.167) | copy-start | bytes 1990660
  175.8 17.1 %collective-permute-start.27 = (bf16[2,432,384]{2,1,0:T(8,128)(2,1)S(1)}, bf16[2,432,384]{2,1,0:T(8,128)(2,1)S(1)}, u32[]{:S(2)}, u32[]{:S(2)}) collective-permute-start(bf16[2,432,384]{2,1,0:T(8,128)(2,1)S(1)} %get-tuple-element.168), channel_id=1, source_target_pairs={{0,8},{4,12},{8,0},{12,4},{16,24},{20,28},{24,16},{28,20},{1,9},{5... | collective-permute-start | bytes 1990664 | tf_op jit(solution)/shard_map/ppermute | solution.py:859
  178.1 13.1 %collective-permute-start.24 = (bf16[8,24,1280]{2,1,0:T(8,128)(2,1)S(1)}, bf16[8,24,1280]{2,1,0:T(8,128)(2,1)S(1)}, u32[]{:S(2)}, u32[]{:S(2)}) collective-permute-start(bf16[8,24,1280]{2,1,0:T(8,128)(2,1)S(1)} %get-tuple-element.191), channel_id=1, source_target_pairs={{0,2},{1,3},{2,0},{3,1},{4,6},{5,7},{6,4},{7,5},{8,10},{9,11},{10,... | collective-permute-start | bytes 1474568 | tf_op jit(solution)/shard_map/ppermute | solution.py:859
  191.3 7.0 %collective-permute-start.25 = (bf16[4,24,1280]{2,1,0:T(8,128)(2,1)S(1)}, bf16[4,24,1280]{2,1,0:T(8,128)(2,1)S(1)}, u32[]{:S(2)}, u32[]{:S(2)}) collective-permute-start(bf16[4,24,1280]{2,1,0:T(8,128)(2,1)S(1)} %fusion.4), channel_id=1, source_target_pairs={{0,4},{4,0},{8,12},{12,8},{16,20},{20,16},{24,28},{28,24},{1,5},{5... | collective-permute-start | bytes 737288 | tf_op jit(solution)/shard_map/ppermute | solution.py:859
  193.0 17.4 %collective-permute-start.29 = (bf16[432,384]{1,0:T(8,128)(2,1)S(1)}, bf16[432,384]{1,0:T(8,128)(2,1)}, u32[]{:S(2)}, u32[]{:S(2)}) collective-permute-start(bf16[432,384]{1,0:T(8,128)(2,1)S(1)} %fusion.1), channel_id=1, source_target_pairs={{0,16},{4,20},{8,24},{12,28},{16,0},{20,4},{24,8},{28,12},{1,17},{... | collective-permute-start | bytes 995336 | tf_op jit(solution)/shard_map/ppermute | solution.py:859
  198.4 12.7 %collective-permute-start.28 = (bf16[2,24,2432]{2,1,0:T(8,128)(2,1)S(1)}, bf16[2,24,2432]{2,1,0:T(8,128)(2,1)S(1)}, u32[]{:S(2)}, u32[]{:S(2)}) collective-permute-start(bf16[2,24,2432]{2,1,0:T(8,128)(2,1)S(1)} %dynamic-slice_bitcast_fusion), channel_id=1, source_target_pairs={{0,8},{4,12},{8,0},{12,4},{16,24},{20,28},{24,16},{28,20},{1,9},{5... | collective-permute-start | bytes 700424 | tf_op jit(solution)/shard_map/ppermute | solution.py:859
  211.1 6.3 %collective-permute-start.30 = (bf16[24,2432]{1,0:T(8,128)(2,1)S(1)}, bf16[24,2432]{1,0:T(8,128)(2,1)S(1)}, u32[]{:S(2)}, u32[]{:S(2)}) collective-permute-start(bf16[24,2432]{1,0:T(8,128)(2,1)S(1)} %fusion.6), channel_id=1, source_target_pairs={{0,16},{4,20},{8,24},{12,28},{16,0},{20,4},{24,8},{28,12},{1,17},{... | collective-permute-start | bytes 350216 | tf_op jit(solution)/shard_map/ppermute | solution.py:859
  212.3 10.0 %collective-permute-start.33 = (bf16[432,384]{1,0:T(8,128)(2,1)S(1)}, bf16[432,384]{1,0:T(8,128)(2,1)S(1)}, u32[]{:S(2)}, u32[]{:S(2)}) collective-permute-start(bf16[432,384]{1,0:T(8,128)(2,1)S(1)} %fusion.3), channel_id=1, source_target_pairs={{0,2},{1,3},{2,0},{3,1},{4,6},{5,7},{6,4},{7,5},{8,10},{9,11},{10,... | collective-permute-start | bytes 995336 | tf_op jit(solution)/shard_map/ppermute | solution.py:859
  217.5 6.1 %collective-permute-start.31 = (bf16[24,2432]{1,0:T(8,128)(2,1)S(1)}, bf16[24,2432]{1,0:T(8,128)(2,1)S(1)}, u32[]{:S(2)}, u32[]{:S(2)}) collective-permute-start(bf16[24,2432]{1,0:T(8,128)(2,1)S(1)} %fusion.8), channel_id=1, source_target_pairs={{0,2},{1,3},{2,0},{3,1},{4,6},{5,7},{6,4},{7,5},{8,10},{9,11},{10,... | collective-permute-start | bytes 350216 | tf_op jit(solution)/shard_map/ppermute | solution.py:859
  222.5 2.2 collective-permute-start.34
  223.7 3.2 %collective-permute-start.32 = (bf16[2,24,2432]{2,1,0:T(8,128)(2,1)S(1)}, bf16[2,24,2432]{2,1,0:T(8,128)(2,1)S(1)}, u32[]{:S(2)}, u32[]{:S(2)}) collective-permute-start(bf16[2,24,2432]{2,1,0:T(8,128)(2,1)S(1)} %pad_maximum_fusion.2.near), channel_id=1, source_target_pairs={{0,1},{1,0},{2,3},{3,2},{4,5},{5,4},{6,7},{7,6},{8,9},{9,8},{10,11... | collective-permute-start | bytes 700424 | tf_op jit(solution)/shard_map/ppermute | solution.py:859
  (39 other events, 343.3 us)

commit v2 on v1

--- a/solution.py
+++ b/solution.py
@@ -69,7 +69,7 @@
     )(*ins)
 
 
-TAIL = ("split_second", "split_third", "input_grad", "unpack_mlp", "unpack_in")
+TAIL = ("far_forward_first", "split_second", "split_third", "input_grad", "unpack_mlp", "unpack_in")
 
 
 def estimate(name, flops, nbytes):
@@ -311,14 +311,14 @@
     return [(b0, min(b0, 2), found[b0]) for b0 in sorted(found)]
 
 
-def remote_parts(refs, members, local, level, tok):
+def remote_parts(refs, members, local, level, tok, pieces=2):
     width = tok >> level
     start = run_start(local, level, tok)
     lane = iota_row(width) + start
     row = pl.multiple_of(local * HD, 16)
     ks, vs, docs, poss = [], [], [], []
     for j in members:
-        for ref in refs[2 * j : 2 * j + 2]:
+        for ref in refs[pieces * j : pieces * (j + 1)]:
             ks.append(ref[pl.ds(row, HD), :])
             vs.append(ref[pl.ds(row + GW, HD), :])
             block = ref[2 * GW : 2 * GW + 16, :].astype(f32)
@@ -330,10 +330,9 @@
     return ks, vs, docs, poss, start, width
 
 
-def far_forward_body(tok, masks, y_ref, qa, qb, da, db, part, *rest):
-    nrem = 2 * len(masks)
-    refs = rest[:nrem]
-    ma, mb, merged, lse, qaugs, kaugs, vaugs, accs = rest[nrem:]
+def far_forward_body(tok, masks, last, y_ref, qa, qb, da, db, part, *rest):
+    refs, rest = rest[: len(masks)], rest[len(masks) :]
+    outs, (qaugs, kaugs, vaugs, accs) = rest[:-4], rest[-4:]
     for i in range(FAR_STEP):
         local = pl.program_id(0) * FAR_STEP + i
         head = y_ref[0] * HG + local
@@ -341,7 +340,7 @@
         acc[...] = part[i]
         for g, (b0, level, members) in enumerate(groups_of(masks)):
             qaug, kaug, vaug = qaugs.at[i, g], kaugs.at[i, g], vaugs.at[i, g]
-            ks, vs, docs, poss, start, width = remote_parts(refs, members, local, level, tok)
+            ks, vs, docs, poss, start, width = remote_parts(refs, members, local, level, tok, 1)
             nk = width * len(ks)
             fill_keys(kaug, vaug, ks, vs, docs, poss, head, b0, tok)
             window = pl.ds(pl.multiple_of(start, 128), width)
@@ -354,6 +353,10 @@
                 acc[:, other] += val[:, width : 2 * width]
 
             attend(qaug, kaug, vaug, 2 * width, nk, 2 * width, put)
+        if not last:
+            outs[0][i] = acc[...]
+            continue
+        ma, mb, merged, lse = outs
         den = acc[HD : HD + 1]
         val = acc[0:HD] / den
         merged[i] = val
@@ -372,26 +375,28 @@
     return sum(2 * HG * 64 * (2 * (tok >> lv)) * ((tok >> lv) * 2 * len(mem)) for _, lv, mem in groups_of(masks))
 
 
-def far_forward(y, qs, docs, part, masks, remote):
+def far_forward(y, qs, docs, part, masks, remote, last):
     tok = qs[0].shape[1]
     nq, nk = remote_sizes(masks, tok)
+    nk = max(nk // 2, 128)
     n = len(groups_of(masks))
     per_head = lambda r: pl.BlockSpec((FAR_STEP, r, 2 * tok), lambda h: (h, 0, 0))
+    final = [sds((GW, tok), bf16)] * 2 + [sds((HG, HD, 2 * tok), f32), sds((HG, 8, 2 * tok), f32)]
     return kcall(
-        functools.partial(far_forward_body, tok, masks),
-        "far_forward",
+        functools.partial(far_forward_body, tok, masks, last),
+        "far_forward" if last else "far_forward_first",
         (y, *qs, *docs, part, *remote),
-        [sds((GW, tok), bf16)] * 2 + [sds((HG, HD, 2 * tok), f32), sds((HG, 8, 2 * tok), f32)],
+        final if last else [sds((HG, 64, 2 * tok), f32)],
         grid=(HG // FAR_STEP,),
         in_specs=[SMEM] + [head_block(tok, FAR_STEP)] * 2 + [full((8, tok))] * 2 + [per_head(64)] + [full(r.shape) for r in remote],
-        out_specs=[head_block(tok, FAR_STEP)] * 2 + [per_head(HD), per_head(8)],
+        out_specs=[head_block(tok, FAR_STEP)] * 2 + [per_head(HD), per_head(8)] if last else [per_head(64)],
         scratch=[
             pltpu.VMEM((FAR_STEP, n, 64, nq), bf16),
             pltpu.VMEM((FAR_STEP, n, 64, nk), bf16),
             pltpu.VMEM((FAR_STEP, n, 64, nk), bf16),
             pltpu.VMEM((FAR_STEP, 64, 2 * tok), f32),
         ],
-        flops=2 * remote_flops(masks, tok),
+        flops=remote_flops(masks, tok),
     )
 
 
@@ -889,19 +894,20 @@
 
 def split_third_body(bits, ka, ga, kb, gb, send, keep):
     low = bits[2] % 2
-    for h in range(2):
-        at = 0
-        for own, got in ((ka, ga), (kb, gb)):
-            rows = slice(at, at + own.shape[1])
-            send[h, rows] = own[2 * h + 1 - low] + got[2 * h + 1 - low]
-            keep[h, rows] = own[2 * h + low] + got[2 * h + low]
-            at += own.shape[1]
+    at = 0
+    for own, got in ((ka, ga), (kb, gb)):
+        rows = slice(at, at + own.shape[1])
+        send[0, rows] = own[1 - low] + got[1 - low]
+        keep[0, rows] = own[low] + got[low]
+        at += own.shape[1]
 
 
 def split_third(bits, ka, ga, kb, gb):
     out = sds((2, ka.shape[1] + kb.shape[1], HALF), bf16)
+    two = lambda v, n: pl.BlockSpec((n,) + v.shape[1:], lambda j: (j, 0, 0))
     return kcall(
-        split_third_body, "split_third", (bits, ka, ga, kb, gb), [out, out], in_specs=[SMEM] + [VMEM] * 4, out_specs=[VMEM] * 2,
+        split_third_body, "split_third", (bits, ka, ga, kb, gb), [out, out], grid=(2,),
+        in_specs=[SMEM] + [two(v, 2) for v in (ka, ga, kb, gb)], out_specs=[two(out, 1)] * 2,
     )
 
 
@@ -950,7 +956,8 @@
     qs, ks, vs, docs = (qa, qb), (ka, kb), (va, vb), (doc_a, doc_b)
     part = own_forward(y, qs, ks, vs, docs)
     remote = [r for pair in zip(remote_a, remote_b, strict=True) for r in pair]
-    mown, msend, merged, lse = far_forward(y, qs, docs, part, masks, remote)
+    part, = far_forward(y, qs, docs, part, masks, remote_a, False)
+    mown, msend, merged, lse = far_forward(y, qs, docs, part, masks, remote_b, True)
     moth = swap(msend, "seq", 1)
     if whole:
         moth, cot_got, mown_got = tie(moth, cot_got, swap(mown, "rep", 1))
@@ -1022,7 +1029,8 @@
         g_down, g_up, g_out = kcall(
             unpack_mlp_body, "unpack_mlp", (bits, near, far),
             [sds((DOWN_ROWS, D), f32), sds((UP_ROWS, FF), f32), sds((UP_ROWS, D), f32)],
-            in_specs=[SMEM, VMEM, VMEM], out_specs=[VMEM] * 3,
+            grid=(1,), in_specs=[SMEM, full(near.shape), full(far.shape)],
+            out_specs=[full((DOWN_ROWS, D)), full((UP_ROWS, FF)), full((UP_ROWS, D))],
         )
         near, far = spread(i_keep + i_got, xbit)
         far, g_down = tie(far, g_down)

time: 229 us -> 226 us (0.987)
  waiting for transfers between devices: 59 us -> 53.7 us
  Pallas kernels: 118 us -> 122 us
    ppermute x35, waiting for transfers between devices: 59 us -> 53.7 us  [swap(): return lax.ppermute(value, axis, [(i, i ^ offset) for i in range(count)])]
    pallas_call x10 -> x11, Pallas kernels: 67.7 us -> 71.4 us  [kcall(): pl.pallas_call(body, out_shape=outs, scratch_shapes=list(scratch), name=n...]
    unnamed x104 -> x94, local copies, waits for them, and re-layouts: 7.03 us -> 7 us
  transfers between devices with their start and end apart: 35 -> 35, of which waited for: 16 -> 14; matrix products, arithmetic and copies ran while one was open for 4% -> 4% of each run, Pallas kernels for 43% -> 45%
where the time goes in v2:
time: 226 us
  Pallas kernels  122 us (54%)
  waiting for transfers between devices  53.7 us (24%)
  starting transfers between devices  33 us (15%)
  local copies, waits for them, and re-layouts  7.02 us (3%)
  matrix products  5 us (2%)
  other arithmetic  3.84 us (2%)
    pallas_call x11, Pallas kernels, kcall(): pl.pallas_call(body, out_shape=outs, scratch_shapes=list(scratch), name=n...  71.4 us
    ppermute x35, waiting for transfers between devices, swap(): return lax.ppermute(value, axis, [(i, i ^ offset) for i in range(count)])  53.7 us
    pallas_call x5, Pallas kernels, pcall(): pl.pallas_call(body, grid_spec=pltpu.PrefetchScalarGridSpec(num_scalar_pr...  50.5 us
    ppermute x35, starting transfers between devices, swap(): return lax.ppermute(value, axis, [(i, i ^ offset) for i in range(count)])  33 us
    unnamed x94, local copies, waits for them, and re-layouts  7 us
    dot_general x1, matrix products, mm(): return lax.dot_general(left, right, dims, preferred_element_type=f32)  5 us
  transfers between devices with their start and end apart: 35, of which 14 were waited for; matrix products, arithmetic and copies ran while one was open for 4% of the time, Pallas kernels for 45%

profile of v2, /device:TPU:0, one launch (start us, length us, event | category | flops | bytes accessed | tf_op | source)
XLA Modules:
  0.0 225.7 jit_solution(14138913056500897607)
XLA Ops:
  0.6 3.0 %collective-permute-start = (bf16[512,768]{1,0:T(8,128)(2,1)}, bf16[512,768]{1,0:T(8,128)(2,1)}, u32[]{:S(2)}, u32[]{:S(2)}) collective-permute-start(bf16[512,768]{1,0:T(8,128)(2,1)} %bitcast.63), channel_id=1, source_target_pairs={{0,4},{4,0},{8,12},{12,8},{16,20},{20,16},{24,28},{28,24},{1,5},{5... | collective-permute-start | bytes 2359304 | tf_op jit(solution)/shard_map/ppermute | solution.py:864
  4.3 5.8 %project.2 = (bf16[768,512]{1,0:T(8,128)(2,1)}, bf16[384,512]{1,0:T(8,128)(2,1)}, bf16[384,512]{1,0:T(8,128)(2,1)}, bf16[384,512]{1,0:T(8,128)(2,1)}, f32[8,512]...) custom-call(s32[4]{0:T(128)} %pad_add_fusion.y_ref.bits, bf16[512,768]{1,0:T(8,128)(2,1)} %bitcast.64, ...), custom_call_target="tpu_custom_call" | custom-call | flops 999999995904 | bytes 10000000000 | tf_op jit(solution)/shard_map/project/pallas_call | solution.py:195
  10.2 3.0 %collective-permute-start.3 = (bf16[784,128]{1,0:T(8,128)(2,1)}, bf16[784,128]{1,0:T(8,128)(2,1)}, u32[]{:S(2)}, u32[]{:S(2)}) collective-permute-start(bf16[784,128]{1,0:T(8,128)(2,1)} %get-tuple-element.113), channel_id=1, source_target_pairs={{0,16},{4,20},{8,24},{12,28},{16,0},{20,4},{24,8},{28,12},{1,17},{... | collective-permute-start | bytes 602120 | tf_op jit(solution)/shard_map/ppermute | solution.py:864
  13.2 1.3 collective-permute-start.4
  14.8 6.8 %cot_down.1.gdown = bf16[512,3072]{1,0:T(8,128)(2,1)} custom-call(bf16[512,768]{1,0:T(8,128)(2,1)} %bitcast.5.cot.refs_5_, bf16[3072,768]{1,0:T(8,128)(2,1)} %down.1), custom_call_target="tpu_custom_call" | custom-call | flops 999999995904 | bytes 10000000000 | tf_op jit(solution)/shard_map/cot_down/pallas_call | solution.py:61
  21.7 5.0 %project.3 = (bf16[768,512]{1,0:T(8,128)(2,1)S(1)}, bf16[384,512]{1,0:T(8,128)(2,1)S(1)}, bf16[384,512]{1,0:T(8,128)(2,1)S(1)}, bf16[384,512]{1,0:T(8,128)(2,1)S...) custom-call(s32[4]{0:T(128)S(1)} %copy-done.16, ...), custom_call_target="tpu_custom_call" | custom-call | flops 999999995904 | bytes 10000000000 | tf_op jit(solution)/shard_map/project/pallas_call | solution.py:195
  26.6 2.9 %collective-permute-start.6 = (bf16[784,128]{1,0:T(8,128)(2,1)}, bf16[784,128]{1,0:T(8,128)(2,1)}, u32[]{:S(2)}, u32[]{:S(2)}) collective-permute-start(bf16[784,128]{1,0:T(8,128)(2,1)} %get-tuple-element.115), channel_id=1, source_target_pairs={{0,16},{4,20},{8,24},{12,28},{16,0},{20,4},{24,8},{28,12},{1,17},{... | collective-permute-start | bytes 602120 | tf_op jit(solution)/shard_map/ppermute | solution.py:864
  29.5 1.3 collective-permute-start.7
  31.1 9.4 %own_forward.1.part = f32[8,64,1024]{2,1,0:T(8,128)S(1)} custom-call(s32[4]{0:T(128)S(1)} %copy-done.16, bf16[384,512]{1,0:T(8,128)(2,1)S(1)} %copy-done.12, bf16[384,512]{1,0:T(8,128)(2,1)S(1)} %get-tuple-element.105.qb, bf16[384,512]{1,0:T(8,128)(2,1)S(1)} %copy-done.36, bf16[384,512]{1,0:T(8,128)(2,1)S(1)} %get-tuple-element.107.kb, ...), custom_call_target="tpu_custom_call" | custom-call | flops 999999995904 | bytes 10000000000 | tf_op jit(solution)/shard_map/own_forward/pallas_call | solution.py:61
  40.6 5.2 %far_forward_first.1.part = f32[8,64,1024]{2,1,0:T(8,128)S(1)} custom-call(s32[4]{0:T(128)S(1)} %copy-done.16, bf16[384,512]{1,0:T(8,128)(2,1)S(1)} %copy-done.12, bf16[384,512]{1,0:T(8,128)(2,1)S(1)} %get-tuple-element.105.qb, f32[8,512]{1,0:T(8,128)S(1)} %copy-done.17, f32[8,512]{1,0:T(8,128)S(1)} %get-tuple-element.111.db, ...), custom_call_target="tpu_custom_call" | custom-call | tf_op jit(solution)/shard_map/far_forward_first/pallas_call | solution.py:61
  45.8 3.6 %collective-permute-done.5.rest_0_.rest_1_ = bf16[784,256]{1,0:T(8,128)(2,1)} collective-permute-done((bf16[784,256]{1,0:T(8,128)(2,1)}, bf16[784,256]{1,0:T(8,128)(2,1)}, u32[]{:S(2)}, u32[]{:S(2)}) %collective-permute-start.5) | collective-permute-done | bytes 401440 | tf_op jit(solution)/shard_map/ppermute | solution.py:864
  49.5 5.5 %far_forward.1 = (bf16[384,512]{1,0:T(8,128)(2,1)S(1)}, bf16[384,512]{1,0:T(8,128)(2,1)S(1)}, f32[8,48,1024]{2,1,0:T(8,128)S(1)}, f32[8,8,1024]{2,1,0:T(8,128)S(1)}) custom-call(s32[4]{0:T(128)S(1)} %copy-done.16, bf16[384,512]{1,0:T(8,128)(2,1)S(1)} %copy-done.12, bf16[384,512]{1,0:T(8,128)(2,1)S(1)} %get-tuple-element.105.qb, f32[8,512]{1,0:T(8,128)S(1)} %copy-done.17, ...), custom_call_target="tpu_custom_call" | custom-call | flops 999999995904 | bytes 10000000000 | tf_op jit(solution)/shard_map/far_forward/pallas_call | solution.py:61
  55.1 1.6 collective-permute-start.8
  57.5 9.1 %collective-permute-done.8.moth.refs_7_ = bf16[384,512]{1,0:T(8,128)(2,1)S(1)} collective-permute-done((bf16[384,512]{1,0:T(8,128)(2,1)S(1)}, bf16[384,512]{1,0:T(8,128)(2,1)S(1)}, u32[]{:S(2)}, u32[]{:S(2)}) %collective-permute-start.8) | collective-permute-done | bytes 393248 | tf_op jit(solution)/shard_map/ppermute | solution.py:864
  66.7 18.7 %mlp.1 = (bf16[3072,512]{1,0:T(8,128)(2,1)S(1)}, bf16[1536,512]{1,0:T(8,128)(2,1)S(1)}, bf16[512,3072]{1,0:T(8,128)(2,1)S(1)}, bf16[512,1536]{1,0:T(8,128)(2,1)S...) custom-call(s32[4]{0:T(128)S(1)} %copy-done.16, ...), custom_call_target="tpu_custom_call" | custom-call | flops 999999995904 | bytes 10000000000 | tf_op jit(solution)/shard_map/mlp/pallas_call | solution.py:195
  86.4 1.6 collective-permute-start.11
  88.0 5.9 %collective-permute-done.15.refs_15_ = bf16[384,512]{1,0:T(8,128)(2,1)S(1)} collective-permute-done((bf16[384,512]{1,0:T(8,128)(2,1)S(1)}, bf16[384,512]{1,0:T(8,128)(2,1)S(1)}, u32[]{:S(2)}, u32[]{:S(2)}) %collective-permute-start.15) | collective-permute-done | bytes 393248 | tf_op jit(solution)/shard_map/ppermute | solution.py:864
  93.9 9.5 %mlp_grads.1 = (bf16[4,2,240,384]{3,2,1,0:T(8,128)(2,1)}, bf16[4,2,240,384]{3,2,1,0:T(8,128)(2,1)S(1)}, bf16[4,2,192,384]{3,2,1,0:T(8,128)(2,1)}, bf16[4,2,192,384]{3,2,1,0:T(8,128)(2,1)S(1)}) custom-call(s32[4]{0:T(128)S(1)} %copy-done.16, bf16[3072,512]{1,0:T(8,128)(2,1)S(1)} %get-tuple-element.122.refs_0_.refs_1_, ...), custom_call_target="tpu_custom_call" | custom-call | flops 999999995904 | bytes 10000000000 | tf_op jit(solution)/shard_map/mlp_grads/pallas_call | solution.py:195
  103.4 1.5 collective-permute-start.16
  105.0 1.5 collective-permute-start.17
  106.5 10.6 %far_backward.1 = (f32[8,48,1024]{2,1,0:T(8,128)S(1)}, bf16[768,512]{1,0:T(8,128)(2,1)}, bf16[768,256]{1,0:T(8,128)(2,1)}, bf16[768,256]{1,0:T(8,128)(2,1)}) custom-call(s32[4]{0:T(128)S(1)} %copy-done.16, bf16[384,512]{1,0:T(8,128)(2,1)S(1)} %copy-done.13, bf16[384,512]{1,0:T(8,128)(2,1)S(1)} %copy-done.15, f32[8,512]{1,0:T(8,128)S(1)} %copy-done.17, ...), custom_call_target="tpu_custom_call" | custom-call | flops 999999995904 | bytes 10000000000 | tf_op jit(solution)/shard_map/far_backward/pallas_call | solution.py:61
  117.6 3.6 %collective-permute-start.19 = (bf16[768,256]{1,0:T(8,128)(2,1)}, bf16[768,256]{1,0:T(8,128)(2,1)}, u32[]{:S(2)}, u32[]{:S(2)}) collective-permute-start(bf16[768,256]{1,0:T(8,128)(2,1)} %get-tuple-element.151), channel_id=1, source_target_pairs={{0,16},{4,20},{8,24},{12,28},{16,0},{20,4},{24,8},{28,12},{1,17},{... | collective-permute-start | bytes 1179656 | tf_op jit(solution)/shard_map/ppermute | solution.py:864
  121.5 21.7 %own_backward.1 = (bf16[384,1024]{1,0:T(8,128)(2,1)S(1)}, f32[8,48,1024]{2,1,0:T(8,128)S(1)}, f32[8,48,1024]{2,1,0:T(8,128)S(1)}) custom-call(s32[4]{0:T(128)S(1)} %copy-done.16, bf16[384,512]{1,0:T(8,128)(2,1)S(1)} %copy-done.13, bf16[384,512]{1,0:T(8,128)(2,1)S(1)} %copy-done.15, bf16[384,512]{1,0:T(8,128)(2,1)S(1)} %copy-done.37, ...), custom_call_target="tpu_custom_call" | custom-call | flops 999999995904 | bytes 10000000000 | tf_op jit(solution)/shard_map/own_backward/pallas_call | solution.py:61
  143.3 4.1 %split_second.1 = (bf16[4,240,384]{2,1,0:T(8,128)(2,1)}, bf16[4,240,384]{2,1,0:T(8,128)(2,1)S(1)}, bf16[4,192,384]{2,1,0:T(8,128)(2,1)}, bf16[4,192,384]{2,1,0:T(8,128)(2,1)S(1)}) custom-call(s32[4]{0:T(128)S(1)} %copy-done.16, bf16[4,2,240,384]{3,2,1,0:T(8,128)(2,1)S(1)} %get-tuple-element.137.ka, bf16[4,2,240,384]{3,2,1,0:T(8,128)(2,1)} %collective-permute-done.16.ga, ...), custom_call_target="tpu_custom_call" | custom-call | tf_op jit(solution)/shard_map/split_second/pallas_call | solution.py:61
  147.4 0.9 copy-done.6
  149.3 5.9 %collective-permute-done.20.rest_2_ = bf16[768,256]{1,0:T(8,128)(2,1)} collective-permute-done((bf16[768,256]{1,0:T(8,128)(2,1)}, bf16[768,256]{1,0:T(8,128)(2,1)}, u32[]{:S(2)}, u32[]{:S(2)}) %collective-permute-start.20) | collective-permute-done | bytes 393248 | tf_op jit(solution)/shard_map/ppermute | solution.py:864
  155.2 11.4 %finish.1 = (f32[512,768]{1,0:T(8,128)S(1)}, bf16[512,768]{1,0:T(8,128)(2,1)S(1)}, bf16[8,48,1280]{2,1,0:T(8,128)(2,1)}, bf16[8,48,1280]{2,1,0:T(8,128)(2,1)S(1)}) custom-call(s32[4]{0:T(128)S(1)} %copy-done.16, bf16[384,1024]{1,0:T(8,128)(2,1)S(1)} %get-tuple-element.143.dq, f32[8,48,1024]{2,1,0:T(8,128)S(1)} %get-tuple-element.144.dk, ...), custom_call_target="tpu_custom_call" | custom-call | flops 999999995904 | bytes 10000000000 | tf_op jit(solution)/shard_map/finish/pallas_call | solution.py:195
  166.6 1.1 copy-done
  167.7 0.9 copy-done.2
  170.2 1.1 copy-done.7
  171.4 1.1 copy-done.11
  172.4 1.8 split_third.1
  175.1 1.4 add_convert_fusion.1
  177.2 5.0 %fusion.9 = f32[512,768]{1,0:T(8,128)S(1)} fusion(bf16[3072,512]{1,0:T(8,128)(2,1)S(1)} %copy-done.33, bf16[3072,768]{1,0:T(8,128)(2,1)} %down.1), kind=kOutput, calls=%fused_computation.30 | convolution fusion | flops 2415919104 | bytes 9437184 | tf_op jit(solution)/shard_map/dot_general | solution.py:41
  182.2 1.1 add_convert_fusion
  183.3 6.3 %collective-permute-done.24 = bf16[8,24,1280]{2,1,0:T(8,128)(2,1)S(1)} collective-permute-done((bf16[8,24,1280]{2,1,0:T(8,128)(2,1)S(1)}, bf16[8,24,1280]{2,1,0:T(8,128)(2,1)S(1)}, u32[]{:S(2)}, u32[]{:S(2)}) %collective-permute-start.24) | collective-permute-done | bytes 491552 | tf_op jit(solution)/shard_map/ppermute | solution.py:864
  189.7 1.5 collective-permute-start.25
  191.4 1.8 collective-permute-start.29
  193.2 2.6 %input_grad.1 = f32[512,768]{1,0:T(8,128)} custom-call(bf16[512,768]{1,0:T(8,128)(2,1)S(1)} %bitcast.67, f32[768]{0:T(1024)S(1)} %copy-done.19, f32[512,768]{1,0:T(8,128)S(1)} %copy-done.1, bf16[512,768]{1,0:T(8,128)(2,1)S(1)} %collective-permute-done.26.got, f32[512,768]{1,0:T(8,128)S(1)} %get-tuple-element.171.gres), custom_call_target="tpu_custom_call" | custom-call | tf_op jit(solution)/shard_map/input_grad/pallas_call | solution.py:61
  196.7 1.3 collective-permute-start.28
  198.0 10.5 %collective-permute-done.29 = bf16[432,384]{1,0:T(8,128)(2,1)S(1)} collective-permute-done((bf16[432,384]{1,0:T(8,128)(2,1)S(1)}, bf16[432,384]{1,0:T(8,128)(2,1)S(1)}, u32[]{:S(2)}, u32[]{:S(2)}) %collective-permute-start.29) | collective-permute-done | bytes 331808 | tf_op jit(solution)/shard_map/ppermute | solution.py:864
  208.6 0.9 collective-permute-done.28
  210.4 5.3 %collective-permute-done.30 = bf16[24,2432]{1,0:T(8,128)(2,1)S(1)} collective-permute-done((bf16[24,2432]{1,0:T(8,128)(2,1)S(1)}, bf16[24,2432]{1,0:T(8,128)(2,1)S(1)}, u32[]{:S(2)}, u32[]{:S(2)}) %collective-permute-start.30) | collective-permute-done | bytes 116768 | tf_op jit(solution)/shard_map/ppermute | solution.py:864
  216.3 3.3 %collective-permute-done.33 = bf16[432,384]{1,0:T(8,128)(2,1)S(1)} collective-permute-done((bf16[432,384]{1,0:T(8,128)(2,1)S(1)}, bf16[432,384]{1,0:T(8,128)(2,1)S(1)}, u32[]{:S(2)}, u32[]{:S(2)}) %collective-permute-start.33) | collective-permute-done | bytes 331808 | tf_op jit(solution)/shard_map/ppermute | solution.py:864
  219.8 1.0 collective-permute-done.31
  221.0 0.9 collective-permute-done.34.far
  221.9 2.2 unpack_mlp.1
  224.1 1.6 unpack_in.1
  (150 shorter events, 11.1 us)
Async XLA Ops:
  0.6 20.9 %collective-permute-start = (bf16[512,768]{1,0:T(8,128)(2,1)}, bf16[512,768]{1,0:T(8,128)(2,1)}, u32[]{:S(2)}, u32[]{:S(2)}) collective-permute-start(bf16[512,768]{1,0:T(8,128)(2,1)} %bitcast.63), channel_id=1, source_target_pairs={{0,4},{4,0},{8,12},{12,8},{16,20},{20,16},{24,28},{28,24},{1,5},{5... | collective-permute-start | bytes 2359304 | tf_op jit(solution)/shard_map/ppermute | solution.py:864
  3.7 17.9 %collective-permute-start.1 = (s32[1,512]{1,0:T(1,128)}, s32[1,512]{1,0:T(1,128)}, u32[]{:S(2)}, u32[]{:S(2)}) collective-permute-start(s32[1,512]{1,0:T(1,128)} %ids_ref.1), channel_id=1, source_target_pairs={{0,4},{4,0},{8,12},{12,8},{16,20},{20,16},{24,28},{28,24},{1,5},{5... | collective-permute-start | bytes 6152 | tf_op jit(solution)/shard_map/ppermute | solution.py:864
  10.2 20.7 %collective-permute-start.3 = (bf16[784,128]{1,0:T(8,128)(2,1)}, bf16[784,128]{1,0:T(8,128)(2,1)}, u32[]{:S(2)}, u32[]{:S(2)}) collective-permute-start(bf16[784,128]{1,0:T(8,128)(2,1)} %get-tuple-element.113), channel_id=1, source_target_pairs={{0,16},{4,20},{8,24},{12,28},{16,0},{20,4},{24,8},{28,12},{1,17},{... | collective-permute-start | bytes 602120 | tf_op jit(solution)/shard_map/ppermute | solution.py:864
  13.2 27.3 %collective-permute-start.4 = (bf16[784,128]{1,0:T(8,128)(2,1)}, bf16[784,128]{1,0:T(8,128)(2,1)}, u32[]{:S(2)}, u32[]{:S(2)}) collective-permute-start(bf16[784,128]{1,0:T(8,128)(2,1)} %get-tuple-element.113), channel_id=1, source_target_pairs={{0,24},{4,28},{8,16},{12,20},{16,8},{20,12},{24,0},{28,4},{1,25},{... | collective-permute-start | bytes 602120 | tf_op jit(solution)/shard_map/ppermute | solution.py:864
  14.5 26.1 %collective-permute-start.2 = (bf16[784,256]{1,0:T(8,128)(2,1)}, bf16[784,256]{1,0:T(8,128)(2,1)}, u32[]{:S(2)}, u32[]{:S(2)}) collective-permute-start(bf16[784,256]{1,0:T(8,128)(2,1)} %get-tuple-element.112), channel_id=1, source_target_pairs={{0,8},{4,12},{8,0},{12,4},{16,24},{20,28},{24,16},{28,20},{1,9},{5... | collective-permute-start | bytes 1204232 | tf_op jit(solution)/shard_map/ppermute | solution.py:864
  26.6 22.8 %copy-start.14 = (bf16[384,512]{1,0:T(8,128)(2,1)}, bf16[384,512]{1,0:T(8,128)(2,1)S(1)}, u32[]{:S(2)}) copy-start(bf16[384,512]{1,0:T(8,128)(2,1)S(1)} %get-tuple-element.105.qb) | copy-start | bytes 1179652
  26.6 19.2 %collective-permute-start.6 = (bf16[784,128]{1,0:T(8,128)(2,1)}, bf16[784,128]{1,0:T(8,128)(2,1)}, u32[]{:S(2)}, u32[]{:S(2)}) collective-permute-start(bf16[784,128]{1,0:T(8,128)(2,1)} %get-tuple-element.115), channel_id=1, source_target_pairs={{0,16},{4,20},{8,24},{12,28},{16,0},{20,4},{24,8},{28,12},{1,17},{... | collective-permute-start | bytes 602120 | tf_op jit(solution)/shard_map/ppermute | solution.py:864
  29.5 16.3 %collective-permute-start.7 = (bf16[784,128]{1,0:T(8,128)(2,1)}, bf16[784,128]{1,0:T(8,128)(2,1)}, u32[]{:S(2)}, u32[]{:S(2)}) collective-permute-start(bf16[784,128]{1,0:T(8,128)(2,1)} %get-tuple-element.115), channel_id=1, source_target_pairs={{0,24},{4,28},{8,16},{12,20},{16,8},{20,12},{24,0},{28,4},{1,25},{... | collective-permute-start | bytes 602120 | tf_op jit(solution)/shard_map/ppermute | solution.py:864
  30.9 18.5 %collective-permute-start.5 = (bf16[784,256]{1,0:T(8,128)(2,1)}, bf16[784,256]{1,0:T(8,128)(2,1)}, u32[]{:S(2)}, u32[]{:S(2)}) collective-permute-start(bf16[784,256]{1,0:T(8,128)(2,1)} %get-tuple-element.114), channel_id=1, source_target_pairs={{0,8},{4,12},{8,0},{12,4},{16,24},{20,28},{24,16},{28,20},{1,9},{5... | collective-permute-start | bytes 1204232 | tf_op jit(solution)/shard_map/ppermute | solution.py:864
  40.5 16.2 %collective-permute-start.9 = (bf16[512,768]{1,0:T(8,128)(2,1)}, bf16[512,768]{1,0:T(8,128)(2,1)}, u32[]{:S(2)}, u32[]{:S(2)}) collective-permute-start(bf16[512,768]{1,0:T(8,128)(2,1)} %bitcast.5.cot.refs_5_), channel_id=1, source_target_pairs={{0,1},{1,0},{2,3},{3,2},{4,5},{5,4},{6,7},{7,6},{8,9},{9,8},{10,11... | collective-permute-start | bytes 2359304 | tf_op jit(solution)/shard_map/ppermute | solution.py:864
  49.4 17.2 %copy-start.4 = (bf16[1,512,768]{2,1,0:T(8,128)(2,1)S(1)}, bf16[1,512,768]{2,1,0:T(8,128)(2,1)}, u32[]{:S(2)}) copy-start(bf16[1,512,768]{2,1,0:T(8,128)(2,1)} %param.15) | copy-start | bytes 2359300
  49.4 17.2 %copy-start.22 = (bf16[768,768]{1,0:T(8,128)(2,1)S(1)}, bf16[768,768]{1,0:T(8,128)(2,1)}, u32[]{:S(2)}) copy-start(bf16[768,768]{1,0:T(8,128)(2,1)} %wout.1) | copy-start | bytes 3538948
  49.4 17.2 %copy-start.27 = (f32[3072]{0:T(1024)S(1)}, f32[3072]{0:T(1024)}, u32[]{:S(2)}) copy-start(f32[3072]{0:T(1024)} %param.26) | copy-start | bytes 36868
  49.4 17.2 %copy-start.29 = (f32[768]{0:T(1024)S(1)}, f32[768]{0:T(1024)}, u32[]{:S(2)}) copy-start(f32[768]{0:T(1024)} %out_b.1) | copy-start | bytes 9220
  49.4 17.2 %copy-start.30 = (f32[768]{0:T(1024)S(1)}, f32[768]{0:T(1024)}, u32[]{:S(2)}) copy-start(f32[768]{0:T(1024)} %n2g.1) | copy-start | bytes 9220
  49.4 17.2 %copy-start.31 = (f32[768]{0:T(1024)S(1)}, f32[768]{0:T(1024)}, u32[]{:S(2)}) copy-start(f32[768]{0:T(1024)} %n2s.1) | copy-start | bytes 9220
  49.4 17.2 %copy-start.34 = (bf16[512,3072]{1,0:T(8,128)(2,1)S(1)}, bf16[512,3072]{1,0:T(8,128)(2,1)}, u32[]{:S(2)}) copy-start(bf16[512,3072]{1,0:T(8,128)(2,1)} %cot_down.1.gdown) | copy-start | bytes 9437188
  55.0 1.8 collective-permute-start.10
  55.1 11.5 %collective-permute-start.8 = (bf16[384,512]{1,0:T(8,128)(2,1)S(1)}, bf16[384,512]{1,0:T(8,128)(2,1)S(1)}, u32[]{:S(2)}, u32[]{:S(2)}) collective-permute-start(bf16[384,512]{1,0:T(8,128)(2,1)S(1)} %get-tuple-element.117), channel_id=1, source_target_pairs={{0,4},{4,0},{8,12},{12,8},{16,20},{20,16},{24,28},{28,24},{1,5},{5... | collective-permute-start | bytes 1179656 | tf_op jit(solution)/shard_map/ppermute | solution.py:864
  66.6 27.3 %copy-start.25 = (bf16[384,512]{1,0:T(8,128)(2,1)S(1)}, bf16[384,512]{1,0:T(8,128)(2,1)}, u32[]{:S(2)}) copy-start(bf16[384,512]{1,0:T(8,128)(2,1)} %copy-done.24) | copy-start | bytes 1179652
  85.4 18.0 %copy-start.32 = (bf16[3072,512]{1,0:T(8,128)(2,1)}, bf16[3072,512]{1,0:T(8,128)(2,1)S(1)}, u32[]{:S(2)}) copy-start(bf16[3072,512]{1,0:T(8,128)(2,1)S(1)} %get-tuple-element.122.refs_0_.refs_1_) | copy-start | bytes 9437188
  85.4 8.5 %collective-permute-start.12 = (bf16[1536,512]{1,0:T(8,128)(2,1)S(1)}, bf16[1536,512]{1,0:T(8,128)(2,1)S(1)}, u32[]{:S(2)}, u32[]{:S(2)}) collective-permute-start(bf16[1536,512]{1,0:T(8,128)(2,1)S(1)} %get-tuple-element.125), channel_id=1, source_target_pairs={{0,1},{1,0},{2,3},{3,2},{4,5},{5,4},{6,7},{7,6},{8,9},{9,8},{10,11... | collective-permute-start | bytes 4718600 | tf_op jit(solution)/shard_map/ppermute | solution.py:864
  85.4 8.5 %collective-permute-start.13 = (bf16[1536,512]{1,0:T(8,128)(2,1)S(1)}, bf16[1536,512]{1,0:T(8,128)(2,1)S(1)}, u32[]{:S(2)}, u32[]{:S(2)}) collective-permute-start(bf16[1536,512]{1,0:T(8,128)(2,1)S(1)} %get-tuple-element.123.refs_2_.refs_3_), channel_id=1, source_target_pairs={{0,1},{1,0},{2,3},{3,2},{4,5},{5,4},{6,7},{7,6},{8,9},{9,8},{10,11... | collective-permute-start | bytes 4718600 | tf_op jit(solution)/shard_map/ppermute | solution.py:864
  85.9 8.0 %collective-permute-start.14 = (bf16[512,1536]{1,0:T(8,128)(2,1)S(1)}, bf16[512,1536]{1,0:T(8,128)(2,1)S(1)}, u32[]{:S(2)}, u32[]{:S(2)}) collective-permute-start(bf16[512,1536]{1,0:T(8,128)(2,1)S(1)} %get-tuple-element.126), channel_id=1, source_target_pairs={{0,1},{1,0},{2,3},{3,2},{4,5},{5,4},{6,7},{7,6},{8,9},{9,8},{10,11... | collective-permute-start | bytes 4718600 | tf_op jit(solution)/shard_map/ppermute | solution.py:864
  85.9 8.0 %collective-permute-start.15 = (bf16[384,512]{1,0:T(8,128)(2,1)S(1)}, bf16[384,512]{1,0:T(8,128)(2,1)S(1)}, u32[]{:S(2)}, u32[]{:S(2)}) collective-permute-start(bf16[384,512]{1,0:T(8,128)(2,1)S(1)} %collective-permute-done.8.moth.refs_7_), channel_id=1, source_target_pairs={{0,1},{1,0},{2,3},{3,2},{4,5},{5,4},{6,7},{7,6},{8,9},{9,8},{10,11... | collective-permute-start | bytes 1179656 | tf_op jit(solution)/shard_map/ppermute | solution.py:864
  86.4 20.0 %collective-permute-start.11 = (bf16[384,512]{1,0:T(8,128)(2,1)}, bf16[384,512]{1,0:T(8,128)(2,1)}, u32[]{:S(2)}, u32[]{:S(2)}) collective-permute-start(bf16[384,512]{1,0:T(8,128)(2,1)} %get-tuple-element.121), channel_id=1, source_target_pairs={{0,4},{4,0},{8,12},{12,8},{16,20},{20,16},{24,28},{28,24},{1,5},{5... | collective-permute-start | bytes 1179656 | tf_op jit(solution)/shard_map/ppermute | solution.py:864
  103.4 39.8 %collective-permute-start.16 = (bf16[4,2,240,384]{3,2,1,0:T(8,128)(2,1)}, bf16[4,2,240,384]{3,2,1,0:T(8,128)(2,1)}, u32[]{:S(2)}, u32[]{:S(2)}) collective-permute-start(bf16[4,2,240,384]{3,2,1,0:T(8,128)(2,1)} %get-tuple-element.129), channel_id=1, source_target_pairs={{0,2},{1,3},{2,0},{3,1},{4,6},{5,7},{6,4},{7,5},{8,10},{9,11},{10,... | collective-permute-start | bytes 4423688 | tf_op jit(solution)/shard_map/ppermute | solution.py:864
  105.0 38.3 %collective-permute-start.17 = (bf16[4,2,192,384]{3,2,1,0:T(8,128)(2,1)}, bf16[4,2,192,384]{3,2,1,0:T(8,128)(2,1)}, u32[]{:S(2)}, u32[]{:S(2)}) collective-permute-start(bf16[4,2,192,384]{3,2,1,0:T(8,128)(2,1)} %get-tuple-element.130), channel_id=1, source_target_pairs={{0,4},{4,0},{8,12},{12,8},{16,20},{20,16},{24,28},{28,24},{1,5},{5... | collective-permute-start | bytes 3538952 | tf_op jit(solution)/shard_map/ppermute | solution.py:864
  106.5 15.0 %copy-start.37 = (bf16[384,512]{1,0:T(8,128)(2,1)S(1)}, bf16[384,512]{1,0:T(8,128)(2,1)}, u32[]{:S(2)}) copy-start(bf16[384,512]{1,0:T(8,128)(2,1)} %get-tuple-element.106.ka) | copy-start | bytes 1179652
  117.1 38.0 %collective-permute-start.18 = (bf16[768,512]{1,0:T(8,128)(2,1)}, bf16[768,512]{1,0:T(8,128)(2,1)}, u32[]{:S(2)}, u32[]{:S(2)}) collective-permute-start(bf16[768,512]{1,0:T(8,128)(2,1)} %get-tuple-element.150), channel_id=1, source_target_pairs={{0,8},{4,12},{8,0},{12,4},{16,24},{20,28},{24,16},{28,20},{1,9},{5... | collective-permute-start | bytes 2359304 | tf_op jit(solution)/shard_map/ppermute | solution.py:864
  117.6 31.7 %collective-permute-start.19 = (bf16[768,256]{1,0:T(8,128)(2,1)}, bf16[768,256]{1,0:T(8,128)(2,1)}, u32[]{:S(2)}, u32[]{:S(2)}) collective-permute-start(bf16[768,256]{1,0:T(8,128)(2,1)} %get-tuple-element.151), channel_id=1, source_target_pairs={{0,16},{4,20},{8,24},{12,28},{16,0},{20,4},{24,8},{28,12},{1,17},{... | collective-permute-start | bytes 1179656 | tf_op jit(solution)/shard_map/ppermute | solution.py:864
  121.2 34.0 %collective-permute-start.20 = (bf16[768,256]{1,0:T(8,128)(2,1)}, bf16[768,256]{1,0:T(8,128)(2,1)}, u32[]{:S(2)}, u32[]{:S(2)}) collective-permute-start(bf16[768,256]{1,0:T(8,128)(2,1)} %get-tuple-element.152), channel_id=1, source_target_pairs={{0,24},{4,28},{8,16},{12,20},{16,8},{20,12},{24,0},{28,4},{1,25},{... | collective-permute-start | bytes 1179656 | tf_op jit(solution)/shard_map/ppermute | solution.py:864
  148.3 18.3 %copy-start.10 = (bf16[4,192,384]{2,1,0:T(8,128)(2,1)}, bf16[4,192,384]{2,1,0:T(8,128)(2,1)S(1)}, u32[]{:S(2)}) copy-start(bf16[4,192,384]{2,1,0:T(8,128)(2,1)S(1)} %get-tuple-element.165.kb) | copy-start | bytes 1769476
  148.3 21.3 %collective-permute-start.21 = (bf16[4,240,384]{2,1,0:T(8,128)(2,1)}, bf16[4,240,384]{2,1,0:T(8,128)(2,1)}, u32[]{:S(2)}, u32[]{:S(2)}) collective-permute-start(bf16[4,240,384]{2,1,0:T(8,128)(2,1)} %get-tuple-element.155), channel_id=1, source_target_pairs={{0,4},{4,0},{8,12},{12,8},{16,20},{20,16},{24,28},{28,24},{1,5},{5... | collective-permute-start | bytes 2211848 | tf_op jit(solution)/shard_map/ppermute | solution.py:864
  148.8 20.8 %collective-permute-start.22 = (bf16[4,192,384]{2,1,0:T(8,128)(2,1)}, bf16[4,192,384]{2,1,0:T(8,128)(2,1)}, u32[]{:S(2)}, u32[]{:S(2)}) collective-permute-start(bf16[4,192,384]{2,1,0:T(8,128)(2,1)} %get-tuple-element.156), channel_id=1, source_target_pairs={{0,2},{1,3},{2,0},{3,1},{4,6},{5,7},{6,4},{7,5},{8,10},{9,11},{10,... | collective-permute-start | bytes 1769480 | tf_op jit(solution)/shard_map/ppermute | solution.py:864
  169.6 5.5 %collective-permute-start.23 = (bf16[8,48,1280]{2,1,0:T(8,128)(2,1)}, bf16[8,48,1280]{2,1,0:T(8,128)(2,1)}, u32[]{:S(2)}, u32[]{:S(2)}) collective-permute-start(bf16[8,48,1280]{2,1,0:T(8,128)(2,1)} %get-tuple-element.157), channel_id=1, source_target_pairs={{0,1},{1,0},{2,3},{3,2},{4,5},{5,4},{6,7},{7,6},{8,9},{9,8},{10,11... | collective-permute-start | bytes 2949128 | tf_op jit(solution)/shard_map/ppermute | solution.py:864
  169.7 23.5 %collective-permute-start.26 = (bf16[512,768]{1,0:T(8,128)(2,1)}, bf16[512,768]{1,0:T(8,128)(2,1)S(1)}, u32[]{:S(2)}, u32[]{:S(2)}) collective-permute-start(bf16[512,768]{1,0:T(8,128)(2,1)} %copy-done.23), channel_id=1, source_target_pairs={{0,4},{4,0},{8,12},{12,8},{16,20},{20,16},{24,28},{28,24},{1,5},{5... | collective-permute-start | bytes 2359304 | tf_op jit(solution)/shard_map/ppermute | solution.py:864
  174.2 17.0 %copy-start.8 = (bf16[2,432,384]{2,1,0:T(8,128)(2,1)}, bf16[2,432,384]{2,1,0:T(8,128)(2,1)S(1)}, u32[]{:S(2)}) copy-start(bf16[2,432,384]{2,1,0:T(8,128)(2,1)S(1)} %get-tuple-element.167) | copy-start | bytes 1990660
  174.3 17.0 %collective-permute-start.27 = (bf16[2,432,384]{2,1,0:T(8,128)(2,1)S(1)}, bf16[2,432,384]{2,1,0:T(8,128)(2,1)S(1)}, u32[]{:S(2)}, u32[]{:S(2)}) collective-permute-start(bf16[2,432,384]{2,1,0:T(8,128)(2,1)S(1)} %get-tuple-element.168), channel_id=1, source_target_pairs={{0,8},{4,12},{8,0},{12,4},{16,24},{20,28},{24,16},{28,20},{1,9},{5... | collective-permute-start | bytes 1990664 | tf_op jit(solution)/shard_map/ppermute | solution.py:864
  176.6 13.1 %collective-permute-start.24 = (bf16[8,24,1280]{2,1,0:T(8,128)(2,1)S(1)}, bf16[8,24,1280]{2,1,0:T(8,128)(2,1)S(1)}, u32[]{:S(2)}, u32[]{:S(2)}) collective-permute-start(bf16[8,24,1280]{2,1,0:T(8,128)(2,1)S(1)} %get-tuple-element.191), channel_id=1, source_target_pairs={{0,2},{1,3},{2,0},{3,1},{4,6},{5,7},{6,4},{7,5},{8,10},{9,11},{10,... | collective-permute-start | bytes 1474568 | tf_op jit(solution)/shard_map/ppermute | solution.py:864
  189.7 6.9 %collective-permute-start.25 = (bf16[4,24,1280]{2,1,0:T(8,128)(2,1)S(1)}, bf16[4,24,1280]{2,1,0:T(8,128)(2,1)S(1)}, u32[]{:S(2)}, u32[]{:S(2)}) collective-permute-start(bf16[4,24,1280]{2,1,0:T(8,128)(2,1)S(1)} %fusion.4), channel_id=1, source_target_pairs={{0,4},{4,0},{8,12},{12,8},{16,20},{20,16},{24,28},{28,24},{1,5},{5... | collective-permute-start | bytes 737288 | tf_op jit(solution)/shard_map/ppermute | solution.py:864
  191.4 17.2 %collective-permute-start.29 = (bf16[432,384]{1,0:T(8,128)(2,1)S(1)}, bf16[432,384]{1,0:T(8,128)(2,1)S(1)}, u32[]{:S(2)}, u32[]{:S(2)}) collective-permute-start(bf16[432,384]{1,0:T(8,128)(2,1)S(1)} %fusion.1), channel_id=1, source_target_pairs={{0,16},{4,20},{8,24},{12,28},{16,0},{20,4},{24,8},{28,12},{1,17},{... | collective-permute-start | bytes 995336 | tf_op jit(solution)/shard_map/ppermute | solution.py:864
  196.7 12.7 %collective-permute-start.28 = (bf16[2,24,2432]{2,1,0:T(8,128)(2,1)S(1)}, bf16[2,24,2432]{2,1,0:T(8,128)(2,1)S(1)}, u32[]{:S(2)}, u32[]{:S(2)}) collective-permute-start(bf16[2,24,2432]{2,1,0:T(8,128)(2,1)S(1)} %dynamic-slice_bitcast_fusion), channel_id=1, source_target_pairs={{0,8},{4,12},{8,0},{12,4},{16,24},{20,28},{24,16},{28,20},{1,9},{5... | collective-permute-start | bytes 700424 | tf_op jit(solution)/shard_map/ppermute | solution.py:864
  209.5 6.1 %collective-permute-start.30 = (bf16[24,2432]{1,0:T(8,128)(2,1)S(1)}, bf16[24,2432]{1,0:T(8,128)(2,1)S(1)}, u32[]{:S(2)}, u32[]{:S(2)}) collective-permute-start(bf16[24,2432]{1,0:T(8,128)(2,1)S(1)} %fusion.6), channel_id=1, source_target_pairs={{0,16},{4,20},{8,24},{12,28},{16,0},{20,4},{24,8},{28,12},{1,17},{... | collective-permute-start | bytes 350216 | tf_op jit(solution)/shard_map/ppermute | solution.py:864
  209.8 9.8 %collective-permute-start.33 = (bf16[432,384]{1,0:T(8,128)(2,1)S(1)}, bf16[432,384]{1,0:T(8,128)(2,1)S(1)}, u32[]{:S(2)}, u32[]{:S(2)}) collective-permute-start(bf16[432,384]{1,0:T(8,128)(2,1)S(1)} %fusion.3), channel_id=1, source_target_pairs={{0,2},{1,3},{2,0},{3,1},{4,6},{5,7},{6,4},{7,5},{8,10},{9,11},{10,... | collective-permute-start | bytes 995336 | tf_op jit(solution)/shard_map/ppermute | solution.py:864
  215.7 5.1 %collective-permute-start.31 = (bf16[24,2432]{1,0:T(8,128)(2,1)S(1)}, bf16[24,2432]{1,0:T(8,128)(2,1)S(1)}, u32[]{:S(2)}, u32[]{:S(2)}) collective-permute-start(bf16[24,2432]{1,0:T(8,128)(2,1)S(1)} %fusion.8), channel_id=1, source_target_pairs={{0,2},{1,3},{2,0},{3,1},{4,6},{5,7},{6,4},{7,5},{8,10},{9,11},{10,... | collective-permute-start | bytes 350216 | tf_op jit(solution)/shard_map/ppermute | solution.py:864
  219.8 2.2 collective-permute-start.34
  220.9 3.2 %collective-permute-start.32 = (bf16[2,24,2432]{2,1,0:T(8,128)(2,1)S(1)}, bf16[2,24,2432]{2,1,0:T(8,128)(2,1)S(1)}, u32[]{:S(2)}, u32[]{:S(2)}) collective-permute-start(bf16[2,24,2432]{2,1,0:T(8,128)(2,1)S(1)} %pad_maximum_fusion.2.near), channel_id=1, source_target_pairs={{0,1},{1,0},{2,3},{3,2},{4,5},{5,4},{6,7},{7,6},{8,9},{9,8},{10,11... | collective-permute-start | bytes 700424 | tf_op jit(solution)/shard_map/ppermute | solution.py:864
  (34 other events, 279.1 us)
